TPU v7x, 32 devices: a whole 2x2x4 slice. The times are simulated.
32 devices in a mesh: grp: 4 (over y, x), rep: 8 (over z, core).
Axes of the slice: x: 2, y: 2, z: 4, core: 2. Of those that a mesh axis runs over, the one named last changes fastest.
Arguments:
- forward: float32 [2, 2097152], P(None, ('grp', 'rep')), may hold values from -40 to 40
- adjoint: float32 [2, 2097152], P(None, ('grp', 'rep')), may hold values from -40 to 40
- edges: int32 [60, 2], replicated, may hold values from 0 to 39, as said below
- weights: int32 [60], replicated, may hold values from 1 to 9
- layout: int32 [40], replicated, may hold values from 0 to 39, each once
- slab_bits: int32 [40], replicated, may hold values from 0 to 1
- angles: float32 [4], replicated, may hold values from 0.6 to 1
Outputs:
- forward_out: float32 [2, 2097152], P(None, ('grp', 'rep'))
- adjoint_out: float32 [2, 2097152], P(None, ('grp', 'rep'))
- grads: float32 [4], replicated
Inputs may be any that keep to these rules, and one draw needn't show every extreme that they name: `edges`: the two end nodes of an edge differ.
All inputs are finite; a program needn't handle non-finite values.
Results may differ from a plain program's by a relative error of at most 0.0003.
Values sent between devices are 32-bit elements; how exact they have to be, the bound alone decides.
No kernel may reach another device: no remote copies, remote signals or barrier semaphores. Data moves between devices by JAX's collectives and lax.ppermute only.
A program may use at most 64 MiB of HBM per device.

v0:
```python
import jax
import jax.numpy as jnp
from jax import lax
from jax.experimental import pallas as pl
from jax.experimental.pallas import tpu as pltpu
from jax.sharding import Mesh, PartitionSpec as P

NODES = 40
LAYERS = 2
LANES = 128
TILE = 8
CORES = 2
F32 = jnp.float32
BF16 = jnp.bfloat16
VMEM_LIMIT = 12 << 20


def vmem_call(body, out_shapes, scratch=(), smem_inputs=(), inputs=(), smem_out=False):
    specs = [pl.BlockSpec(memory_space=pltpu.SMEM)] * len(smem_inputs)
    specs += [pl.BlockSpec(memory_space=pltpu.VMEM)] * len(inputs)
    place = pltpu.SMEM if smem_out else pltpu.VMEM
    return pl.pallas_call(
        body,
        out_shape=[jax.ShapeDtypeStruct(shape, kind) for shape, kind in out_shapes],
        in_specs=specs,
        out_specs=[pl.BlockSpec(memory_space=place)] * len(out_shapes),
        scratch_shapes=list(scratch),
        compiler_params=pltpu.CompilerParams(vmem_limit_bytes=VMEM_LIMIT),
    )(*smem_inputs, *inputs)


def half_angle(x):
    y = 0.5 * x
    z = y * y
    sin_y = jnp.full_like(z, -1.0 / 1307674368000.0)
    for factor in (6227020800.0, -39916800.0, 362880.0, -5040.0, 120.0, -6.0, 1.0):
        sin_y = sin_y * z + 1.0 / factor
    sin_y = sin_y * y
    cos_y = jnp.full_like(z, 1.0 / 20922789888000.0)
    for factor in (-87178291200.0, 479001600.0, -3628800.0, 40320.0, -720.0, 24.0, -2.0, 1.0):
        cos_y = cos_y * z + 1.0 / factor
    return 2.0 * sin_y * cos_y, 1.0 - 2.0 * sin_y * sin_y


def split(value):
    high = value.astype(BF16)
    return high, (value - high.astype(F32)).astype(BF16)


def dot(left, right):
    return jnp.dot(left, right, preferred_element_type=F32)


def mixer_mats(size, cos_beta, sin_beta, least=0):
    row = lax.broadcasted_iota(jnp.int32, (size, size), 0)
    col = lax.broadcasted_iota(jnp.int32, (size, size), 1)
    differ = jnp.bitwise_xor(row, col)
    real = jnp.ones((size, size), F32)
    real = jnp.where(jnp.bitwise_and(differ, (1 << least) - 1) == 0, real, 0.0)
    imag = jnp.zeros((size, size), F32)
    for bit in range(least, size.bit_length() - 1):
        flagged = jnp.bitwise_and(differ, 1 << bit) != 0
        real, imag = (
            jnp.where(flagged, -imag * sin_beta, real * cos_beta),
            jnp.where(flagged, real * sin_beta, imag * cos_beta),
        )
    return real, imag


def flip_mat(size, least=0):
    row = lax.broadcasted_iota(jnp.int32, (size, size), 0)
    col = lax.broadcasted_iota(jnp.int32, (size, size), 1)
    differ = jnp.bitwise_xor(row, col)
    count = jnp.zeros((size, size), jnp.int32)
    for bit in range(size.bit_length() - 1):
        count = count + jnp.bitwise_and(differ >> bit, 1)
    rest = jnp.bitwise_and(differ, (1 << least) - 1)
    return jnp.where(jnp.logical_and(count == 1, rest == 0), 1.0, 0.0).astype(BF16)


def rotate_all(planes, lane_high, lane_low, row_high, row_low, cos_beta, sin_beta):
    low = planes[0].shape[0]
    mixed = []
    for block in planes:
        high, rest = split(block)
        if lane_high is not None:
            lanes = dot(high, lane_high) + dot(rest, lane_high) + dot(high, lane_low)
            high, rest = split(lanes)
        both = dot(row_high, high) + dot(row_high, rest) + dot(row_low, high)
        real = both[:low, :LANES] - both[low:, LANES:]
        imag = both[:low, LANES:] + both[low:, :LANES]
        mixed.append((real, imag))
    stride = 1
    while stride < len(mixed):
        for first in range(len(mixed)):
            if first & stride:
                continue
            (ar, ai), (br, bi) = mixed[first], mixed[first + stride]
            mixed[first] = (cos_beta * ar - sin_beta * bi, cos_beta * ai + sin_beta * br)
            mixed[first + stride] = (cos_beta * br - sin_beta * ai, cos_beta * bi + sin_beta * ar)
        stride *= 2
    return mixed


def flips_all(planes, lane_flip, row_flip):
    out = []
    for index, block in enumerate(planes):
        high, rest = split(block)
        total = dot(row_flip, high) + dot(row_flip, rest)
        if lane_flip is not None:
            total = total + dot(high, lane_flip) + dot(rest, lane_flip)
        stride = 1
        while stride < len(planes):
            total = total + planes[index ^ stride]
            stride *= 2
        out.append(total)
    return out


def fold_rows(value):
    folded = value[:TILE]
    for start in range(TILE, value.shape[0], TILE):
        folded = folded + value[start : start + TILE]
    return jnp.sum(folded, axis=0, keepdims=True)


def cross_imag(lam, other):
    return fold_rows(lam[:, :LANES] * other[:, LANES:] - lam[:, LANES:] * other[:, :LANES])


def spin_rows(position, layout, slab, known):
    lane_bits = LANES.bit_length() - 1
    shift = jnp.clip(layout - lane_bits, 0, known - 1)
    inside = jnp.bitwise_and(jnp.right_shift(position, shift), 1)
    bit = jnp.where(layout < known + lane_bits, inside, slab)
    return jnp.where(layout < lane_bits, 0, 1 - 2 * bit).astype(F32)


def table_body(row_count, place_first, place_second, known, low):
    lane_bits = LANES.bit_length() - 1

    def body(angles, edges, weights, layout, slab, *outs):
        cost_a, cos_a, sin_a, cost_b, cos_b, sin_b = outs[:6]
        mats = outs[6:]
        node = lax.broadcasted_iota(jnp.int32, (edges.shape[0], NODES), 1)
        first = jnp.where(edges[:, 0:1] == node, 1.0, 0.0)
        second = jnp.where(edges[:, 1:2] == node, 1.0, 0.0)
        weight = weights[...].astype(F32)
        total = jnp.sum(weight, axis=0, keepdims=True)
        across = (((0,), (0,)), ((), ()))
        exact = lax.Precision.HIGHEST

        def full(left, right, dims):
            return lax.dot_general(left, right, dims, precision=exact, preferred_element_type=F32)

        matrix = full(first * weight, second, across) + full(second * weight, first, across)
        lane = lax.broadcasted_iota(jnp.int32, (LANES, NODES), 0)
        lane_layout = layout[...]
        lane_bit = jnp.bitwise_and(jnp.right_shift(lane, jnp.clip(lane_layout, 0, lane_bits - 1)), 1)
        lane_spin = jnp.where(lane_layout < lane_bits, 1 - 2 * lane_bit, 0).astype(F32)
        plain = (((1,), (0,)), ((), ()))
        turned = (((1,), (1,)), ((), ()))
        lane_energy = full(jnp.ones((TILE, NODES), F32), lane_spin * full(lane_spin, matrix, plain), turned)[0:1]

        def field(position, cost, cos_out, sin_out, gamma):
            spins = spin_rows(position, lane_layout, slab[...], known)
            pulled = full(spins, matrix, plain)
            energy = jnp.sum(pulled * spins, axis=1, keepdims=True)
            energy = energy + lane_energy + 2.0 * full(pulled, lane_spin, turned)
            value = 2.0 - energy / total
            cost[...] = value
            sine, cosine = half_angle(gamma * value)
            cos_out[...] = cosine
            sin_out[...] = sine

        row = lax.broadcasted_iota(jnp.int32, (row_count, 1), 0)
        field(place_first(row), cost_a, cos_a, sin_a, angles[0])
        field(place_second(row), cost_b, cos_b, sin_b, angles[2])
        for layer in range(LAYERS):
            sine, cosine = half_angle(jnp.full((1, 1), angles[2 * layer + 1], F32))
            real, imag = mixer_mats(LANES, cosine, sine)
            lanes = jnp.concatenate(
                [jnp.concatenate([real, imag], axis=1), jnp.concatenate([-imag, real], axis=1)], axis=0
            )
            mats[4 * layer][...], mats[4 * layer + 1][...] = split(lanes)
            real, imag = mixer_mats(low, cosine, sine)
            mats[4 * layer + 2][...], mats[4 * layer + 3][...] = split(jnp.concatenate([real, imag], axis=0))

    return body


def make_tables(angles, edges, weights, layout, slab, rows, low, place_first, place_second, known):
    grid = ((rows, LANES), F32)
    shapes = [grid] * 6
    for _ in range(LAYERS):
        shapes += [((2 * LANES, 2 * LANES), BF16)] * 2 + [((2 * low, low), BF16)] * 2
    out = vmem_call(
        table_body(rows, place_first, place_second, known, low),
        shapes,
        smem_inputs=(angles,),
        inputs=(edges, weights, layout, slab),
    )
    return out[:3], out[3:6], [out[6 + 4 * layer : 10 + 4 * layer] for layer in range(LAYERS)]


class Shape:
    def __init__(self, groups, depth, amp_dev):
        self.groups = groups
        self.depth = depth
        self.wide = groups * CORES
        self.devices = self.wide * depth
        self.rows = amp_dev // LANES
        self.part = self.rows // self.devices
        self.low = min(self.rows, 2 * LANES)
        self.known = (self.rows * self.devices).bit_length() - 1
        self.planes = self.rows // self.low

    def piece(self, wide, level):
        return ((wide // CORES) * self.depth + level) * CORES + wide % CORES


def slots(shape):
    return [(k, w) for k in range(shape.depth) for w in range(shape.wide)]


def angle_pair(angle):
    return half_angle(jnp.full((TILE, LANES), angle, F32))


def butterflies(real, imag, tangent, scale):
    count = len(real)
    stride = 1
    while stride < count:
        for first in range(count):
            if first & stride:
                continue
            other = first + stride
            ar, ai, br, bi = real[first], imag[first], real[other], imag[other]
            real[first], imag[first] = ar - tangent * bi, ai + tangent * br
            real[other], imag[other] = br - tangent * ai, bi + tangent * ar
        stride *= 2
    return [scale * v for v in real], [scale * v for v in imag]


def flip_sum(values, index):
    total = None
    stride = 1
    while stride < len(values):
        term = values[index ^ stride]
        total = term if total is None else total + term
        stride *= 2
    return total


def mixer_scale(sine, cosine, count):
    scale = cosine
    for _ in range(count - 1):
        scale = scale * cosine
    return sine / cosine, scale


def load_pair(ref, piece, part, start):
    base = (piece * part + start) * 2
    return (
        ref[pl.ds(base, TILE, stride=2), :],
        ref[pl.ds(base + 1, TILE, stride=2), :],
    )


def ordered_slots(shape):
    return slots(shape)


def level_now(shape):
    return lax.axis_index("z")


def pre_body(shape, by_level):
    part = shape.part

    def body(angles, state, *outs):
        level = level_now(shape)
        sine, cosine = angle_pair(angles[3])
        order = ordered_slots(shape)
        tangent, scale = mixer_scale(sine, cosine, shape.devices.bit_length() - 1)
        for start in range(0, part, TILE):
            real, imag = [], []
            for k, w in order:
                piece = shape.piece(w, jnp.bitwise_xor(level, k))
                re, im = load_pair(state, piece, part, start)
                real.append(re)
                imag.append(im)
            real, imag = butterflies(real, imag, tangent, scale)
            for (k, w), re, im in zip(order, real, imag):
                if by_level:
                    ref, base = outs[k], w * 2 * part + start
                else:
                    ref, base = outs[0], (w * shape.depth + k) * 2 * part + start
                ref[base : base + TILE, :] = re
                ref[base + part : base + part + TILE, :] = im

    return body


def level_shape(shape):
    return ((shape.wide * 2 * shape.part, LANES), F32)


def whole_shape(shape):
    return ((shape.devices * 2 * shape.part, LANES), F32)


def pre(shape, angles, state, by_level):
    outs = [level_shape(shape)] * shape.depth if by_level else [whole_shape(shape)]
    return vmem_call(pre_body(shape, by_level), outs, smem_inputs=(angles,), inputs=(state,))


def flip_pre(shape, forward, adjoint):
    part = shape.part

    def body(psi, lam, out):
        total = None
        for start in range(0, part, TILE):
            real, imag = [], []
            for piece in range(shape.devices):
                re, im = load_pair(psi, piece, part, start)
                real.append(re)
                imag.append(im)
            for piece in range(shape.devices):
                re, im = load_pair(lam, piece, part, start)
                term = re * flip_sum(imag, piece) - im * flip_sum(real, piece)
                total = term if total is None else total + term
        out[...] = jnp.sum(total, axis=0, keepdims=True)

    return vmem_call(body, [((1, LANES), F32)], inputs=(forward, adjoint))[0]


def swap_order(shape, arrays, join):
    size = 2 * shape.part

    def body(*refs):
        for k in range(shape.depth):
            for w in range(shape.wide):
                base = (w * shape.depth + k) * size
                if join:
                    refs[-1][base : base + size, :] = refs[k][w * size : (w + 1) * size, :]
                else:
                    refs[1 + k][w * size : (w + 1) * size, :] = refs[0][base : base + size, :]

    outs = [whole_shape(shape)] if join else [level_shape(shape)] * shape.depth
    out = vmem_call(body, outs, inputs=tuple(arrays))
    return out[0] if join else out


def slot_place(shape, refs, k, w):
    if len(refs) == 1:
        return refs[0], (w * shape.depth + k) * 2 * shape.part
    return refs[k], w * 2 * shape.part


def load_planes(shape, refs):
    part = shape.part
    pairs = []
    for k, w in slots(shape):
        ref, base = slot_place(shape, refs, k, w)
        pairs.append(jnp.concatenate([ref[base : base + part, :], ref[base + part : base + 2 * part, :]], axis=1))
    per = shape.low // part
    return [jnp.concatenate(pairs[i * per : (i + 1) * per], axis=0) for i in range(shape.planes)]


def phased(real, imag, cosine, sine):
    return real * cosine - imag * sine, imag * cosine + real * sine


def mid_math(shape, angles, planes, mats, cos_b, sin_b):
    low = shape.low
    sine, cosine = half_angle(jnp.full((1, 1), angles[3], F32))
    first = rotate_all(planes, *[m[...] for m in mats[4:8]], cosine, sine)
    turned = []
    for i, (re, im) in enumerate(first):
        re, im = phased(re, im, cos_b[i * low : (i + 1) * low, :], sin_b[i * low : (i + 1) * low, :])
        turned.append(jnp.concatenate([re, im], axis=1))
    sine, cosine = half_angle(jnp.full((1, 1), angles[1], F32))
    second = rotate_all(turned, *[m[...] for m in mats[0:4]], cosine, sine)
    return first, second


def mid(shape, angles, arrays, field_b, mats, by_level):
    count = len(arrays)
    part = shape.part

    def body(*refs):
        angle = refs[0]
        states = refs[1 : 1 + count]
        cos_b, sin_b = refs[1 + count : 3 + count]
        matrices = refs[3 + count : 11 + count]
        before = refs[11 + count]
        outs = refs[12 + count :]
        first, second = mid_math(shape, angle, load_planes(shape, states), matrices, cos_b, sin_b)
        for i, (re, im) in enumerate(first):
            before[i * shape.low : (i + 1) * shape.low, :LANES] = re
            before[i * shape.low : (i + 1) * shape.low, LANES:] = im
        per = shape.low // part
        for i, (k, w) in enumerate(slots(shape)):
            re, im = second[i // per]
            at = (i % per) * part
            ref, base = slot_place(shape, outs, k, w)
            ref[base : base + part, :] = re[at : at + part]
            ref[base + part : base + 2 * part, :] = im[at : at + part]

    outs = [((shape.rows, 2 * LANES), F32)]
    outs += [level_shape(shape)] * shape.depth if by_level else [whole_shape(shape)]
    result = vmem_call(
        body,
        outs,
        smem_inputs=(angles,),
        inputs=tuple(arrays) + (field_b[1], field_b[2]) + tuple(mats[0]) + tuple(mats[1]),
    )
    return result[0], result[1:]


def gradients_mid(shape, cost_b, psi_before, lam_before, psi_after, lam_after, canonical=False):
    n_psi, n_lam = len(psi_after), len(lam_after)
    low = shape.low

    def body(*refs):
        cost, psi_ref, lam_ref = refs[:3]
        psi_refs = refs[3 : 3 + n_psi]
        lam_refs = refs[3 + n_psi : 3 + n_psi + n_lam]
        out = refs[-1]
        small = flip_mat(LANES)
        zero = jnp.zeros_like(small)
        lane_flip = jnp.concatenate(
            [jnp.concatenate([small, zero], axis=1), jnp.concatenate([zero, small], axis=1)], axis=0
        )
        row_flip = flip_mat(low)
        spans = [slice(i * low, (i + 1) * low) for i in range(shape.planes)]
        psi = [psi_ref[span, :] for span in spans]
        lam = [lam_ref[span, :] for span in spans]
        inter = jnp.zeros((1, LANES), F32)
        mix_one = jnp.zeros((1, LANES), F32)
        for i, flips in enumerate(flips_all(psi, lane_flip, row_flip)):
            mix_one = mix_one + cross_imag(lam[i], flips)
            weighted = jnp.concatenate([cost[spans[i], :]] * 2, axis=1) * psi[i]
            inter = inter + cross_imag(lam[i], weighted)
        if canonical:
            psi = [psi_refs[0][span, :] for span in spans]
            lam = [lam_refs[0][span, :] for span in spans]
        else:
            psi = load_planes(shape, psi_refs)
            lam = load_planes(shape, lam_refs)
        mix_zero = jnp.zeros((1, LANES), F32)
        for i, flips in enumerate(flips_all(psi, lane_flip, row_flip)):
            mix_zero = mix_zero + cross_imag(lam[i], flips)
        out[...] = jnp.concatenate([mix_zero, inter, mix_one], axis=0)

    return vmem_call(
        body,
        [((3, LANES), F32)],
        inputs=(cost_b, psi_before, lam_before) + tuple(psi_after) + tuple(lam_after),
    )[0]


def load_slots(shape, refs, start):
    part = shape.part
    real, imag = [], []
    for k, w in ordered_slots(shape):
        ref, base = slot_place(shape, refs, k, w)
        real.append(ref[base + start : base + start + TILE, :])
        imag.append(ref[base + part + start : base + part + start + TILE, :])
    return real, imag


def post_mix(shape, angles, arrays):
    count = len(arrays)
    part = shape.part
    half = shape.devices * part

    def body(*refs):
        angle, states = refs[0], refs[1 : 1 + count]
        mixed, flipped = refs[1 + count :]
        sine, cosine = angle_pair(angle[1])
        tangent, scale = mixer_scale(sine, cosine, shape.devices.bit_length() - 1)
        for start in range(0, part, TILE):
            real, imag = load_slots(shape, states, start)
            real, imag = butterflies(real, imag, tangent, scale)
            for i in range(shape.devices):
                base = i * part + start
                mixed[base : base + TILE, :] = real[i]
                mixed[half + base : half + base + TILE, :] = imag[i]
                flipped[base : base + TILE, :] = flip_sum(real, i)
                flipped[half + base : half + base + TILE, :] = flip_sum(imag, i)

    shapes = [((2 * half, LANES), F32)] * 2
    return vmem_call(body, shapes, smem_inputs=(angles,), inputs=tuple(arrays))


def post_mix_grads(shape, angles, arrays, mixed_psi, flips_psi, cost_a):
    count = len(arrays)
    part = shape.part
    half = shape.devices * part

    def body(*refs):
        angle, states = refs[0], refs[1 : 1 + count]
        psi, flips, cost = refs[1 + count : 4 + count]
        mixed, out = refs[4 + count :]
        level = level_now(shape)
        order = ordered_slots(shape)
        sine, cosine = angle_pair(angle[1])
        tangent, scale = mixer_scale(sine, cosine, shape.devices.bit_length() - 1)
        mix = jnp.zeros((TILE, LANES), F32)
        inter = jnp.zeros((TILE, LANES), F32)
        for start in range(0, part, TILE):
            real, imag = load_slots(shape, states, start)
            real, imag = butterflies(real, imag, tangent, scale)
            for i, (k, w) in enumerate(order):
                base = i * part + start
                high = half + base
                mixed[base : base + TILE, :] = real[i]
                mixed[high : high + TILE, :] = imag[i]
                mix = mix + real[i] * flips[high : high + TILE, :] - imag[i] * flips[base : base + TILE, :]
                piece = shape.piece(w, jnp.bitwise_xor(level, k))
                value = cost[pl.ds(pl.multiple_of(piece * part + start, TILE), TILE), :]
                inter = inter + value * (
                    real[i] * psi[high : high + TILE, :] - imag[i] * psi[base : base + TILE, :]
                )
        out[0:1, :] = jnp.sum(inter, axis=0, keepdims=True)
        out[1:2, :] = jnp.sum(mix, axis=0, keepdims=True)

    shapes = [((2 * half, LANES), F32), ((2, LANES), F32)]
    return vmem_call(
        body, shapes, smem_inputs=(angles,), inputs=tuple(arrays) + (mixed_psi, flips_psi, cost_a)
    )


def post_phase(shape, mixed, field_a):
    part = shape.part
    half = shape.devices * part

    def body(state, cos_a, sin_a, out):
        level = level_now(shape)
        for i, (k, w) in enumerate(ordered_slots(shape)):
            piece = shape.piece(w, jnp.bitwise_xor(level, k))
            for start in range(0, part, TILE):
                base = i * part + start
                real = state[base : base + TILE, :]
                imag = state[half + base : half + base + TILE, :]
                row = pl.multiple_of(piece * part + start, TILE)
                re, im = phased(real, imag, cos_a[pl.ds(row, TILE), :], sin_a[pl.ds(row, TILE), :])
                out[pl.ds(2 * row, TILE, stride=2), :] = re
                out[pl.ds(2 * row + 1, TILE, stride=2), :] = im

    return vmem_call(body, [((2 * half, LANES), F32)], inputs=(mixed, field_a[1], field_a[2]))[0]


def send_levels(shape, arrays):
    out = [arrays[0]]
    for k in range(1, shape.depth):
        pairs = [(i, i ^ k) for i in range(shape.depth)]
        out.append(lax.ppermute(arrays[k], "z", pairs))
    return out


def send_wide(shape, array):
    block = array.reshape(shape.wide, -1, LANES)
    return lax.all_to_all(block, ("grp", "core"), 0, 0, tiled=True).reshape(array.shape)


def total_grads(shape, parts):
    count = shape.devices

    def join(*refs):
        early, mid_part, late, out = refs
        rows = [late[0:1, :], late[1:2, :] + mid_part[0:1, :], mid_part[1:2, :], mid_part[2:3, :] + early[...]]
        block = jnp.concatenate(rows + [jnp.zeros((TILE - 4, LANES), F32)], axis=0)
        for i in range(count):
            out[i * TILE : (i + 1) * TILE, :] = block

    block = vmem_call(join, [((count * TILE, LANES), F32)], inputs=tuple(parts))[0]
    every = lax.all_to_all(
        block.reshape(count, TILE, LANES), ("grp", "z", "core"), 0, 0, tiled=True
    ).reshape(count * TILE, LANES)
    scale = 2.0 / (shape.rows * LANES * count)

    def finish(refs, out):
        block = refs[0:TILE, :]
        for i in range(1, count):
            block = block + refs[i * TILE : (i + 1) * TILE, :]
        block = jnp.sum(block, axis=1, keepdims=True) * scale
        for i in range(2 * LAYERS):
            out[i] = jnp.sum(block[i : i + 1, :])

    return vmem_call(finish, [((2 * LAYERS,), F32)], inputs=(every,), smem_out=True)[0]


def after(values, first):
    return lax.optimization_barrier((values, first))[0]


def piece_mix(shape, angles, which, state):
    low = shape.low
    least = shape.part.bit_length() - 1

    def body(angle, ref, mixed, flipped):
        sine, cosine = half_angle(jnp.full((1, 1), angle[which], F32))
        real, imag = mixer_mats(low, cosine, sine, least)
        row_high, row_low = split(jnp.concatenate([real, imag], axis=0))
        row_flip = flip_mat(low, least)
        blocks = [ref[i * low : (i + 1) * low, :] for i in range(shape.planes)]
        for i, (re, im) in enumerate(rotate_all(blocks, None, None, row_high, row_low, cosine, sine)):
            mixed[i * low : (i + 1) * low, :LANES] = re
            mixed[i * low : (i + 1) * low, LANES:] = im
        for i, block in enumerate(flips_all(blocks, None, row_flip)):
            flipped[i * low : (i + 1) * low, :] = block

    return vmem_call(
        body, [((shape.rows, 2 * LANES), F32)] * 2, smem_inputs=(angles,), inputs=(state,)
    )


def plain_cross(lam, other):
    def body(lam_ref, other_ref, out):
        out[...] = cross_imag(lam_ref[...], other_ref[...])

    return vmem_call(body, [((1, LANES), F32)], inputs=(lam, other))[0]


def plain_phase(shape, state, field, gradient):
    def body(ref, cost, cosine, sine, out):
        real, imag = ref[:, :LANES], ref[:, LANES:]
        if gradient:
            re, im = cost[...] * real, cost[...] * imag
        else:
            re, im = phased(real, imag, cosine[...], sine[...])
        out[:, :LANES] = re
        out[:, LANES:] = im

    return vmem_call(body, [((shape.rows, 2 * LANES), F32)], inputs=(state,) + tuple(field))[0]


def plain_mid(shape, angles, state, field_b, mats):
    low = shape.low

    def body(angle, ref, cos_b, sin_b, *rest):
        blocks = [ref[i * low : (i + 1) * low, :] for i in range(shape.planes)]
        for out, pairs in zip(rest[8:], mid_math(shape, angle, blocks, rest[:8], cos_b, sin_b)):
            for i, (re, im) in enumerate(pairs):
                out[i * low : (i + 1) * low, :LANES] = re
                out[i * low : (i + 1) * low, LANES:] = im

    return vmem_call(
        body,
        [((shape.rows, 2 * LANES), F32)] * 2,
        smem_inputs=(angles,),
        inputs=(state, field_b[1], field_b[2]) + tuple(mats[0]) + tuple(mats[1]),
    )


def exchange_all(shape, state):
    block = state.reshape(shape.devices, -1, 2 * LANES)
    return lax.all_to_all(block, ("grp", "z", "core"), 0, 0, tiled=True).reshape(state.shape)


def plain(shape, forward, adjoint, edges, weights, layout, slab_bits, angles):
    rows = shape.rows

    def wide(array):
        return array.reshape(2, rows, LANES).transpose(1, 0, 2).reshape(rows, 2 * LANES)

    def narrow(array):
        return array.reshape(rows, 2, LANES).transpose(1, 0, 2).reshape(2, rows * LANES)

    def device():
        return shape.piece(lax.axis_index("grp") * CORES + lax.axis_index("core"), lax.axis_index("z"))

    def before(row):
        return device() * rows + row

    def beyond(row):
        return (row // shape.part) * rows + device() * shape.part + row % shape.part

    small = (angles, edges, weights.reshape(-1, 1), layout.reshape(1, -1), slab_bits.reshape(1, -1))
    field_a, field_b, mats = make_tables(*small, rows, shape.low, before, beyond, shape.known)
    psi, flips = piece_mix(shape, angles, 3, wide(forward))
    lam, _ = piece_mix(shape, angles, 3, wide(adjoint))
    early = plain_cross(wide(adjoint), flips)
    psi_before, psi_after = plain_mid(shape, angles, exchange_all(shape, psi), field_b, mats)
    lam_before, lam_after = plain_mid(shape, angles, exchange_all(shape, lam), field_b, mats)
    mid_part = gradients_mid(shape, field_b[0], psi_before, lam_before, [psi_after], [lam_after], True)
    psi, lam = exchange_all(shape, psi_after), exchange_all(shape, lam_after)
    psi_mixed, flips = piece_mix(shape, angles, 1, psi)
    lam_mixed, _ = piece_mix(shape, angles, 1, lam)
    late = jnp.concatenate(
        [plain_cross(lam_mixed, plain_phase(shape, psi_mixed, field_a, True)), plain_cross(lam, flips)], axis=0
    )
    grads = total_grads(shape, (early, mid_part, late))
    outs = [narrow(plain_phase(shape, state, field_a, False)) for state in (psi_mixed, lam_mixed)]
    return outs[0], outs[1], grads


def interleave(array, rows):
    return array.reshape(2, rows, LANES).transpose(1, 0, 2).reshape(2 * rows, LANES)


def deinterleave(array, rows):
    return array.reshape(rows, 2, LANES).transpose(1, 0, 2).reshape(2, rows * LANES)


def places(shape):
    def device():
        return shape.piece(lax.axis_index("grp") * CORES + lax.axis_index("core"), lax.axis_index("z"))

    def before(row):
        return device() * shape.rows + row

    def beyond(row):
        slot, inner = row // shape.part, row % shape.part
        source = shape.piece(slot % shape.wide, jnp.bitwise_xor(slot // shape.wide, lax.axis_index("z")))
        return source * shape.rows + device() * shape.part + inner

    return before, beyond


def pipelined(shape, forward, adjoint, edges, weights, layout, slab_bits, angles):
    rows = shape.rows
    psi_raw, lam_raw = interleave(forward, rows), interleave(adjoint, rows)
    psi = pre(shape, angles, psi_raw, True)
    psi = send_levels(shape, psi)
    lam = pre(shape, angles, lam_raw, False)
    lam = send_wide(shape, lam[0])
    before, beyond = places(shape)
    small = after((angles, edges, weights.reshape(-1, 1), layout.reshape(1, -1), slab_bits.reshape(1, -1)), psi[0])
    field_a, field_b, mats = make_tables(*small, rows, shape.low, before, beyond, shape.known)
    early = flip_pre(shape, psi_raw, lam_raw)
    lam = swap_order(shape, [lam], False)
    lam = send_levels(shape, lam)
    psi = send_wide(shape, swap_order(shape, psi, True))
    psi_before, psi = mid(shape, angles, [psi], field_b, mats, True)
    psi_after = psi
    psi = send_levels(shape, psi)
    lam_before, lam = mid(shape, angles, lam, field_b, mats, False)
    lam_after = lam
    lam = send_wide(shape, lam[0])
    mid_part = gradients_mid(shape, field_b[0], psi_before, lam_before, psi_after, lam_after)
    lam = swap_order(shape, [lam], False)
    lam = send_levels(shape, lam)
    psi = send_wide(shape, swap_order(shape, psi, True))
    psi_mixed, psi_flips = post_mix(shape, angles, [psi])
    lam_mixed, late = post_mix_grads(shape, angles, lam, psi_mixed, psi_flips, field_a[0])
    grads = total_grads(shape, (early, mid_part, late))
    psi_out = post_phase(shape, psi_mixed, field_a)
    lam_out = post_phase(shape, lam_mixed, field_a)
    return deinterleave(psi_out, rows), deinterleave(lam_out, rows), grads


def solution(mesh):
    groups, rest = mesh.shape["grp"], mesh.shape["rep"]
    depth = rest // CORES
    fine = Mesh(mesh.devices.reshape(groups, depth, CORES), ("grp", "z", "core"))

    def per_device(forward, *others):
        shape = Shape(groups, depth, forward.shape[1])
        whole_tiles = shape.part % TILE == 0
        return (pipelined if whole_tiles else plain)(shape, forward, *others)

    state = P(None, ("grp", "z", "core"))
    return jax.shard_map(
        per_device,
        mesh=fine,
        in_specs=(state, state, P(), P(), P(), P(), P()),
        out_specs=(state, state, P()),
        check_vma=False,
    )
```

profile of v0, /device:TPU:0, one launch (start us, length us, event | category | flops | bytes accessed | tf_op | source)
XLA Modules:
  0.0 115.4 jit_solution(7890586003658220781)
XLA Ops:
  0.6 0.6 copy-done.31
  1.3 1.0 copy-done.1
  2.3 1.6 %shard_map.101 = f32[1024,128]{1,0:T(8,128)} custom-call(f32[4]{0:T(128)S(1)} %copy-done.31, f32[1024,128]{1,0:T(8,128)S(1)} %bitcast.38), custom_call_target="tpu_custom_call" | custom-call | tf_op jit(solution)/shard_map/pallas_call | solution.py:22
  3.9 5.3 %all-to-all-start.2 = ((f32[8,128,128]{2,1,0:T(8,128)}), f32[8,128,128]{2,1,0:T(8,128)S(1)}, u32[]{:S(2)}, u32[]{:S(2)}) async-start(f32[8,128,128]{2,1,0:T(8,128)} %bitcast.16), calls=%async_computation.2 | async-start | bytes 1048576 | tf_op jit(solution)/shard_map/all_to_all | solution.py:566
  9.2 0.8 shard_map.94
  10.0 1.6 %collective-permute-start = (f32[256,128]{1,0:T(8,128)S(1)}, f32[256,128]{1,0:T(8,128)S(1)}, u32[]{:S(2)}, u32[]{:S(2)}) collective-permute-start(f32[256,128]{1,0:T(8,128)S(1)} %get-tuple-element.46), channel_id=1, source_target_pairs={{0,2},{2,0},{4,6},{6,4},{1,3},{3,1},{5,7},{7,5},{8,10},{10,8},{12,... | collective-permute-start | bytes 393224 | tf_op jit(solution)/shard_map/ppermute | solution.py:560
  11.6 2.6 %collective-permute-start.1 = (f32[256,128]{1,0:T(8,128)S(1)}, f32[256,128]{1,0:T(8,128)S(1)}, u32[]{:S(2)}, u32[]{:S(2)}) collective-permute-start(f32[256,128]{1,0:T(8,128)S(1)} %get-tuple-element.47), channel_id=1, source_target_pairs={{0,4},{2,6},{4,0},{6,2},{1,5},{3,7},{5,1},{7,3},{8,12},{10,14},{12... | collective-permute-start | bytes 393224 | tf_op jit(solution)/shard_map/ppermute | solution.py:560
  14.2 0.2 collective-permute-start.2
  14.4 3.8 %collective-permute-done.refs_1_ = f32[256,128]{1,0:T(8,128)S(1)} collective-permute-done((f32[256,128]{1,0:T(8,128)S(1)}, f32[256,128]{1,0:T(8,128)S(1)}, u32[]{:S(2)}, u32[]{:S(2)}) %collective-permute-start) | collective-permute-done | bytes 131104 | tf_op jit(solution)/shard_map/ppermute | solution.py:560
  18.3 6.2 %collective-permute-done.1.refs_2_ = f32[256,128]{1,0:T(8,128)S(1)} collective-permute-done((f32[256,128]{1,0:T(8,128)S(1)}, f32[256,128]{1,0:T(8,128)S(1)}, u32[]{:S(2)}, u32[]{:S(2)}) %collective-permute-start.1) | collective-permute-done | bytes 131104 | tf_op jit(solution)/shard_map/ppermute | solution.py:560
  24.5 0.8 shard_map.95
  25.4 4.2 %all-to-all-start = ((f32[8,128,128]{2,1,0:T(8,128)}), f32[8,128,128]{2,1,0:T(8,128)S(1)}, u32[]{:S(2)}, u32[]{:S(2)}) async-start(f32[8,128,128]{2,1,0:T(8,128)} %bitcast.3), calls=%async_computation | async-start | bytes 1048576 | tf_op jit(solution)/shard_map/all_to_all | solution.py:566
  29.6 0.8 shard_map.102
  30.4 0.6 copy-done.21
  31.0 2.3 %collective-permute-start.6 = (f32[256,128]{1,0:T(8,128)}, f32[256,128]{1,0:T(8,128)}, u32[]{:S(2)}, u32[]{:S(2)}) collective-permute-start(f32[256,128]{1,0:T(8,128)} %get-tuple-element.72), channel_id=1, source_target_pairs={{0,2},{2,0},{4,6},{6,4},{1,3},{3,1},{5,7},{7,5},{8,10},{10,8},{12,... | collective-permute-start | bytes 393224 | tf_op jit(solution)/shard_map/ppermute | solution.py:560
  33.3 1.0 collective-permute-start.7
  34.3 1.5 %collective-permute-start.8 = (f32[256,128]{1,0:T(8,128)}, f32[256,128]{1,0:T(8,128)}, u32[]{:S(2)}, u32[]{:S(2)}) collective-permute-start(f32[256,128]{1,0:T(8,128)} %get-tuple-element.74), channel_id=1, source_target_pairs={{0,6},{2,4},{4,2},{6,0},{1,7},{3,5},{5,3},{7,1},{8,14},{10,12},{12... | collective-permute-start | bytes 393224 | tf_op jit(solution)/shard_map/ppermute | solution.py:560
  35.8 0.7 copy.11.edges
  36.5 0.7 copy.12.weights
  37.2 0.8 copy-done.23
  38.0 0.8 copy-done.24
  38.7 4.5 %shard_map.96 = (f32[512,128]{1,0:T(8,128)S(1)}, f32[512,128]{1,0:T(8,128)S(1)}, f32[512,128]{1,0:T(8,128)S(1)}, f32[512,128]{1,0:T(8,128)S(1)}, f32[512,128]{1,...) custom-call(f32[4]{0:T(128)S(1)} %copy-done.31, ...), custom_call_target="tpu_custom_call" | custom-call | tf_op jit(solution)/shard_map/pallas_call | solution.py:22
  43.2 0.7 copy-done.17
  44.0 0.7 copy-done.19
  44.7 1.8 %collective-permute-done.7.refs_3_ = f32[256,128]{1,0:T(8,128)} collective-permute-done((f32[256,128]{1,0:T(8,128)}, f32[256,128]{1,0:T(8,128)}, u32[]{:S(2)}, u32[]{:S(2)}) %collective-permute-start.7) | collective-permute-done | bytes 131104 | tf_op jit(solution)/shard_map/ppermute | solution.py:560
  46.5 3.7 %shard_map.103 = (f32[512,256]{1,0:T(8,128)S(1)}, f32[1024,128]{1,0:T(8,128)}) custom-call(f32[4]{0:T(128)S(1)} %copy-done.31, f32[256,128]{1,0:T(8,128)S(1)} %copy-done.22, f32[256,128]{1,0:T(8,128)} %collective-permute-done.6.refs_2_, f32[256,128]{1,0:T(8,128)} %collective-permute-done.7.refs_3_, f32[256,128]{1,0:T(8,128)} %collective-permute-done.8.refs_4_, ...), custom_call_target="tpu_custom_call" | custom-call | tf_op jit(solution)/shard_map/pallas_call | solution.py:22
  50.3 0.6 copy-done.5
  50.9 0.6 copy-done.7
  51.6 0.8 copy-done.11
  52.4 4.2 %all-to-all-start.3 = ((f32[8,128,128]{2,1,0:T(8,128)}), f32[8,128,128]{2,1,0:T(8,128)S(1)}, u32[]{:S(2)}, u32[]{:S(2)}) async-start(f32[8,128,128]{2,1,0:T(8,128)} %bitcast.18), calls=%async_computation.3 | async-start | bytes 1048576 | tf_op jit(solution)/shard_map/all_to_all | solution.py:566
  56.6 0.9 copy-done.4
  57.5 0.9 copy-done.6
  58.4 0.9 copy-done.8
  59.3 0.9 copy-done.10
  60.2 2.5 %shard_map.97 = (f32[512,256]{1,0:T(8,128)S(1)}, f32[256,128]{1,0:T(8,128)S(1)}, f32[256,128]{1,0:T(8,128)S(1)}, f32[256,128]{1,0:T(8,128)S(1)}, f32[256,128]{1,0:T(8,128)S(1)}) custom-call(f32[4]{0:T(128)S(1)} %copy-done.31, f32[1024,128]{1,0:T(8,128)S(1)} %bitcast.40, f32[512,128]{1,0:T(8,128)S(1)} %get-tuple-element.54.refs_2_.refs_5_, ...), custom_call_target="tpu_custom_call" | custom-call | tf_op jit(solution)/shard_map/pallas_call | solution.py:22
  62.7 0.8 copy-done.13
  63.5 2.3 %collective-permute-start.3 = (f32[256,128]{1,0:T(8,128)S(1)}, f32[256,128]{1,0:T(8,128)S(1)}, u32[]{:S(2)}, u32[]{:S(2)}) collective-permute-start(f32[256,128]{1,0:T(8,128)S(1)} %get-tuple-element.65.refs_4_), channel_id=1, source_target_pairs={{0,2},{2,0},{4,6},{6,4},{1,3},{3,1},{5,7},{7,5},{8,10},{10,8},{12,... | collective-permute-start | bytes 393224 | tf_op jit(solution)/shard_map/ppermute | solution.py:560
  65.8 0.6 copy-done.25
  66.4 1.0 collective-permute-start.4
  67.4 0.6 copy-done.27
  68.1 1.5 %collective-permute-start.5 = (f32[256,128]{1,0:T(8,128)S(1)}, f32[256,128]{1,0:T(8,128)S(1)}, u32[]{:S(2)}, u32[]{:S(2)}) collective-permute-start(f32[256,128]{1,0:T(8,128)S(1)} %get-tuple-element.67.refs_6_), channel_id=1, source_target_pairs={{0,6},{2,4},{4,2},{6,0},{1,7},{3,5},{5,3},{7,1},{8,14},{10,12},{12... | collective-permute-start | bytes 393224 | tf_op jit(solution)/shard_map/ppermute | solution.py:560
  69.5 0.6 copy-done.29
  70.2 9.1 %collective-permute-done.4.refs_2_ = f32[256,128]{1,0:T(8,128)S(1)} collective-permute-done((f32[256,128]{1,0:T(8,128)S(1)}, f32[256,128]{1,0:T(8,128)S(1)}, u32[]{:S(2)}, u32[]{:S(2)}) %collective-permute-start.4) | collective-permute-done | bytes 131104 | tf_op jit(solution)/shard_map/ppermute | solution.py:560
  79.3 0.8 shard_map.98
  80.1 0.7 copy-done.15
  80.8 4.4 %all-to-all-start.1 = ((f32[8,128,128]{2,1,0:T(8,128)}), f32[8,128,128]{2,1,0:T(8,128)S(1)}, u32[]{:S(2)}, u32[]{:S(2)}) async-start(f32[8,128,128]{2,1,0:T(8,128)} %bitcast.8), calls=%async_computation.1 | async-start | bytes 1048576 | tf_op jit(solution)/shard_map/all_to_all | solution.py:566
  85.2 0.8 shard_map.104
  86.0 3.2 %collective-permute-start.10 = (f32[256,128]{1,0:T(8,128)}, f32[256,128]{1,0:T(8,128)S(1)}, u32[]{:S(2)}, u32[]{:S(2)}) collective-permute-start(f32[256,128]{1,0:T(8,128)} %get-tuple-element.78), channel_id=1, source_target_pairs={{0,4},{2,6},{4,0},{6,2},{1,5},{3,7},{5,1},{7,3},{8,12},{10,14},{12... | collective-permute-start | bytes 393224 | tf_op jit(solution)/shard_map/ppermute | solution.py:560
  89.2 1.4 %collective-permute-start.11 = (f32[256,128]{1,0:T(8,128)}, f32[256,128]{1,0:T(8,128)S(1)}, u32[]{:S(2)}, u32[]{:S(2)}) collective-permute-start(f32[256,128]{1,0:T(8,128)} %get-tuple-element.79), channel_id=1, source_target_pairs={{0,6},{2,4},{4,2},{6,0},{1,7},{3,5},{5,3},{7,1},{8,14},{10,12},{12... | collective-permute-start | bytes 393224 | tf_op jit(solution)/shard_map/ppermute | solution.py:560
  90.6 0.1 shard_map.107.refs_0_
  90.8 0.9 copy-done.12
  91.7 0.2 copy-done.14
  91.8 1.9 %shard_map.108.refs_1_ = f32[3,128]{1,0:T(4,128)S(1)} custom-call(f32[512,128]{1,0:T(8,128)S(1)} %copy-done.20, f32[512,256]{1,0:T(8,128)S(1)} %copy-done.14, f32[512,256]{1,0:T(8,128)S(1)} %copy-done.12, f32[256,128]{1,0:T(8,128)S(1)} %copy-done.16, f32[256,128]{1,0:T(8,128)S(1)} %copy-done.26, f32[256,128]{1,0:T(8,128)S(1)} %copy-done.28, ...), custom_call_target="tpu_custom_call" | custom-call | tf_op jit(solution)/shard_map/pallas_call | solution.py:22
  93.8 1.2 %all-to-all-done.1 = f32[8,128,128]{2,1,0:T(8,128)S(1)} async-done(((f32[8,128,128]{2,1,0:T(8,128)}), f32[8,128,128]{2,1,0:T(8,128)S(1)}, u32[]{:S(2)}, u32[]{:S(2)}) %all-to-all-start.1) | async-done | bytes 524320 | tf_op jit(solution)/shard_map/all_to_all | solution.py:566
  95.0 0.8 shard_map.99
  95.8 3.6 %collective-permute-done.10.refs_3_ = f32[256,128]{1,0:T(8,128)S(1)} collective-permute-done((f32[256,128]{1,0:T(8,128)}, f32[256,128]{1,0:T(8,128)S(1)}, u32[]{:S(2)}, u32[]{:S(2)}) %collective-permute-start.10) | collective-permute-done | bytes 131104 | tf_op jit(solution)/shard_map/ppermute | solution.py:560
  99.4 1.1 collective-permute-done.9.refs_2_
  100.6 0.9 shard_map.105
  101.5 0.7 shard_map.109
  102.1 4.4 %all-to-all-start.4 = ((f32[32,8,128]{2,1,0:T(8,128)}), f32[32,8,128]{2,1,0:T(8,128)S(1)}, u32[]{:S(2)}, u32[]{:S(2)}) async-start(f32[32,8,128]{2,1,0:T(8,128)} %bitcast.27), calls=%async_computation.4 | async-start | bytes 262144 | tf_op jit(solution)/shard_map/all_to_all | solution.py:580
  106.6 0.9 shard_map.100
  107.4 0.9 shard_map.106
  108.3 6.4 %all-to-all-done.4 = f32[32,8,128]{2,1,0:T(8,128)S(1)} async-done(((f32[32,8,128]{2,1,0:T(8,128)}), f32[32,8,128]{2,1,0:T(8,128)S(1)}, u32[]{:S(2)}, u32[]{:S(2)}) %all-to-all-start.4) | async-done | bytes 131104 | tf_op jit(solution)/shard_map/all_to_all | solution.py:580
  114.7 0.7 shard_map.110
  (61 shorter events, 0.1 us)
Async XLA Ops:
  0.6 0.7 copy-start.31
  1.3 1.0 copy-start.1
  3.9 5.3 %copy-start = (f32[2,65536]{1,0:T(2,128)S(1)}, f32[2,65536]{1,0:T(2,128)}, u32[]{:S(2)}) copy-start(f32[2,65536]{1,0:T(2,128)} %param.7) | copy-start | bytes 1572868
  3.9 21.5 %all-to-all-start.2 = ((f32[8,128,128]{2,1,0:T(8,128)}), f32[8,128,128]{2,1,0:T(8,128)S(1)}, u32[]{:S(2)}, u32[]{:S(2)}) async-start(f32[8,128,128]{2,1,0:T(8,128)} %bitcast.16), calls=%async_computation.2 | async-start | bytes 1048576 | tf_op jit(solution)/shard_map/all_to_all | solution.py:566
  10.0 8.3 %collective-permute-start = (f32[256,128]{1,0:T(8,128)S(1)}, f32[256,128]{1,0:T(8,128)S(1)}, u32[]{:S(2)}, u32[]{:S(2)}) collective-permute-start(f32[256,128]{1,0:T(8,128)S(1)} %get-tuple-element.46), channel_id=1, source_target_pairs={{0,2},{2,0},{4,6},{6,4},{1,3},{3,1},{5,7},{7,5},{8,10},{10,8},{12,... | collective-permute-start | bytes 393224 | tf_op jit(solution)/shard_map/ppermute | solution.py:560
  11.6 12.9 %collective-permute-start.1 = (f32[256,128]{1,0:T(8,128)S(1)}, f32[256,128]{1,0:T(8,128)S(1)}, u32[]{:S(2)}, u32[]{:S(2)}) collective-permute-start(f32[256,128]{1,0:T(8,128)S(1)} %get-tuple-element.47), channel_id=1, source_target_pairs={{0,4},{2,6},{4,0},{6,2},{1,5},{3,7},{5,1},{7,3},{8,12},{10,14},{12... | collective-permute-start | bytes 393224 | tf_op jit(solution)/shard_map/ppermute | solution.py:560
  14.2 10.3 %collective-permute-start.2 = (f32[256,128]{1,0:T(8,128)S(1)}, f32[256,128]{1,0:T(8,128)S(1)}, u32[]{:S(2)}, u32[]{:S(2)}) collective-permute-start(f32[256,128]{1,0:T(8,128)S(1)} %get-tuple-element.48), channel_id=1, source_target_pairs={{0,6},{2,4},{4,2},{6,0},{1,7},{3,5},{5,3},{7,1},{8,14},{10,12},{12... | collective-permute-start | bytes 393224 | tf_op jit(solution)/shard_map/ppermute | solution.py:560
  25.4 27.0 %all-to-all-start = ((f32[8,128,128]{2,1,0:T(8,128)}), f32[8,128,128]{2,1,0:T(8,128)S(1)}, u32[]{:S(2)}, u32[]{:S(2)}) async-start(f32[8,128,128]{2,1,0:T(8,128)} %bitcast.3), calls=%async_computation | async-start | bytes 1048576 | tf_op jit(solution)/shard_map/all_to_all | solution.py:566
  29.6 6.2 %copy-start.34 = (s32[60,2]{0,1:T(2,128)S(1)}, s32[60,2]{0,1:T(2,128)}, u32[]{:S(2)}) copy-start(s32[60,2]{0,1:T(2,128)} %param.9) | copy-start | bytes 1444
  29.6 6.9 %copy-start.35 = (s32[60]{0:T(128)S(1)}, s32[60]{0:T(128)}, u32[]{:S(2)}) copy-start(s32[60]{0:T(128)} %param.10) | copy-start | bytes 724
  29.6 7.6 %copy-start.32 = (s32[40]{0:T(128)S(1)}, s32[40]{0:T(128)}, u32[]{:S(2)}) copy-start(s32[40]{0:T(128)} %param.11) | copy-start | bytes 484
  29.6 7.6 %copy-start.33 = (s32[40]{0:T(128)S(1)}, s32[40]{0:T(128)}, u32[]{:S(2)}) copy-start(s32[40]{0:T(128)} %param.12) | copy-start | bytes 484
  30.4 0.6 copy-start.21
  31.0 15.5 %copy-start.22 = (f32[256,128]{1,0:T(8,128)S(1)}, f32[256,128]{1,0:T(8,128)}, u32[]{:S(2)}) copy-start(f32[256,128]{1,0:T(8,128)} %copy-done.21) | copy-start | bytes 393220
  31.0 13.7 %collective-permute-start.6 = (f32[256,128]{1,0:T(8,128)}, f32[256,128]{1,0:T(8,128)}, u32[]{:S(2)}, u32[]{:S(2)}) collective-permute-start(f32[256,128]{1,0:T(8,128)} %get-tuple-element.72), channel_id=1, source_target_pairs={{0,2},{2,0},{4,6},{6,4},{1,3},{3,1},{5,7},{7,5},{8,10},{10,8},{12,... | collective-permute-start | bytes 393224 | tf_op jit(solution)/shard_map/ppermute | solution.py:560
  33.3 13.2 %collective-permute-start.7 = (f32[256,128]{1,0:T(8,128)}, f32[256,128]{1,0:T(8,128)}, u32[]{:S(2)}, u32[]{:S(2)}) collective-permute-start(f32[256,128]{1,0:T(8,128)} %get-tuple-element.73), channel_id=1, source_target_pairs={{0,4},{2,6},{4,0},{6,2},{1,5},{3,7},{5,1},{7,3},{8,12},{10,14},{12... | collective-permute-start | bytes 393224 | tf_op jit(solution)/shard_map/ppermute | solution.py:560
  34.3 12.2 %collective-permute-start.8 = (f32[256,128]{1,0:T(8,128)}, f32[256,128]{1,0:T(8,128)}, u32[]{:S(2)}, u32[]{:S(2)}) collective-permute-start(f32[256,128]{1,0:T(8,128)} %get-tuple-element.74), channel_id=1, source_target_pairs={{0,6},{2,4},{4,2},{6,0},{1,7},{3,5},{5,3},{7,1},{8,14},{10,12},{12... | collective-permute-start | bytes 393224 | tf_op jit(solution)/shard_map/ppermute | solution.py:560
  37.2 0.8 copy-start.23
  38.0 0.8 copy-start.24
  43.2 0.7 copy-start.17
  44.0 0.7 copy-start.19
  44.7 5.6 %copy-start.3 = (bf16[512,256]{1,0:T(8,128)(2,1)}, bf16[512,256]{1,0:T(8,128)(2,1)S(1)}, u32[]{:S(2)}) copy-start(bf16[512,256]{1,0:T(8,128)(2,1)S(1)} %get-tuple-element.63.refs_11_.refs_14_) | copy-start | bytes 786436
  44.7 5.6 %copy-start.9 = (bf16[256,256]{1,0:T(8,128)(2,1)}, bf16[256,256]{1,0:T(8,128)(2,1)S(1)}, u32[]{:S(2)}) copy-start(bf16[256,256]{1,0:T(8,128)(2,1)S(1)} %get-tuple-element.61.refs_9_.refs_12_) | copy-start | bytes 393220
  50.3 0.6 copy-start.5
  50.9 0.6 copy-start.7
  51.6 0.8 copy-start.11
  52.4 28.4 %all-to-all-start.3 = ((f32[8,128,128]{2,1,0:T(8,128)}), f32[8,128,128]{2,1,0:T(8,128)S(1)}, u32[]{:S(2)}, u32[]{:S(2)}) async-start(f32[8,128,128]{2,1,0:T(8,128)} %bitcast.18), calls=%async_computation.3 | async-start | bytes 1048576 | tf_op jit(solution)/shard_map/all_to_all | solution.py:566
  56.6 0.9 copy-start.4
  57.5 0.9 copy-start.6
  58.4 0.9 copy-start.8
  59.3 0.9 copy-start.10
  62.7 0.8 copy-start.13
  63.5 6.7 %collective-permute-start.3 = (f32[256,128]{1,0:T(8,128)S(1)}, f32[256,128]{1,0:T(8,128)S(1)}, u32[]{:S(2)}, u32[]{:S(2)}) collective-permute-start(f32[256,128]{1,0:T(8,128)S(1)} %get-tuple-element.65.refs_4_), channel_id=1, source_target_pairs={{0,2},{2,0},{4,6},{6,4},{1,3},{3,1},{5,7},{7,5},{8,10},{10,8},{12,... | collective-permute-start | bytes 393224 | tf_op jit(solution)/shard_map/ppermute | solution.py:560
  65.8 0.7 copy-start.25
  66.4 12.8 %collective-permute-start.4 = (f32[256,128]{1,0:T(8,128)S(1)}, f32[256,128]{1,0:T(8,128)S(1)}, u32[]{:S(2)}, u32[]{:S(2)}) collective-permute-start(f32[256,128]{1,0:T(8,128)S(1)} %get-tuple-element.66.refs_5_), channel_id=1, source_target_pairs={{0,4},{2,6},{4,0},{6,2},{1,5},{3,7},{5,1},{7,3},{8,12},{10,14},{12... | collective-permute-start | bytes 393224 | tf_op jit(solution)/shard_map/ppermute | solution.py:560
  67.4 0.6 copy-start.27
  68.1 11.2 %collective-permute-start.5 = (f32[256,128]{1,0:T(8,128)S(1)}, f32[256,128]{1,0:T(8,128)S(1)}, u32[]{:S(2)}, u32[]{:S(2)}) collective-permute-start(f32[256,128]{1,0:T(8,128)S(1)} %get-tuple-element.67.refs_6_), channel_id=1, source_target_pairs={{0,6},{2,4},{4,2},{6,0},{1,7},{3,5},{5,3},{7,1},{8,14},{10,12},{12... | collective-permute-start | bytes 393224 | tf_op jit(solution)/shard_map/ppermute | solution.py:560
  69.5 0.7 copy-start.29
  80.1 0.7 copy-start.15
  80.8 10.0 %copy-start.16 = (f32[256,128]{1,0:T(8,128)S(1)}, f32[256,128]{1,0:T(8,128)}, u32[]{:S(2)}) copy-start(f32[256,128]{1,0:T(8,128)} %copy-done.15) | copy-start | bytes 393220
  80.8 10.0 %copy-start.20 = (f32[512,128]{1,0:T(8,128)S(1)}, f32[512,128]{1,0:T(8,128)}, u32[]{:S(2)}) copy-start(f32[512,128]{1,0:T(8,128)} %copy-done.19) | copy-start | bytes 786436
  80.8 10.0 %copy-start.26 = (f32[256,128]{1,0:T(8,128)S(1)}, f32[256,128]{1,0:T(8,128)}, u32[]{:S(2)}) copy-start(f32[256,128]{1,0:T(8,128)} %copy-done.25) | copy-start | bytes 393220
  80.8 10.0 %copy-start.28 = (f32[256,128]{1,0:T(8,128)S(1)}, f32[256,128]{1,0:T(8,128)}, u32[]{:S(2)}) copy-start(f32[256,128]{1,0:T(8,128)} %copy-done.27) | copy-start | bytes 393220
  80.8 10.0 %copy-start.30 = (f32[256,128]{1,0:T(8,128)S(1)}, f32[256,128]{1,0:T(8,128)}, u32[]{:S(2)}) copy-start(f32[256,128]{1,0:T(8,128)} %copy-done.29) | copy-start | bytes 393220
  80.8 14.1 %all-to-all-start.1 = ((f32[8,128,128]{2,1,0:T(8,128)}), f32[8,128,128]{2,1,0:T(8,128)S(1)}, u32[]{:S(2)}, u32[]{:S(2)}) async-start(f32[8,128,128]{2,1,0:T(8,128)} %bitcast.8), calls=%async_computation.1 | async-start | bytes 1048576 | tf_op jit(solution)/shard_map/all_to_all | solution.py:566
  85.2 5.4 %copy-start.2 = (f32[2,65536]{1,0:T(2,128)S(1)}, f32[2,65536]{1,0:T(2,128)}, u32[]{:S(2)}) copy-start(f32[2,65536]{1,0:T(2,128)} %param.8) | copy-start | bytes 1572868
  86.0 13.4 %collective-permute-start.10 = (f32[256,128]{1,0:T(8,128)}, f32[256,128]{1,0:T(8,128)S(1)}, u32[]{:S(2)}, u32[]{:S(2)}) collective-permute-start(f32[256,128]{1,0:T(8,128)} %get-tuple-element.78), channel_id=1, source_target_pairs={{0,4},{2,6},{4,0},{6,2},{1,5},{3,7},{5,1},{7,3},{8,12},{10,14},{12... | collective-permute-start | bytes 393224 | tf_op jit(solution)/shard_map/ppermute | solution.py:560
  89.2 10.2 %collective-permute-start.11 = (f32[256,128]{1,0:T(8,128)}, f32[256,128]{1,0:T(8,128)S(1)}, u32[]{:S(2)}, u32[]{:S(2)}) collective-permute-start(f32[256,128]{1,0:T(8,128)} %get-tuple-element.79), channel_id=1, source_target_pairs={{0,6},{2,4},{4,2},{6,0},{1,7},{3,5},{5,3},{7,1},{8,14},{10,12},{12... | collective-permute-start | bytes 393224 | tf_op jit(solution)/shard_map/ppermute | solution.py:560
  90.6 1.0 copy-start.12
  90.6 1.2 %copy-start.14 = (f32[512,256]{1,0:T(8,128)S(1)}, f32[512,256]{1,0:T(8,128)}, u32[]{:S(2)}) copy-start(f32[512,256]{1,0:T(8,128)} %copy-done.13) | copy-start | bytes 1572868
  90.6 10.0 %collective-permute-start.9 = (f32[256,128]{1,0:T(8,128)}, f32[256,128]{1,0:T(8,128)S(1)}, u32[]{:S(2)}, u32[]{:S(2)}) collective-permute-start(f32[256,128]{1,0:T(8,128)} %get-tuple-element.77), channel_id=1, source_target_pairs={{0,2},{2,0},{4,6},{6,4},{1,3},{3,1},{5,7},{7,5},{8,10},{10,8},{12,... | collective-permute-start | bytes 393224 | tf_op jit(solution)/shard_map/ppermute | solution.py:560
  95.0 5.6 %copy-start.18 = (f32[512,128]{1,0:T(8,128)S(1)}, f32[512,128]{1,0:T(8,128)}, u32[]{:S(2)}) copy-start(f32[512,128]{1,0:T(8,128)} %copy-done.17) | copy-start | bytes 786436
  102.1 12.6 %all-to-all-start.4 = ((f32[32,8,128]{2,1,0:T(8,128)}), f32[32,8,128]{2,1,0:T(8,128)S(1)}, u32[]{:S(2)}, u32[]{:S(2)}) async-start(f32[32,8,128]{2,1,0:T(8,128)} %bitcast.27), calls=%async_computation.4 | async-start | bytes 262144 | tf_op jit(solution)/shard_map/all_to_all | solution.py:580
where the time goes:
time: 116 us; the launch traced here: 115 us
  starting transfers between devices  41.1 us (35%)
  waiting for transfers between devices  33.4 us (29%)
  Pallas kernels  23.1 us (20%)
  local copies, waits for them, and re-layouts  16.9 us (15%)
    ppermute x12, waiting for transfers between devices, send_levels(): out.append(lax.ppermute(arrays[k], 'z', pairs))  25.8 us
    pallas_call x17, Pallas kernels, vmem_call(): pl.pallas_call(body, out_shape=[jax.ShapeDtypeStruct(shape, kind) for sha...  23.1 us
    ppermute x12, starting transfers between devices, send_levels(): out.append(lax.ppermute(arrays[k], 'z', pairs))  18.6 us
    all_to_all x4, starting transfers between devices, send_wide(): lax.all_to_all(block, ('grp', 'core'), 0, 0, tiled=True)  18.1 us
    unnamed x72, local copies, waits for them, and re-layouts  15.5 us
    all_to_all x1, waiting for transfers between devices, total_grads(): lax.all_to_all(block.reshape(count, TILE, LANES), ('grp', 'z', 'core'), 0...  6.4 us
    all_to_all x1, starting transfers between devices, total_grads(): lax.all_to_all(block.reshape(count, TILE, LANES), ('grp', 'z', 'core'), 0...  4.42 us
  transfers between devices with their start and end apart: 17, of which 8 were waited for; matrix products, arithmetic and copies ran while one was open for 1% of the time, Pallas kernels for 17%

commit v1 on v0

v1 whole, which is shorter than its diff:
```python
import jax
import jax.numpy as jnp
from jax import lax
from jax.experimental import pallas as pl
from jax.experimental.pallas import tpu as pltpu
from jax.sharding import Mesh, PartitionSpec as P

NODES = 40
LAYERS = 2
LANES = 128
TILE = 8
CORES = 2
F32 = jnp.float32
BF16 = jnp.bfloat16
VMEM_LIMIT = 12 << 20
VMEM_FIRST = 62 << 20


def vmem_call(name, body, out_shapes, inputs=(), smem_out=False, hold=()):
    if hold:
        taken = len(inputs)
        inner = body

        def body(*refs):
            inner(*refs[:taken], *refs[taken + len(hold) :])

        inputs = tuple(inputs) + tuple(hold)
    specs = [pl.BlockSpec(memory_space=pltpu.VMEM)] * len(inputs)
    place = pltpu.SMEM if smem_out else pltpu.VMEM
    return pl.pallas_call(
        body,
        name=name,
        out_shape=[jax.ShapeDtypeStruct(shape, kind) for shape, kind in out_shapes],
        in_specs=specs,
        out_specs=[pl.BlockSpec(memory_space=place)] * len(out_shapes),
        compiler_params=pltpu.CompilerParams(vmem_limit_bytes=VMEM_LIMIT),
    )(*inputs)


def half_angle(x):
    y = 0.5 * x
    z = y * y
    sin_y = jnp.full_like(z, -1.0 / 1307674368000.0)
    for factor in (6227020800.0, -39916800.0, 362880.0, -5040.0, 120.0, -6.0, 1.0):
        sin_y = sin_y * z + 1.0 / factor
    sin_y = sin_y * y
    cos_y = jnp.full_like(z, 1.0 / 20922789888000.0)
    for factor in (-87178291200.0, 479001600.0, -3628800.0, 40320.0, -720.0, 24.0, -2.0, 1.0):
        cos_y = cos_y * z + 1.0 / factor
    return 2.0 * sin_y * cos_y, 1.0 - 2.0 * sin_y * sin_y


def split(value):
    high = value.astype(BF16)
    return high, (value - high.astype(F32)).astype(BF16)


def dot(left, right):
    return jnp.dot(left, right, preferred_element_type=F32)


def mixer_mats(size, cos_beta, sin_beta, least=0):
    row = lax.broadcasted_iota(jnp.int32, (size, size), 0)
    col = lax.broadcasted_iota(jnp.int32, (size, size), 1)
    differ = jnp.bitwise_xor(row, col)
    real = jnp.ones((size, size), F32)
    real = jnp.where(jnp.bitwise_and(differ, (1 << least) - 1) == 0, real, 0.0)
    imag = jnp.zeros((size, size), F32)
    for bit in range(least, size.bit_length() - 1):
        flagged = jnp.bitwise_and(differ, 1 << bit) != 0
        real, imag = (
            jnp.where(flagged, -imag * sin_beta, real * cos_beta),
            jnp.where(flagged, real * sin_beta, imag * cos_beta),
        )
    return real, imag


def flip_mat(size, least=0):
    row = lax.broadcasted_iota(jnp.int32, (size, size), 0)
    col = lax.broadcasted_iota(jnp.int32, (size, size), 1)
    differ = jnp.bitwise_xor(row, col)
    count = jnp.zeros((size, size), jnp.int32)
    for bit in range(size.bit_length() - 1):
        count = count + jnp.bitwise_and(differ >> bit, 1)
    rest = jnp.bitwise_and(differ, (1 << least) - 1)
    return jnp.where(jnp.logical_and(count == 1, rest == 0), 1.0, 0.0).astype(BF16)


def rotate_all(planes, lane_high, lane_low, row_high, row_low, cos_beta, sin_beta):
    low = planes[0].shape[0]
    mixed = []
    for block in planes:
        high, rest = split(block)
        if lane_high is not None:
            lanes = dot(high, lane_high) + dot(rest, lane_high) + dot(high, lane_low)
            high, rest = split(lanes)
        both = dot(row_high, high) + dot(row_high, rest) + dot(row_low, high)
        real = both[:low, :LANES] - both[low:, LANES:]
        imag = both[:low, LANES:] + both[low:, :LANES]
        mixed.append((real, imag))
    stride = 1
    while stride < len(mixed):
        for first in range(len(mixed)):
            if first & stride:
                continue
            (ar, ai), (br, bi) = mixed[first], mixed[first + stride]
            mixed[first] = (cos_beta * ar - sin_beta * bi, cos_beta * ai + sin_beta * br)
            mixed[first + stride] = (cos_beta * br - sin_beta * ai, cos_beta * bi + sin_beta * ar)
        stride *= 2
    return mixed


def flips_all(planes, lane_flip, row_flip):
    out = []
    for index, block in enumerate(planes):
        high, rest = split(block)
        total = dot(row_flip, high) + dot(row_flip, rest)
        if lane_flip is not None:
            total = total + dot(high, lane_flip) + dot(rest, lane_flip)
        stride = 1
        while stride < len(planes):
            total = total + planes[index ^ stride]
            stride *= 2
        out.append(total)
    return out


def fold_rows(value):
    folded = value[:TILE]
    for start in range(TILE, value.shape[0], TILE):
        folded = folded + value[start : start + TILE]
    return jnp.sum(folded, axis=0, keepdims=True)


def cross_imag(lam, other):
    return fold_rows(lam[:, :LANES] * other[:, LANES:] - lam[:, LANES:] * other[:, :LANES])


def spin_rows(position, layout, slab, known):
    lane_bits = LANES.bit_length() - 1
    shift = jnp.clip(layout - lane_bits, 0, known - 1)
    inside = jnp.bitwise_and(jnp.right_shift(position, shift), 1)
    bit = jnp.where(layout < known + lane_bits, inside, slab)
    return jnp.where(layout < lane_bits, 0, 1 - 2 * bit).astype(F32)


def field_body(place_first, place_second, known):
    lane_bits = LANES.bit_length() - 1

    def body(angles, edges, weights, layout, slab, cost_a, cos_a, sin_a, cost_b, cos_b, sin_b):
        node = lax.broadcasted_iota(jnp.int32, (NODES, edges.shape[1]), 0)
        first = jnp.where(edges[0:1, :] == node, 1.0, 0.0)
        second = jnp.where(edges[1:2, :] == node, 1.0, 0.0)
        weight = weights[...].astype(F32)
        total = jnp.sum(weight, axis=1, keepdims=True)
        exact = lax.Precision.HIGHEST

        def full(left, right, dims):
            return lax.dot_general(left, right, dims, precision=exact, preferred_element_type=F32)

        plain = (((1,), (0,)), ((), ()))
        turned = (((1,), (1,)), ((), ()))
        matrix = full(first * weight, second, turned) + full(second * weight, first, turned)
        lane = lax.broadcasted_iota(jnp.int32, (LANES, NODES), 0)
        lane_layout = layout[...]
        lane_bit = jnp.bitwise_and(jnp.right_shift(lane, jnp.clip(lane_layout, 0, lane_bits - 1)), 1)
        lane_spin = jnp.where(lane_layout < lane_bits, 1 - 2 * lane_bit, 0).astype(F32)
        lane_energy = full(jnp.ones((TILE, NODES), F32), lane_spin * full(lane_spin, matrix, plain), turned)[0:1]

        def field(position, cost, cos_out, sin_out, gamma):
            spins = spin_rows(position, lane_layout, slab[...], known)
            pulled = full(spins, matrix, plain)
            energy = jnp.sum(pulled * spins, axis=1, keepdims=True)
            energy = energy + lane_energy + 2.0 * full(pulled, lane_spin, turned)
            value = 2.0 - energy / total
            cost[...] = value
            sine, cosine = half_angle(gamma * value)
            cos_out[...] = cosine
            sin_out[...] = sine

        row = lax.broadcasted_iota(jnp.int32, (cost_a.shape[0], 1), 0)
        field(place_first(row), cost_a, cos_a, sin_a, angles[0:1, 0:1])
        row = lax.broadcasted_iota(jnp.int32, (cost_b.shape[0], 1), 0)
        field(place_second(row), cost_b, cos_b, sin_b, angles[0:1, 2:3])
    return body


def make_fields(angles, edges, weights, layout, slab, rows, place_first, place_second, known, core=None, hold=()):
    inner = field_body(place_first, place_second, known)
    shapes = [((rows[0], LANES), F32)] * 3 + [((rows[1], LANES), F32)] * 3
    small = (angles, edges, weights, layout, slab)
    held = tuple(hold)

    def body(*refs):
        refs = refs[: len(small)] + refs[len(small) + len(held) :]
        if core is None:
            inner(*refs)
        else:

            @pl.when(lax.axis_index("core") == core)
            def _():
                inner(*refs)

    return pl.pallas_call(
        body,
        name="make_fields",
        out_shape=[jax.ShapeDtypeStruct(size, kind) for size, kind in shapes],
        in_specs=[pl.BlockSpec(memory_space=pltpu.VMEM)] * (len(small) + len(held)),
        out_specs=[pl.BlockSpec(memory_space=pltpu.VMEM)] * len(shapes),
        input_output_aliases={len(small) + i: i for i in range(len(shapes))} if len(held) == len(shapes) else {},
        compiler_params=pltpu.CompilerParams(vmem_limit_bytes=VMEM_LIMIT),
    )(*small, *held)


def make_mats(angles, low, hold=()):
    def body(angles, *mats):
        for layer in range(LAYERS):
            sine, cosine = half_angle(angles[0:1, 2 * layer + 1 : 2 * layer + 2])
            real, imag = mixer_mats(LANES, cosine, sine)
            lanes = jnp.concatenate(
                [jnp.concatenate([real, imag], axis=1), jnp.concatenate([-imag, real], axis=1)], axis=0
            )
            mats[4 * layer][...], mats[4 * layer + 1][...] = split(lanes)
            real, imag = mixer_mats(low, cosine, sine)
            mats[4 * layer + 2][...], mats[4 * layer + 3][...] = split(jnp.concatenate([real, imag], axis=0))

    shapes = ([((2 * LANES, 2 * LANES), BF16)] * 2 + [((2 * low, low), BF16)] * 2) * LAYERS
    out = vmem_call("make_mats", body, shapes, inputs=(angles,), hold=hold)
    return [out[4 * layer : 4 + 4 * layer] for layer in range(LAYERS)]


def small_inputs(edges, weights, layout, slab_bits):
    return edges.T, weights.reshape(1, -1), layout.reshape(1, -1), slab_bits.reshape(1, -1)


class Shape:
    def __init__(self, groups, depth, amp_dev):
        self.groups = groups
        self.depth = depth
        self.devices = groups * depth * CORES
        self.rows = amp_dev // LANES
        self.known = (self.rows * self.devices).bit_length() - 1
        self.tiles = groups == depth and self.rows % (groups * depth * TILE) == 0
        self.part = self.rows // (groups * depth if self.tiles else self.devices)
        self.low = depth * self.part if self.tiles else min(self.rows, 2 * LANES)
        self.planes = self.rows // self.low

    def own(self):
        return self.chip() * CORES + lax.axis_index("core")

    def chip(self):
        return lax.axis_index("grp") * self.depth + lax.axis_index("z")

    def slots(self):
        return [(u, v) for u in range(self.depth) for v in range(self.depth)]

    def bits(self, letters):
        each = self.depth.bit_length() - 1
        return [bit + (each if letter == "u" else 0) for letter in letters for bit in range(each)]

    def piece(self):
        core = lax.axis_index("core")
        chip = self.chip()
        step_u = 1 + core * (self.depth - 1)
        step_v = self.depth - core * (self.depth - 1)
        return lambda u, v: jnp.bitwise_xor(chip, u * step_u + v * step_v)

    def array(self):
        return ((2 * self.rows // self.depth, LANES), F32)

    def whole(self):
        return ((2 * self.rows, LANES), F32)

    def place(self, form, refs, u, v):
        index, inner = {
            "u": (u, v),
            "v": (v, u),
            "all": (0, u * self.depth + v),
            "other": (0, v * self.depth + u),
        }[form]
        return refs[index], inner * 2 * self.part


def angle_pair(angles, which):
    return half_angle(jnp.broadcast_to(angles[0:1, which : which + 1], (TILE, LANES)))


def butterflies(real, imag, pair, bits):
    sine, cosine = pair
    tangent = sine / cosine
    scale = cosine
    for _ in bits[1:]:
        scale = scale * cosine
    for bit in bits:
        for first in range(len(real)):
            other = first | (1 << bit)
            if other == first:
                continue
            ar, ai, br, bi = real[first], imag[first], real[other], imag[other]
            real[first], imag[first] = ar - tangent * bi, ai + tangent * br
            real[other], imag[other] = br - tangent * ai, bi + tangent * ar
    return [scale * v for v in real], [scale * v for v in imag]


def flip_sum(values, index):
    total = None
    stride = 1
    while stride < len(values):
        term = values[index ^ stride]
        total = term if total is None else total + term
        stride *= 2
    return total


def load_slots(shape, form, refs, start, slots):
    real, imag = [], []
    for slot in slots:
        ref, base = shape.place(form, refs, *slot)
        real.append(ref[base + start : base + start + TILE, :])
        imag.append(ref[base + shape.part + start : base + shape.part + start + TILE, :])
    return real, imag


def store_slots(shape, form, refs, start, slots, real, imag):
    for slot, re, im in zip(slots, real, imag):
        ref, base = shape.place(form, refs, *slot)
        ref[base + start : base + start + TILE, :] = re
        ref[base + shape.part + start : base + shape.part + start + TILE, :] = im


def load_planes(shape, form, refs):
    planes = []
    for u in range(shape.depth):
        pairs = []
        for v in range(shape.depth):
            ref, base = shape.place(form, refs, u, v)
            middle = base + shape.part
            pairs.append(jnp.concatenate([ref[base:middle, :], ref[middle : middle + shape.part, :]], axis=1))
        planes.append(jnp.concatenate(pairs, axis=0))
    return planes


def store_planes(shape, form, refs, planes):
    for u, v in shape.slots():
        re, im = planes[u]
        at = v * shape.part
        ref, base = shape.place(form, refs, u, v)
        middle = base + shape.part
        ref[base:middle, :] = re[at : at + shape.part]
        ref[middle : middle + shape.part, :] = im[at : at + shape.part]


def phased(real, imag, cosine, sine):
    return real * cosine - imag * sine, imag * cosine + real * sine


def load_raw(ref, base):
    return ref[pl.ds(base, TILE, stride=2), :], ref[pl.ds(base + 1, TILE, stride=2), :]


def first_rotations(shape, angle, raw, outs):
    piece = shape.piece()
    pair = angle_pair(angle, 3)
    for start in range(0, shape.part, TILE):
        for v in range(shape.depth):
            slots = [(u, v) for u in range(shape.depth)]
            parts = [load_raw(raw, (piece(*slot) * shape.part + start) * 2) for slot in slots]
            real, imag = butterflies([p[0] for p in parts], [p[1] for p in parts], pair, shape.bits("v"))
            store_slots(shape, "u", outs, start, slots, real, imag)


COPIES = 4


def pre_near(shape, angles, psi, lam):
    step = 2 * shape.rows // COPIES

    def body(angle, psi_ref, lam_ref, own, send, *rest):
        outs, angle_here, sems = rest[:-2], rest[-2], rest[-1]
        fetch = pltpu.make_async_copy(angle, angle_here, sems.at[2 * COPIES])
        fetch.start()

        def copies(own_ref, send_ref):
            pairs = [(own_ref, own, 0), (send_ref, send, COPIES)]
            return [
                pltpu.make_async_copy(
                    source.at[pl.ds(i * step, step), :], target.at[pl.ds(i * step, step), :], sems.at[first + i]
                )
                for source, target, first in pairs
                for i in range(COPIES)
            ]

        @pl.when(lax.axis_index("core") == 0)
        def _():
            for copy in copies(psi_ref, lam_ref):
                copy.start()

        @pl.when(lax.axis_index("core") != 0)
        def _():
            for copy in copies(lam_ref, psi_ref):
                copy.start()

        waits = copies(psi_ref, lam_ref)
        fetch.wait()
        for copy in waits[:COPIES]:
            copy.wait()
        first_rotations(shape, angle_here, own, outs)
        for copy in waits[COPIES:]:
            copy.wait()

    shapes = [shape.whole()] * 2 + [shape.array()] * shape.depth
    out = pl.pallas_call(
        body,
        name="pre_near",
        out_shape=[jax.ShapeDtypeStruct(size, kind) for size, kind in shapes],
        in_specs=[pl.BlockSpec(memory_space=pltpu.HBM)] * 3,
        out_specs=[pl.BlockSpec(memory_space=pltpu.VMEM)] * len(shapes),
        scratch_shapes=[pltpu.VMEM(angles.shape, F32), pltpu.SemaphoreType.DMA((2 * COPIES + 1,))],
        compiler_params=pltpu.CompilerParams(vmem_limit_bytes=VMEM_FIRST),
    )(angles, psi, lam)
    return out[0], out[1], out[2:]


def pre_far(shape, angles, raw):
    def body(angle, ref, *outs):
        first_rotations(shape, angle, ref, outs)

    return vmem_call("pre_far", body, [shape.array()] * shape.depth, inputs=(angles, raw))


def rotate_local(shape, angles, arrays, form, new_form, mats, which, hold=()):
    count = len(arrays)

    def body(*refs):
        matrices = [m[...] for m in refs[1 + count : 5 + count]]
        sine, cosine = half_angle(refs[0][0:1, which : which + 1])
        planes = load_planes(shape, form, refs[1 : 1 + count])
        store_planes(shape, new_form, refs[5 + count :], rotate_all(planes, *matrices, cosine, sine))

    return vmem_call(
        "rotate_local",
        body,
        [shape.array()] * shape.depth,
        inputs=(angles,) + tuple(arrays) + tuple(mats),
        hold=hold,
    )


def halves(shape, ref):
    size = 2 * shape.rows
    return [ref.at[pl.ds(i * size, size), :] for i in range(2)]


def turn(shape, angles, near, far, field_b):
    size = shape.depth

    def body(*refs):
        states = refs[1 : 1 + size], refs[1 + size : 1 + 2 * size]
        cos_b, sin_b = refs[1 + 2 * size : 3 + 2 * size]
        before = halves(shape, refs[3 + 2 * size])
        outs = refs[4 + 2 * size : 4 + 3 * size], refs[4 + 3 * size :]
        pair_one, pair_zero = angle_pair(refs[0], 3), angle_pair(refs[0], 1)
        bits = list(range(size.bit_length()))
        for start in range(0, shape.part, TILE):
            for u in range(size):
                slots = [(u, v) for v in range(size)]
                real, imag = load_slots(shape, "v", states[0], start, slots)
                far_real, far_imag = load_slots(shape, "v", states[1], start, slots)
                real, imag = butterflies(real + far_real, imag + far_imag, pair_one, bits)
                store_slots(shape, "all", before[:1], start, slots, real[:size], imag[:size])
                store_slots(shape, "all", before[1:], start, slots, real[size:], imag[size:])
                for i in range(2 * size):
                    row = (i // size) * shape.rows + (u * size + i % size) * shape.part + start
                    real[i], imag[i] = phased(
                        real[i], imag[i], cos_b[row : row + TILE, :], sin_b[row : row + TILE, :]
                    )
                real, imag = butterflies(real, imag, pair_zero, bits)
                store_slots(shape, "v", outs[0], start, slots, real[:size], imag[:size])
                store_slots(shape, "v", outs[1], start, slots, real[size:], imag[size:])

    result = vmem_call(
        "turn",
        body,
        [((4 * shape.rows, LANES), F32)] + [shape.array()] * (2 * size),
        inputs=(angles,) + tuple(near) + tuple(far) + (field_b[1], field_b[2]),
    )
    return result[0], result[1 : 1 + size], result[1 + size :]


def flip_raw(shape, own, other, hold=()):
    pieces = shape.rows // shape.part

    def body(own_ref, other_ref, out):
        total = jnp.zeros((TILE, LANES), F32)
        for start in range(0, shape.part, TILE):
            parts = [load_raw(own_ref, (i * shape.part + start) * 2) for i in range(pieces)]
            own_re, own_im = [p[0] for p in parts], [p[1] for p in parts]
            for i in range(pieces):
                other_re, other_im = load_raw(other_ref, (i * shape.part + start) * 2)
                total = total + other_re * flip_sum(own_im, i) - other_im * flip_sum(own_re, i)
        out[...] = sign(jnp.sum(total, axis=0, keepdims=True))

    return vmem_call("flip_raw", body, [((1, LANES), F32)], inputs=(own, other), hold=hold)[0]


def sign(value):
    return jnp.where(lax.axis_index("core") == 0, value, -value)


def flip_mats(low):
    small = flip_mat(LANES)
    zero = jnp.zeros_like(small)
    lane_flip = jnp.concatenate(
        [jnp.concatenate([small, zero], axis=1), jnp.concatenate([zero, small], axis=1)], axis=0
    )
    return lane_flip, flip_mat(low)


def gradients_mid(shape, field_b, own_before, other_before):
    low = shape.low

    def body(cost, cos_b, sin_b, own_ref, other_ref, out):
        lane_flip, row_flip = flip_mats(low)

        def turned(block, row):
            re, im = phased(
                block[:, :LANES], block[:, LANES:], cos_b[row : row + low, :], sin_b[row : row + low, :]
            )
            return jnp.concatenate([re, im], axis=1)

        near, far = (load_planes(shape, "all", [ref]) for ref in halves(shape, own_ref))
        other_far, other = (load_planes(shape, "other", [ref]) for ref in halves(shape, other_ref))
        inter = jnp.zeros((1, LANES), F32)
        mix_one = jnp.zeros((1, LANES), F32)
        mix_zero = jnp.zeros((1, LANES), F32)
        for u, flips in enumerate(flips_all(near, lane_flip, row_flip)):
            mix_one = mix_one + cross_imag(other[u], flips + 0.5 * far[u]) + cross_imag(other_far[u], 0.5 * near[u])
            weight = cost[u * low : (u + 1) * low, :]
            inter = inter + cross_imag(other[u], jnp.concatenate([weight] * 2, axis=1) * near[u])
        near = [turned(block, u * low) for u, block in enumerate(near)]
        for u, flips in enumerate(flips_all(near, lane_flip, row_flip)):
            across = 0.5 * turned(far[u], shape.rows + u * low)
            mix_zero = mix_zero + cross_imag(turned(other[u], u * low), flips + across)
            mix_zero = mix_zero + cross_imag(turned(other_far[u], shape.rows + u * low), 0.5 * near[u])
        out[...] = sign(jnp.concatenate([mix_zero, inter, mix_one], axis=0))

    return vmem_call(
        "gradients_mid", body, [((3, LANES), F32)], inputs=tuple(field_b) + (own_before, other_before)
    )[0]


def post_send(shape, angles, arrays, hold=()):
    count = len(arrays)

    def body(*refs):
        pair = angle_pair(refs[0], 1)
        for start in range(0, shape.part, TILE):
            for v in range(shape.depth):
                slots = [(u, v) for u in range(shape.depth)]
                real, imag = load_slots(shape, "u", refs[1 : 1 + count], start, slots)
                real, imag = butterflies(real, imag, pair, shape.bits("v"))
                store_slots(shape, "all", [refs[1 + count]], start, slots, real, imag)

    return vmem_call("post_send", body, [shape.whole()], inputs=(angles,) + tuple(arrays), hold=hold)[0]


def flips_other(shape, other):
    def body(ref, out):
        slots = shape.slots()
        for start in range(0, shape.part, TILE):
            real, imag = load_slots(shape, "other", [ref], start, slots)
            flips = [[flip_sum(values, i) for i in range(len(slots))] for values in (real, imag)]
            store_slots(shape, "all", [out], start, slots, *flips)

    return vmem_call("flips_other", body, [shape.whole()], inputs=(other,))[0]


def post_grads(shape, angles, arrays, other, flips, cost_a, hold=()):
    count = len(arrays)

    def body(*refs):
        other_ref, flips_ref, cost = refs[1 + count : 4 + count]
        mixed, out = refs[4 + count :]
        piece = shape.piece()
        pair = angle_pair(refs[0], 1)
        mix = jnp.zeros((TILE, LANES), F32)
        inter = jnp.zeros((TILE, LANES), F32)
        for start in range(0, shape.part, TILE):
            for v in range(shape.depth):
                slots = [(u, v) for u in range(shape.depth)]
                real, imag = load_slots(shape, "u", refs[1 : 1 + count], start, slots)
                real, imag = butterflies(real, imag, pair, shape.bits("v"))
                store_slots(shape, "all", [mixed], start, slots, real, imag)
                other_re, other_im = load_slots(shape, "other", [other_ref], start, slots)
                flip_re, flip_im = load_slots(shape, "all", [flips_ref], start, slots)
                for i, slot in enumerate(slots):
                    mix = mix + flip_re[i] * imag[i] - flip_im[i] * real[i]
                    row = pl.multiple_of(piece(*slot) * shape.part + start, TILE)
                    value = cost[pl.ds(row, TILE), :]
                    inter = inter + value * (other_re[i] * imag[i] - other_im[i] * real[i])
        out[0:1, :] = sign(jnp.sum(inter, axis=0, keepdims=True))
        out[1:2, :] = sign(jnp.sum(mix, axis=0, keepdims=True))

    return vmem_call(
        "post_grads",
        body,
        [shape.whole(), ((2, LANES), F32)],
        inputs=(angles,) + tuple(arrays) + (other, flips, cost_a),
        hold=hold,
    )


def post_phase(shape, mixed, other, field_a):
    def body(own_ref, other_ref, cos_a, sin_a, psi_out, lam_out):
        first = lax.axis_index("core") == 0
        piece = shape.piece()
        slots = shape.slots()
        for start in range(0, shape.part, TILE):
            own_re, own_im = load_slots(shape, "all", [own_ref], start, slots)
            other_re, other_im = load_slots(shape, "other", [other_ref], start, slots)
            for i, slot in enumerate(slots):
                row = pl.multiple_of(piece(*slot) * shape.part + start, TILE)
                cosine, sine = cos_a[pl.ds(row, TILE), :], sin_a[pl.ds(row, TILE), :]
                own_pair = phased(own_re[i], own_im[i], cosine, sine)
                other_pair = phased(other_re[i], other_im[i], cosine, sine)
                for j in range(2):
                    span = pl.ds(2 * row + j, TILE, stride=2)
                    psi_out[span, :] = jnp.where(first, own_pair[j], other_pair[j])
                    lam_out[span, :] = jnp.where(first, other_pair[j], own_pair[j])

    return vmem_call(
        "post_phase", body, [shape.whole()] * 2, inputs=(mixed, other, field_a[1], field_a[2])
    )


AXES = ("grp", "z", "core")


def swap_cores(array):
    return lax.ppermute(array, "core", [(0, 1), (1, 0)])


def swap(shape, arrays, form):
    size = shape.depth
    out = list(arrays)
    with jax.named_scope("exchange_" + form):
        for i in sorted(range(1, size), key=lambda i: (i.bit_count() == 1, -i)):
            pairs = []
            for chip in range(size * size):
                for core in range(CORES):
                    step = i if (core == 0) == (form == "u") else i * size
                    pairs.append((chip * CORES + core, (chip ^ step) * CORES + core))
            out[i] = lax.ppermute(arrays[i], AXES, pairs)
    return out


def total_grads(shape, parts):
    def join(early, mid_part, late, out):
        rows = [late[0:1, :], late[1:2, :] + mid_part[0:1, :], mid_part[1:2, :], mid_part[2:3, :] + early[...]]
        out[...] = jnp.concatenate(rows + [jnp.zeros((TILE - 4, LANES), F32)], axis=0)

    def add(*refs):
        values = [ref[...] for ref in refs[:-1]]
        while len(values) > 1:
            values = [left + right for left, right in zip(values[::2], values[1::2])]
        refs[-1][...] = values[0]

    block_shape = [((TILE, LANES), F32)]
    block = vmem_call("join_grads", join, block_shape, inputs=tuple(parts))[0]
    for axis, size in (("core", CORES), ("grp", shape.groups), ("z", shape.depth)):
        stride = 1
        while stride < size:
            reach = min(4, size // stride)
            others = [
                lax.ppermute(block, axis, [(j, j ^ (stride * i)) for j in range(size)]) for i in range(1, reach)
            ]
            block = vmem_call("add_grads", add, block_shape, inputs=(block, *others))[0]
            stride *= reach
    scale = 2.0 / (shape.rows * LANES * shape.devices)

    def finish(ref, out):
        summed = jnp.sum(ref[...], axis=1, keepdims=True) * scale
        for i in range(2 * LAYERS):
            out[i] = jnp.sum(summed[i : i + 1, :])

    return vmem_call("finish_grads", finish, [((2 * LAYERS,), F32)], inputs=(block,), smem_out=True)[0]


def after(values, first):
    return lax.optimization_barrier((values, first))[0]


def piece_mix(shape, angles, which, state):
    low = shape.low
    least = shape.part.bit_length() - 1

    def body(angle, ref, mixed, flipped):
        sine, cosine = half_angle(angle[0:1, which : which + 1])
        real, imag = mixer_mats(low, cosine, sine, least)
        row_high, row_low = split(jnp.concatenate([real, imag], axis=0))
        row_flip = flip_mat(low, least)
        blocks = [ref[i * low : (i + 1) * low, :] for i in range(shape.planes)]
        for i, (re, im) in enumerate(rotate_all(blocks, None, None, row_high, row_low, cosine, sine)):
            mixed[i * low : (i + 1) * low, :LANES] = re
            mixed[i * low : (i + 1) * low, LANES:] = im
        for i, block in enumerate(flips_all(blocks, None, row_flip)):
            flipped[i * low : (i + 1) * low, :] = block

    return vmem_call(
        "piece_mix",
        body, [((shape.rows, 2 * LANES), F32)] * 2, inputs=(angles, state,)
    )


def plain_cross(lam, other):
    def body(lam_ref, other_ref, out):
        out[...] = cross_imag(lam_ref[...], other_ref[...])

    return vmem_call("plain_cross", body, [((1, LANES), F32)], inputs=(lam, other))[0]


def plain_gradients(shape, field_b, psi_before, lam_before):
    low = shape.low

    def body(cost, cos_b, sin_b, psi_ref, lam_ref, out):
        lane_flip, row_flip = flip_mats(low)
        spans = [slice(i * low, (i + 1) * low) for i in range(shape.planes)]
        psi = [psi_ref[span, :] for span in spans]
        lam = [lam_ref[span, :] for span in spans]
        inter = jnp.zeros((1, LANES), F32)
        mix_one = jnp.zeros((1, LANES), F32)
        mix_zero = jnp.zeros((1, LANES), F32)
        for i, flips in enumerate(flips_all(psi, lane_flip, row_flip)):
            mix_one = mix_one + cross_imag(lam[i], flips)
            inter = inter + cross_imag(lam[i], jnp.concatenate([cost[spans[i], :]] * 2, axis=1) * psi[i])

        def turned(block, span):
            re, im = phased(block[:, :LANES], block[:, LANES:], cos_b[span, :], sin_b[span, :])
            return jnp.concatenate([re, im], axis=1)

        psi = [turned(block, span) for block, span in zip(psi, spans)]
        for i, flips in enumerate(flips_all(psi, lane_flip, row_flip)):
            mix_zero = mix_zero + cross_imag(turned(lam[i], spans[i]), flips)
        out[...] = jnp.concatenate([mix_zero, inter, mix_one], axis=0)

    return vmem_call("plain_gradients", body, [((3, LANES), F32)], inputs=tuple(field_b) + (psi_before, lam_before))[0]


def plain_phase(shape, state, field, gradient):
    def body(ref, cost, cosine, sine, out):
        real, imag = ref[:, :LANES], ref[:, LANES:]
        if gradient:
            re, im = cost[...] * real, cost[...] * imag
        else:
            re, im = phased(real, imag, cosine[...], sine[...])
        out[:, :LANES] = re
        out[:, LANES:] = im

    return vmem_call("plain_phase", body, [((shape.rows, 2 * LANES), F32)], inputs=(state,) + tuple(field))[0]


def mid_math(shape, angles, planes, mats, cos_b, sin_b):
    low = shape.low
    sine, cosine = half_angle(angles[0:1, 3:4])
    first = rotate_all(planes, *[m[...] for m in mats[4:8]], cosine, sine)
    turned = []
    for i, (re, im) in enumerate(first):
        re, im = phased(re, im, cos_b[i * low : (i + 1) * low, :], sin_b[i * low : (i + 1) * low, :])
        turned.append(jnp.concatenate([re, im], axis=1))
    sine, cosine = half_angle(angles[0:1, 1:2])
    second = rotate_all(turned, *[m[...] for m in mats[0:4]], cosine, sine)
    return first, second


def plain_mid(shape, angles, state, field_b, mats):
    low = shape.low

    def body(angle, ref, cos_b, sin_b, *rest):
        blocks = [ref[i * low : (i + 1) * low, :] for i in range(shape.planes)]
        for out, pairs in zip(rest[8:], mid_math(shape, angle, blocks, rest[:8], cos_b, sin_b)):
            for i, (re, im) in enumerate(pairs):
                out[i * low : (i + 1) * low, :LANES] = re
                out[i * low : (i + 1) * low, LANES:] = im

    return vmem_call(
        "plain_mid",
        body,
        [((shape.rows, 2 * LANES), F32)] * 2,
        inputs=(angles, state, field_b[1], field_b[2]) + tuple(mats[0]) + tuple(mats[1]),
    )


def exchange_all(shape, state):
    block = state.reshape(shape.devices, -1, 2 * LANES)
    return lax.all_to_all(block, AXES, 0, 0, tiled=True).reshape(state.shape)


def plain(shape, forward, adjoint, edges, weights, layout, slab_bits, angles):
    rows = shape.rows

    def wide(array):
        return array.reshape(2, rows, LANES).transpose(1, 0, 2).reshape(rows, 2 * LANES)

    def narrow(array):
        return array.reshape(rows, 2, LANES).transpose(1, 0, 2).reshape(2, rows * LANES)

    def before(row):
        return shape.own() * rows + row

    def beyond(row):
        return (row // shape.part) * rows + shape.own() * shape.part + row % shape.part

    angles = angles.reshape(1, -1)
    small = small_inputs(edges, weights, layout, slab_bits)
    fields = make_fields(angles, *small, (rows, rows), before, beyond, shape.known)
    field_a, field_b = fields[:3], fields[3:]
    mats = make_mats(angles, shape.low)
    psi, flips = piece_mix(shape, angles, 3, wide(forward))
    lam, _ = piece_mix(shape, angles, 3, wide(adjoint))
    early = plain_cross(wide(adjoint), flips)
    psi_before, psi_after = plain_mid(shape, angles, exchange_all(shape, psi), field_b, mats)
    lam_before, lam_after = plain_mid(shape, angles, exchange_all(shape, lam), field_b, mats)
    mid_part = plain_gradients(shape, field_b, psi_before, lam_before)
    psi, lam = exchange_all(shape, psi_after), exchange_all(shape, lam_after)
    psi_mixed, flips = piece_mix(shape, angles, 1, psi)
    lam_mixed, _ = piece_mix(shape, angles, 1, lam)
    late = jnp.concatenate(
        [plain_cross(lam_mixed, plain_phase(shape, psi_mixed, field_a, True)), plain_cross(lam, flips)], axis=0
    )
    grads = total_grads(shape, (early, mid_part, late))
    outs = [narrow(plain_phase(shape, state, field_a, False)) for state in (psi_mixed, lam_mixed)]
    return outs[0], outs[1], grads


def interleave(array, rows):
    return array.reshape(2, rows, LANES).transpose(1, 0, 2).reshape(2 * rows, LANES)


def deinterleave(array, rows):
    return array.reshape(rows, 2, LANES).transpose(1, 0, 2).reshape(2, rows * LANES)


def places(shape):
    def before(row):
        return shape.own() * shape.rows + row

    def beyond(row):
        far, slot, inner = row // shape.rows, (row % shape.rows) // shape.part, row % shape.part
        source = shape.piece()(slot // shape.depth, slot % shape.depth) * CORES
        source = source + jnp.bitwise_xor(lax.axis_index("core"), far)
        return source * shape.rows + shape.chip() * shape.part + inner

    return before, beyond


def pipelined(shape, forward, adjoint, edges, weights, layout, slab_bits, angles):
    rows = shape.rows
    angles = angles.reshape(1, -1)
    own_raw, other_raw, near = pre_near(shape, angles, interleave(forward, rows), interleave(adjoint, rows))
    far_raw = swap_cores(other_raw)
    mats = make_mats(angles, shape.low, hold=near[:1])
    before, beyond = places(shape)
    small = small_inputs(edges, weights, layout, slab_bits)
    sizes = (rows, 2 * rows), before, beyond, shape.known
    fields = make_fields(angles, *small, *sizes, core=1, hold=near[:1])
    near = swap(shape, near, "u")
    far = swap(shape, pre_far(shape, angles, far_raw), "u")
    near = swap(shape, rotate_local(shape, angles, near, "u", "v", mats[1], 3, hold=fields[:1]), "v")
    far = rotate_local(shape, angles, far, "u", "v", mats[1], 3)
    fields = make_fields(angles, *small, *sizes, core=0, hold=after(fields, far[0]))
    field_a, field_b = fields[:3], fields[3:]
    early = flip_raw(shape, own_raw, other_raw, hold=far[:1])
    far = swap(shape, far, "v")
    own_before, near, far = turn(shape, angles, near, far, field_b)
    far = swap(shape, far, "v")
    near = swap(shape, near, "v")
    other_before = swap_cores(own_before)
    far = swap(shape, rotate_local(shape, angles, far, "v", "u", mats[0], 1), "u")
    near = rotate_local(shape, angles, near, "v", "u", mats[0], 1)
    other = swap_cores(post_send(shape, angles, far, hold=near[:1]))
    near = swap(shape, near, "u")
    mid_part = gradients_mid(shape, field_b, own_before, other_before)
    flips = flips_other(shape, other)
    mixed, late = post_grads(shape, angles, near, other, flips, field_a[0], hold=(mid_part, early))
    grads = total_grads(shape, (early, mid_part, late))
    psi_out, lam_out = post_phase(shape, mixed, other, field_a)
    return deinterleave(psi_out, rows), deinterleave(lam_out, rows), grads


def solution(mesh):
    groups, rest = mesh.shape["grp"], mesh.shape["rep"]
    depth = rest // CORES
    fine = Mesh(mesh.devices.reshape(groups, depth, CORES), AXES)

    def per_device(forward, *others):
        shape = Shape(groups, depth, forward.shape[1])
        return (pipelined if shape.tiles else plain)(shape, forward, *others)

    state = P(None, AXES)
    return jax.shard_map(
        per_device,
        mesh=fine,
        in_specs=(state, state, P(), P(), P(), P(), P()),
        out_specs=(state, state, P()),
        check_vma=False,
    )
```

time: 116 us -> 81.1 us (0.70)
  local copies, waits for them, and re-layouts: 16.9 us -> 2.24 us
  waiting for transfers between devices: 33.4 us -> 19.4 us
  Pallas kernels: 23.1 us -> 16.8 us
    ppermute x12 -> x34, starting transfers between devices: 18.6 us -> 41.5 us  [the longest x24 32.7 us: swap(): out[i] = lax.ppermute(arrays[i], AXES, pairs)]
    all_to_all x5 -> x0, starting transfers between devices: 22.5 us -> none  [the longest x4 18.1 us: send_wide(): lax.all_to_all(block, ('grp', 'core'), 0, 0, tiled=True)]
    unnamed x72 -> x18, local copies, waits for them, and re-layouts: 15.5 us -> 2.24 us
    all_to_all x5 -> x0, waiting for transfers between devices: 7.59 us -> none  [the longest x1 6.4 us: total_grads(): lax.all_to_all(block.reshape(count, TILE, LANES), ('grp', 'z', 'core'), 0...]
    ppermute x12 -> x34, waiting for transfers between devices: 25.8 us -> 19.4 us  [the longest x24 14.1 us: swap(): out[i] = lax.ppermute(arrays[i], AXES, pairs)]
    pallas_call x17 -> x21, Pallas kernels: 23.1 us -> 16.8 us  [the longest x18 10.5 us: vmem_call(): pl.pallas_call(body, name=name, out_shape=[jax.ShapeDtypeStruct(shape, ki...]
    optimization_barrier x2 -> x0, local copies, waits for them, and re-layouts: 1.4 us -> none  [after(): return lax.optimization_barrier((values, first))[0]]
  transfers between devices with their start and end apart: 17 -> 34, of which waited for: 8 -> 13; matrix products, arithmetic and copies ran while one was open for 1% -> 0% of each run, Pallas kernels for 17% -> 15%
where the time goes in v1:
time: 81.1 us; the launch traced here: 81 us
  starting transfers between devices  41.5 us (51%)
  waiting for transfers between devices  19.4 us (24%)
  Pallas kernels  16.8 us (21%)
  local copies, waits for them, and re-layouts  2.24 us (3%)
  between operations  1.03 us (1%)
    ppermute x24, starting transfers between devices, swap(): out[i] = lax.ppermute(arrays[i], AXES, pairs)  32.7 us
    ppermute x24, waiting for transfers between devices, swap(): out[i] = lax.ppermute(arrays[i], AXES, pairs)  14.1 us
    pallas_call x18, Pallas kernels, vmem_call(): pl.pallas_call(body, name=name, out_shape=[jax.ShapeDtypeStruct(shape, ki...  10.5 us
    ppermute x7, starting transfers between devices, total_grads(): lax.ppermute(block, axis, [(j, j ^ stride * i) for j in range(size)])  7.95 us
    ppermute x7, waiting for transfers between devices, total_grads(): lax.ppermute(block, axis, [(j, j ^ stride * i) for j in range(size)])  5.29 us
    pallas_call x2, Pallas kernels, make_fields(): pl.pallas_call(body, name='make_fields', out_shape=[jax.ShapeDtypeStruct(...  3.76 us
    pallas_call x1, Pallas kernels, pre_near(): pl.pallas_call(body, name='pre_near', out_shape=[jax.ShapeDtypeStruct(siz...  2.52 us
    unnamed x18, local copies, waits for them, and re-layouts  2.24 us
  transfers between devices with their start and end apart: 34, of which 13 were waited for; matrix products, arithmetic and copies ran while one was open for 0% of the time, Pallas kernels for 15%

profile of v1, /device:TPU:0, one launch (start us, length us, event | category | flops | bytes accessed | tf_op | source)
XLA Modules:
  0.0 81.0 jit_solution(615912216276559815)
XLA Ops:
  0.6 2.5 %pre_near.1 = (f32[1024,128]{1,0:T(8,128)}, f32[1024,128]{1,0:T(8,128)}, f32[256,128]{1,0:T(8,128)}, f32[256,128]{1,0:T(8,128)}, f32[256,128]{1,0:T(8,128)}, /*index=5*/f32[256,128]{1,0:T(8,128)}) custom-call(f32[1,4]{1,0:T(1,128)} %bitcast.25, f32[1024,128]{1,0:T(8,128)} %bitcast.45, f32[1024,128]{1,0:T(8,128)} %bitcast.46), custom_call_target="tpu_custom_call" | custom-call | tf_op jit(solution)/shard_map/pre_near/pallas_call | solution.py:412
  3.2 0.5 collective-permute-start.6
  3.7 2.6 %collective-permute-start = (f32[256,128]{1,0:T(8,128)}, f32[256,128]{1,0:T(8,128)S(1)}, u32[]{:S(2)}, u32[]{:S(2)}) collective-permute-start(f32[256,128]{1,0:T(8,128)} %get-tuple-element.69), channel_id=1, source_target_pairs={{0,2},{1,9},{2,0},{3,11},{4,6},{5,13},{6,4},{7,15},{8,10},{9,1},{1... | collective-permute-start | bytes 393224 | tf_op jit(solution)/shard_map/exchange_u/ppermute | solution.py:653
  6.3 2.6 %collective-permute-start.1 = (f32[256,128]{1,0:T(8,128)}, f32[256,128]{1,0:T(8,128)S(1)}, u32[]{:S(2)}, u32[]{:S(2)}) collective-permute-start(f32[256,128]{1,0:T(8,128)} %get-tuple-element.70), channel_id=1, source_target_pairs={{0,4},{1,17},{2,6},{3,19},{4,0},{5,21},{6,2},{7,23},{8,12},{9,25},... | collective-permute-start | bytes 393224 | tf_op jit(solution)/shard_map/exchange_u/ppermute | solution.py:653
  8.9 0.7 copy-done.4
  9.6 0.9 %copy-done = f32[256,128]{1,0:T(8,128)S(1)} copy-done((f32[256,128]{1,0:T(8,128)S(1)}, f32[256,128]{1,0:T(8,128)}, u32[]{:S(2)}) %copy-start) | copy-done | bytes 131096
  10.5 0.4 make_mats.1
  10.9 0.2 copy-done.7
  11.2 0.4 copy-done.5
  11.6 0.2 pre_far.1
  11.8 0.5 collective-permute-start.7
  12.3 3.3 %collective-permute-start.8 = (f32[256,128]{1,0:T(8,128)S(1)}, f32[256,128]{1,0:T(8,128)S(1)}, u32[]{:S(2)}, u32[]{:S(2)}) collective-permute-start(f32[256,128]{1,0:T(8,128)S(1)} %get-tuple-element.84), channel_id=1, source_target_pairs={{0,4},{1,17},{2,6},{3,19},{4,0},{5,21},{6,2},{7,23},{8,12},{9,25},... | collective-permute-start | bytes 393224 | tf_op jit(solution)/shard_map/exchange_u/ppermute | solution.py:653
  15.6 0.7 collective-permute-start.9
  16.3 1.4 %rotate_local.4 = (f32[256,128]{1,0:T(8,128)S(1)}, f32[256,128]{1,0:T(8,128)S(1)}, f32[256,128]{1,0:T(8,128)S(1)}, f32[256,128]{1,0:T(8,128)S(1)}) custom-call(f32[1,4]{1,0:T(1,128)S(1)} %bitcast.29, f32[256,128]{1,0:T(8,128)S(1)} %copy-done.1, f32[256,128]{1,0:T(8,128)S(1)} %collective-permute-done.refs_2_, f32[256,128]{1,0:T(8,128)S(1)} %collective-permute-done.1.refs_3_, ...), custom_call_target="tpu_custom_call" | custom-call | tf_op jit(solution)/shard_map/rotate_local/pallas_call | solution.py:30
  17.6 1.6 %collective-permute-start.3 = (f32[256,128]{1,0:T(8,128)S(1)}, f32[256,128]{1,0:T(8,128)S(1)}, u32[]{:S(2)}, u32[]{:S(2)}) collective-permute-start(f32[256,128]{1,0:T(8,128)S(1)} %get-tuple-element.78), channel_id=1, source_target_pairs={{0,8},{1,3},{2,10},{3,1},{4,12},{5,7},{6,14},{7,5},{8,0},{9,11},{1... | collective-permute-start | bytes 393224 | tf_op jit(solution)/shard_map/exchange_v/ppermute | solution.py:653
  19.2 1.5 %collective-permute-start.4 = (f32[256,128]{1,0:T(8,128)S(1)}, f32[256,128]{1,0:T(8,128)S(1)}, u32[]{:S(2)}, u32[]{:S(2)}) collective-permute-start(f32[256,128]{1,0:T(8,128)S(1)} %get-tuple-element.79), channel_id=1, source_target_pairs={{0,16},{1,5},{2,18},{3,7},{4,20},{5,1},{6,22},{7,3},{8,24},{9,13},... | collective-permute-start | bytes 393224 | tf_op jit(solution)/shard_map/exchange_v/ppermute | solution.py:653
  20.7 0.5 collective-permute-start.5
  21.2 1.3 %collective-permute-done.9.refs_4_ = f32[256,128]{1,0:T(8,128)S(1)} collective-permute-done((f32[256,128]{1,0:T(8,128)S(1)}, f32[256,128]{1,0:T(8,128)S(1)}, u32[]{:S(2)}, u32[]{:S(2)}) %collective-permute-start.9) | collective-permute-done | bytes 131104 | tf_op jit(solution)/shard_map/exchange_u/ppermute | solution.py:653
  22.5 1.4 %rotate_local.5 = (f32[256,128]{1,0:T(8,128)S(1)}, f32[256,128]{1,0:T(8,128)S(1)}, f32[256,128]{1,0:T(8,128)S(1)}, f32[256,128]{1,0:T(8,128)S(1)}) custom-call(f32[1,4]{1,0:T(1,128)S(1)} %bitcast.30, f32[256,128]{1,0:T(8,128)S(1)} %get-tuple-element.82.refs_1_, f32[256,128]{1,0:T(8,128)S(1)} %collective-permute-done.7.refs_2_, ...), custom_call_target="tpu_custom_call" | custom-call | tf_op jit(solution)/shard_map/rotate_local/pallas_call | solution.py:30
  23.9 1.6 %collective-permute-start.10 = (f32[256,128]{1,0:T(8,128)S(1)}, f32[256,128]{1,0:T(8,128)S(1)}, u32[]{:S(2)}, u32[]{:S(2)}) collective-permute-start(f32[256,128]{1,0:T(8,128)S(1)} %get-tuple-element.87), channel_id=1, source_target_pairs={{0,8},{1,3},{2,10},{3,1},{4,12},{5,7},{6,14},{7,5},{8,0},{9,11},{1... | collective-permute-start | bytes 393224 | tf_op jit(solution)/shard_map/exchange_v/ppermute | solution.py:653
  25.5 1.5 %collective-permute-start.11 = (f32[256,128]{1,0:T(8,128)S(1)}, f32[256,128]{1,0:T(8,128)S(1)}, u32[]{:S(2)}, u32[]{:S(2)}) collective-permute-start(f32[256,128]{1,0:T(8,128)S(1)} %get-tuple-element.88), channel_id=1, source_target_pairs={{0,16},{1,5},{2,18},{3,7},{4,20},{5,1},{6,22},{7,3},{8,24},{9,13},... | collective-permute-start | bytes 393224 | tf_op jit(solution)/shard_map/exchange_v/ppermute | solution.py:653
  27.0 0.5 collective-permute-start.12
  27.5 3.8 %make_fields.3 = (f32[512,128]{1,0:T(8,128)S(1)}, f32[512,128]{1,0:T(8,128)S(1)}, f32[512,128]{1,0:T(8,128)S(1)}, f32[1024,128]{1,0:T(8,128)S(1)}, f32[1024,128]{1,0:T(8,128)S(1)}, /*index=5*/f32[1024,128]{1,0:T(8,128)S(1)}) custom-call(f32[1,4]{1,0:T(1,128)S(1)} %bitcast.31, ...), custom_call_target="tpu_custom_call", output_to_operand_aliasing={{0}: (5, {}), {1}: (6, {}), {2}: (7, {}), {3}: (8, {}), {4}... | custom-call | tf_op jit(solution)/shard_map/make_fields/pallas_call | solution.py:204
  31.3 1.6 %collective-permute-done.12.refs_8_ = f32[256,128]{1,0:T(8,128)S(1)} collective-permute-done((f32[256,128]{1,0:T(8,128)S(1)}, f32[256,128]{1,0:T(8,128)S(1)}, u32[]{:S(2)}, u32[]{:S(2)}) %collective-permute-start.12) | collective-permute-done | bytes 131104 | tf_op jit(solution)/shard_map/exchange_v/ppermute | solution.py:653
  32.9 0.8 turn.1
  33.6 0.2 collective-permute-start.26
  33.8 0.9 %collective-permute-start.19 = (f32[256,128]{1,0:T(8,128)S(1)}, f32[256,128]{1,0:T(8,128)S(1)}, u32[]{:S(2)}, u32[]{:S(2)}) collective-permute-start(f32[256,128]{1,0:T(8,128)S(1)} %get-tuple-element.116), channel_id=1, source_target_pairs={{0,8},{1,3},{2,10},{3,1},{4,12},{5,7},{6,14},{7,5},{8,0},{9,11},{1... | collective-permute-start | bytes 393224 | tf_op jit(solution)/shard_map/exchange_v/ppermute | solution.py:653
  34.8 1.5 %collective-permute-start.20 = (f32[256,128]{1,0:T(8,128)S(1)}, f32[256,128]{1,0:T(8,128)S(1)}, u32[]{:S(2)}, u32[]{:S(2)}) collective-permute-start(f32[256,128]{1,0:T(8,128)S(1)} %get-tuple-element.117), channel_id=1, source_target_pairs={{0,16},{1,5},{2,18},{3,7},{4,20},{5,1},{6,22},{7,3},{8,24},{9,13},... | collective-permute-start | bytes 393224 | tf_op jit(solution)/shard_map/exchange_v/ppermute | solution.py:653
  36.3 1.0 %collective-permute-start.21 = (f32[256,128]{1,0:T(8,128)S(1)}, f32[256,128]{1,0:T(8,128)S(1)}, u32[]{:S(2)}, u32[]{:S(2)}) collective-permute-start(f32[256,128]{1,0:T(8,128)S(1)} %get-tuple-element.118), channel_id=1, source_target_pairs={{0,24},{1,7},{2,26},{3,5},{4,28},{5,3},{6,30},{7,1},{8,16},{9,15},... | collective-permute-start | bytes 393224 | tf_op jit(solution)/shard_map/exchange_v/ppermute | solution.py:653
  37.3 0.9 %collective-permute-start.13 = (f32[256,128]{1,0:T(8,128)S(1)}, f32[256,128]{1,0:T(8,128)S(1)}, u32[]{:S(2)}, u32[]{:S(2)}) collective-permute-start(f32[256,128]{1,0:T(8,128)S(1)} %get-tuple-element.104), channel_id=1, source_target_pairs={{0,8},{1,3},{2,10},{3,1},{4,12},{5,7},{6,14},{7,5},{8,0},{9,11},{1... | collective-permute-start | bytes 393224 | tf_op jit(solution)/shard_map/exchange_v/ppermute | solution.py:653
  38.3 0.5 collective-permute-done.19.refs_2_
  38.8 1.0 %collective-permute-start.14 = (f32[256,128]{1,0:T(8,128)S(1)}, f32[256,128]{1,0:T(8,128)S(1)}, u32[]{:S(2)}, u32[]{:S(2)}) collective-permute-start(f32[256,128]{1,0:T(8,128)S(1)} %get-tuple-element.105), channel_id=1, source_target_pairs={{0,16},{1,5},{2,18},{3,7},{4,20},{5,1},{6,22},{7,3},{8,24},{9,13},... | collective-permute-start | bytes 393224 | tf_op jit(solution)/shard_map/exchange_v/ppermute | solution.py:653
  39.8 1.4 %collective-permute-start.15 = (f32[256,128]{1,0:T(8,128)S(1)}, f32[256,128]{1,0:T(8,128)S(1)}, u32[]{:S(2)}, u32[]{:S(2)}) collective-permute-start(f32[256,128]{1,0:T(8,128)S(1)} %get-tuple-element.106), channel_id=1, source_target_pairs={{0,24},{1,7},{2,26},{3,5},{4,28},{5,3},{6,30},{7,1},{8,16},{9,15},... | collective-permute-start | bytes 393224 | tf_op jit(solution)/shard_map/exchange_v/ppermute | solution.py:653
  41.2 0.9 %collective-permute-done.21.refs_4_ = f32[256,128]{1,0:T(8,128)S(1)} collective-permute-done((f32[256,128]{1,0:T(8,128)S(1)}, f32[256,128]{1,0:T(8,128)S(1)}, u32[]{:S(2)}, u32[]{:S(2)}) %collective-permute-start.21) | collective-permute-done | bytes 131104 | tf_op jit(solution)/shard_map/exchange_v/ppermute | solution.py:653
  42.2 1.3 %rotate_local.7 = (f32[256,128]{1,0:T(8,128)S(1)}, f32[256,128]{1,0:T(8,128)S(1)}, f32[256,128]{1,0:T(8,128)S(1)}, f32[256,128]{1,0:T(8,128)S(1)}) custom-call(f32[1,4]{1,0:T(1,128)S(1)} %bitcast.33, f32[256,128]{1,0:T(8,128)S(1)} %get-tuple-element.115.refs_1_, f32[256,128]{1,0:T(8,128)S(1)} %collective-permute-done.19.refs_2_, ...), custom_call_target="tpu_custom_call" | custom-call | tf_op jit(solution)/shard_map/rotate_local/pallas_call | solution.py:30
  43.5 2.0 %collective-permute-start.22 = (f32[256,128]{1,0:T(8,128)S(1)}, f32[256,128]{1,0:T(8,128)S(1)}, u32[]{:S(2)}, u32[]{:S(2)}) collective-permute-start(f32[256,128]{1,0:T(8,128)S(1)} %get-tuple-element.120), channel_id=1, source_target_pairs={{0,2},{1,9},{2,0},{3,11},{4,6},{5,13},{6,4},{7,15},{8,10},{9,1},{1... | collective-permute-start | bytes 393224 | tf_op jit(solution)/shard_map/exchange_u/ppermute | solution.py:653
  45.5 1.1 %collective-permute-start.23 = (f32[256,128]{1,0:T(8,128)S(1)}, f32[256,128]{1,0:T(8,128)S(1)}, u32[]{:S(2)}, u32[]{:S(2)}) collective-permute-start(f32[256,128]{1,0:T(8,128)S(1)} %get-tuple-element.121), channel_id=1, source_target_pairs={{0,4},{1,17},{2,6},{3,19},{4,0},{5,21},{6,2},{7,23},{8,12},{9,25},... | collective-permute-start | bytes 393224 | tf_op jit(solution)/shard_map/exchange_u/ppermute | solution.py:653
  46.7 1.4 %collective-permute-start.24 = (f32[256,128]{1,0:T(8,128)S(1)}, f32[256,128]{1,0:T(8,128)S(1)}, u32[]{:S(2)}, u32[]{:S(2)}) collective-permute-start(f32[256,128]{1,0:T(8,128)S(1)} %get-tuple-element.122), channel_id=1, source_target_pairs={{0,6},{1,25},{2,4},{3,27},{4,2},{5,29},{6,0},{7,31},{8,14},{9,17},... | collective-permute-start | bytes 393224 | tf_op jit(solution)/shard_map/exchange_u/ppermute | solution.py:653
  48.1 1.4 %rotate_local.6 = (f32[256,128]{1,0:T(8,128)S(1)}, f32[256,128]{1,0:T(8,128)S(1)}, f32[256,128]{1,0:T(8,128)S(1)}, f32[256,128]{1,0:T(8,128)S(1)}) custom-call(f32[1,4]{1,0:T(1,128)S(1)} %bitcast.34, f32[256,128]{1,0:T(8,128)S(1)} %get-tuple-element.103.refs_1_, f32[256,128]{1,0:T(8,128)S(1)} %collective-permute-done.13.refs_2_, ...), custom_call_target="tpu_custom_call" | custom-call | tf_op jit(solution)/shard_map/rotate_local/pallas_call | solution.py:30
  49.5 0.8 collective-permute-done.22.refs_2_
  50.3 4.1 %collective-permute-done.23.refs_3_ = f32[256,128]{1,0:T(8,128)S(1)} collective-permute-done((f32[256,128]{1,0:T(8,128)S(1)}, f32[256,128]{1,0:T(8,128)S(1)}, u32[]{:S(2)}, u32[]{:S(2)}) %collective-permute-start.23) | collective-permute-done | bytes 131104 | tf_op jit(solution)/shard_map/exchange_u/ppermute | solution.py:653
  54.4 0.2 post_send.1
  54.7 2.0 %collective-permute-start.16 = (f32[256,128]{1,0:T(8,128)S(1)}, f32[256,128]{1,0:T(8,128)S(1)}, u32[]{:S(2)}, u32[]{:S(2)}) collective-permute-start(f32[256,128]{1,0:T(8,128)S(1)} %get-tuple-element.112), channel_id=1, source_target_pairs={{0,2},{1,9},{2,0},{3,11},{4,6},{5,13},{6,4},{7,15},{8,10},{9,1},{1... | collective-permute-start | bytes 393224 | tf_op jit(solution)/shard_map/exchange_u/ppermute | solution.py:653
  56.7 1.1 %collective-permute-start.17 = (f32[256,128]{1,0:T(8,128)S(1)}, f32[256,128]{1,0:T(8,128)S(1)}, u32[]{:S(2)}, u32[]{:S(2)}) collective-permute-start(f32[256,128]{1,0:T(8,128)S(1)} %get-tuple-element.113), channel_id=1, source_target_pairs={{0,4},{1,17},{2,6},{3,19},{4,0},{5,21},{6,2},{7,23},{8,12},{9,25},... | collective-permute-start | bytes 393224 | tf_op jit(solution)/shard_map/exchange_u/ppermute | solution.py:653
  57.8 1.4 %collective-permute-start.18 = (f32[256,128]{1,0:T(8,128)S(1)}, f32[256,128]{1,0:T(8,128)S(1)}, u32[]{:S(2)}, u32[]{:S(2)}) collective-permute-start(f32[256,128]{1,0:T(8,128)S(1)} %get-tuple-element.114), channel_id=1, source_target_pairs={{0,6},{1,25},{2,4},{3,27},{4,2},{5,29},{6,0},{7,31},{8,14},{9,17},... | collective-permute-start | bytes 393224 | tf_op jit(solution)/shard_map/exchange_u/ppermute | solution.py:653
  59.2 0.1 flip_raw.1.refs_9_.early
  59.3 0.1 flips_other.1.refs_6_
  59.4 1.2 %gradients_mid.1.refs_8_.mid_part = f32[3,128]{1,0:T(4,128)S(1)} custom-call(f32[1024,128]{1,0:T(8,128)S(1)} %get-tuple-element.124.cost, f32[1024,128]{1,0:T(8,128)S(1)} %get-tuple-element.101.refs_9_.cos_b, f32[1024,128]{1,0:T(8,128)S(1)} %get-tuple-element.102.refs_10_.sin_b, f32[2048,128]{1,0:T(8,128)S(1)} %get-tuple-element.125.own_ref, ...), custom_call_target="tpu_custom_call" | custom-call | tf_op jit(solution)/shard_map/gradients_mid/pallas_call | solution.py:30
  60.6 4.8 %collective-permute-done.17.refs_3_ = f32[256,128]{1,0:T(8,128)S(1)} collective-permute-done((f32[256,128]{1,0:T(8,128)S(1)}, f32[256,128]{1,0:T(8,128)S(1)}, u32[]{:S(2)}, u32[]{:S(2)}) %collective-permute-start.17) | collective-permute-done | bytes 131104 | tf_op jit(solution)/shard_map/exchange_u/ppermute | solution.py:653
  65.4 0.3 post_grads.1
  65.8 1.2 %collective-permute-done.27.refs_1_ = f32[8,128]{1,0:T(8,128)S(1)} collective-permute-done((f32[8,128]{1,0:T(8,128)S(1)}, f32[8,128]{1,0:T(8,128)S(1)}, u32[]{:S(2)}, u32[]{:S(2)}) %collective-permute-start.27) | collective-permute-done | bytes 4128 | tf_op jit(solution)/shard_map/ppermute | solution.py:675
  67.0 2.0 %collective-permute-start.30 = (f32[8,128]{1,0:T(8,128)S(1)}, f32[8,128]{1,0:T(8,128)S(1)}, u32[]{:S(2)}, u32[]{:S(2)}) collective-permute-start(f32[8,128]{1,0:T(8,128)S(1)} %add_grads.3.refs_0_), channel_id=1, source_target_pairs={{0,24},{8,16},{16,8},{24,0},{1,25},{9,17},{17,9},{25,1},{2,26},{10... | collective-permute-start | bytes 12296 | tf_op jit(solution)/shard_map/ppermute | solution.py:675
  69.0 0.5 collective-permute-start.29
  69.5 0.9 %collective-permute-start.28 = (f32[8,128]{1,0:T(8,128)S(1)}, f32[8,128]{1,0:T(8,128)S(1)}, u32[]{:S(2)}, u32[]{:S(2)}) collective-permute-start(f32[8,128]{1,0:T(8,128)S(1)} %add_grads.3.refs_0_), channel_id=1, source_target_pairs={{0,8},{8,0},{16,24},{24,16},{1,9},{9,1},{17,25},{25,17},{2,10},{10... | collective-permute-start | bytes 12296 | tf_op jit(solution)/shard_map/ppermute | solution.py:675
  70.4 1.0 %collective-permute-done.30.refs_3_ = f32[8,128]{1,0:T(8,128)S(1)} collective-permute-done((f32[8,128]{1,0:T(8,128)S(1)}, f32[8,128]{1,0:T(8,128)S(1)}, u32[]{:S(2)}, u32[]{:S(2)}) %collective-permute-start.30) | collective-permute-done | bytes 4128 | tf_op jit(solution)/shard_map/ppermute | solution.py:675
  71.5 1.1 %collective-permute-done.29.refs_2_ = f32[8,128]{1,0:T(8,128)S(1)} collective-permute-done((f32[8,128]{1,0:T(8,128)S(1)}, f32[8,128]{1,0:T(8,128)S(1)}, u32[]{:S(2)}, u32[]{:S(2)}) %collective-permute-start.29) | collective-permute-done | bytes 4128 | tf_op jit(solution)/shard_map/ppermute | solution.py:675
  72.6 0.5 collective-permute-done.28.refs_1_
  73.1 2.3 %collective-permute-start.33 = (f32[8,128]{1,0:T(8,128)S(1)}, f32[8,128]{1,0:T(8,128)S(1)}, u32[]{:S(2)}, u32[]{:S(2)}) collective-permute-start(f32[8,128]{1,0:T(8,128)S(1)} %add_grads.4.refs_0_), channel_id=1, source_target_pairs={{0,6},{2,4},{4,2},{6,0},{1,7},{3,5},{5,3},{7,1},{8,14},{10,12},{12... | collective-permute-start | bytes 12296 | tf_op jit(solution)/shard_map/ppermute | solution.py:675
  75.4 1.1 %collective-permute-start.32 = (f32[8,128]{1,0:T(8,128)S(1)}, f32[8,128]{1,0:T(8,128)S(1)}, u32[]{:S(2)}, u32[]{:S(2)}) collective-permute-start(f32[8,128]{1,0:T(8,128)S(1)} %add_grads.4.refs_0_), channel_id=1, source_target_pairs={{0,4},{2,6},{4,0},{6,2},{1,5},{3,7},{5,1},{7,3},{8,12},{10,14},{12... | collective-permute-start | bytes 12296 | tf_op jit(solution)/shard_map/ppermute | solution.py:675
  76.5 1.0 %collective-permute-start.31 = (f32[8,128]{1,0:T(8,128)S(1)}, f32[8,128]{1,0:T(8,128)S(1)}, u32[]{:S(2)}, u32[]{:S(2)}) collective-permute-start(f32[8,128]{1,0:T(8,128)S(1)} %add_grads.4.refs_0_), channel_id=1, source_target_pairs={{0,2},{2,0},{4,6},{6,4},{1,3},{3,1},{5,7},{7,5},{8,10},{10,8},{12,... | collective-permute-start | bytes 12296 | tf_op jit(solution)/shard_map/ppermute | solution.py:675
  77.5 1.2 %post_phase.1 = (f32[1024,128]{1,0:T(8,128)}, f32[1024,128]{1,0:T(8,128)}) custom-call(f32[1024,128]{1,0:T(8,128)S(1)} %get-tuple-element.127.own_ref, f32[1024,128]{1,0:T(8,128)S(1)} %collective-permute-done.25.ref.refs_5_.other_ref, f32[512,128]{1,0:T(8,128)S(1)} %get-tuple-element.128.cos_a, f32[512,128]{1,0:T(8,128)S(1)} %get-tuple-element.129.sin_a), custom_call_target="tpu_custom_call" | custom-call | tf_op jit(solution)/shard_map/post_phase/pallas_call | solution.py:30
  78.7 1.2 %collective-permute-done.32.refs_2_ = f32[8,128]{1,0:T(8,128)S(1)} collective-permute-done((f32[8,128]{1,0:T(8,128)S(1)}, f32[8,128]{1,0:T(8,128)S(1)}, u32[]{:S(2)}, u32[]{:S(2)}) %collective-permute-start.32) | collective-permute-done | bytes 4128 | tf_op jit(solution)/shard_map/ppermute | solution.py:675
  79.9 0.2 collective-permute-done.31.refs_1_
  80.2 0.6 finish_grads.1
  (43 shorter events, 0.3 us)
Async XLA Ops:
  3.2 8.4 %collective-permute-start.6 = (f32[1024,128]{1,0:T(8,128)}, f32[1024,128]{1,0:T(8,128)S(1)}, u32[]{:S(2)}, u32[]{:S(2)}) collective-permute-start(f32[1024,128]{1,0:T(8,128)} %get-tuple-element.81.refs_1_), channel_id=1, source_target_pairs={{0,1},{1,0},{2,3},{3,2},{4,5},{5,4},{6,7},{7,6},{8,9},{9,8},{10,11... | collective-permute-start | bytes 1572872 | tf_op jit(solution)/shard_map/ppermute | solution.py:640
  3.7 11.9 %collective-permute-start = (f32[256,128]{1,0:T(8,128)}, f32[256,128]{1,0:T(8,128)S(1)}, u32[]{:S(2)}, u32[]{:S(2)}) collective-permute-start(f32[256,128]{1,0:T(8,128)} %get-tuple-element.69), channel_id=1, source_target_pairs={{0,2},{1,9},{2,0},{3,11},{4,6},{5,13},{6,4},{7,15},{8,10},{9,1},{1... | collective-permute-start | bytes 393224 | tf_op jit(solution)/shard_map/exchange_u/ppermute | solution.py:653
  6.3 9.9 %collective-permute-start.1 = (f32[256,128]{1,0:T(8,128)}, f32[256,128]{1,0:T(8,128)S(1)}, u32[]{:S(2)}, u32[]{:S(2)}) collective-permute-start(f32[256,128]{1,0:T(8,128)} %get-tuple-element.70), channel_id=1, source_target_pairs={{0,4},{1,17},{2,6},{3,19},{4,0},{5,21},{6,2},{7,23},{8,12},{9,25},... | collective-permute-start | bytes 393224 | tf_op jit(solution)/shard_map/exchange_u/ppermute | solution.py:653
  8.9 0.7 copy-start.4
  8.9 7.4 %collective-permute-start.2 = (f32[256,128]{1,0:T(8,128)}, f32[256,128]{1,0:T(8,128)S(1)}, u32[]{:S(2)}, u32[]{:S(2)}) collective-permute-start(f32[256,128]{1,0:T(8,128)} %get-tuple-element.71), channel_id=1, source_target_pairs={{0,6},{1,25},{2,4},{3,27},{4,2},{5,29},{6,0},{7,31},{8,14},{9,17},... | collective-permute-start | bytes 393224 | tf_op jit(solution)/shard_map/exchange_u/ppermute | solution.py:653
  9.6 0.9 %copy-start = (f32[256,128]{1,0:T(8,128)S(1)}, f32[256,128]{1,0:T(8,128)}, u32[]{:S(2)}) copy-start(f32[256,128]{1,0:T(8,128)} %get-tuple-element.68.refs_1_.refs_5_) | copy-start | bytes 393220
  10.5 0.7 copy-start.7
  10.5 0.7 copy-start.8
  10.9 0.7 copy-start.5
  10.9 0.7 copy-start.6
  11.6 4.7 %copy-start.1 = (f32[256,128]{1,0:T(8,128)S(1)}, f32[256,128]{1,0:T(8,128)}, u32[]{:S(2)}) copy-start(f32[256,128]{1,0:T(8,128)} %get-tuple-element.68.refs_1_.refs_5_) | copy-start | bytes 393220
  11.8 8.9 %collective-permute-start.7 = (f32[256,128]{1,0:T(8,128)S(1)}, f32[256,128]{1,0:T(8,128)S(1)}, u32[]{:S(2)}, u32[]{:S(2)}) collective-permute-start(f32[256,128]{1,0:T(8,128)S(1)} %get-tuple-element.83), channel_id=1, source_target_pairs={{0,2},{1,9},{2,0},{3,11},{4,6},{5,13},{6,4},{7,15},{8,10},{9,1},{1... | collective-permute-start | bytes 393224 | tf_op jit(solution)/shard_map/exchange_u/ppermute | solution.py:653
  12.3 8.9 %collective-permute-start.8 = (f32[256,128]{1,0:T(8,128)S(1)}, f32[256,128]{1,0:T(8,128)S(1)}, u32[]{:S(2)}, u32[]{:S(2)}) collective-permute-start(f32[256,128]{1,0:T(8,128)S(1)} %get-tuple-element.84), channel_id=1, source_target_pairs={{0,4},{1,17},{2,6},{3,19},{4,0},{5,21},{6,2},{7,23},{8,12},{9,25},... | collective-permute-start | bytes 393224 | tf_op jit(solution)/shard_map/exchange_u/ppermute | solution.py:653
  15.6 6.9 %collective-permute-start.9 = (f32[256,128]{1,0:T(8,128)S(1)}, f32[256,128]{1,0:T(8,128)S(1)}, u32[]{:S(2)}, u32[]{:S(2)}) collective-permute-start(f32[256,128]{1,0:T(8,128)S(1)} %get-tuple-element.85), channel_id=1, source_target_pairs={{0,6},{1,25},{2,4},{3,27},{4,2},{5,29},{6,0},{7,31},{8,14},{9,17},... | collective-permute-start | bytes 393224 | tf_op jit(solution)/shard_map/exchange_u/ppermute | solution.py:653
  17.6 9.3 %collective-permute-start.3 = (f32[256,128]{1,0:T(8,128)S(1)}, f32[256,128]{1,0:T(8,128)S(1)}, u32[]{:S(2)}, u32[]{:S(2)}) collective-permute-start(f32[256,128]{1,0:T(8,128)S(1)} %get-tuple-element.78), channel_id=1, source_target_pairs={{0,8},{1,3},{2,10},{3,1},{4,12},{5,7},{6,14},{7,5},{8,0},{9,11},{1... | collective-permute-start | bytes 393224 | tf_op jit(solution)/shard_map/exchange_v/ppermute | solution.py:653
  19.2 12.0 %collective-permute-start.4 = (f32[256,128]{1,0:T(8,128)S(1)}, f32[256,128]{1,0:T(8,128)S(1)}, u32[]{:S(2)}, u32[]{:S(2)}) collective-permute-start(f32[256,128]{1,0:T(8,128)S(1)} %get-tuple-element.79), channel_id=1, source_target_pairs={{0,16},{1,5},{2,18},{3,7},{4,20},{5,1},{6,22},{7,3},{8,24},{9,13},... | collective-permute-start | bytes 393224 | tf_op jit(solution)/shard_map/exchange_v/ppermute | solution.py:653
  20.7 10.5 %collective-permute-start.5 = (f32[256,128]{1,0:T(8,128)S(1)}, f32[256,128]{1,0:T(8,128)S(1)}, u32[]{:S(2)}, u32[]{:S(2)}) collective-permute-start(f32[256,128]{1,0:T(8,128)S(1)} %get-tuple-element.80), channel_id=1, source_target_pairs={{0,24},{1,7},{2,26},{3,5},{4,28},{5,3},{6,30},{7,1},{8,16},{9,15},... | collective-permute-start | bytes 393224 | tf_op jit(solution)/shard_map/exchange_v/ppermute | solution.py:653
  23.9 7.4 %collective-permute-start.10 = (f32[256,128]{1,0:T(8,128)S(1)}, f32[256,128]{1,0:T(8,128)S(1)}, u32[]{:S(2)}, u32[]{:S(2)}) collective-permute-start(f32[256,128]{1,0:T(8,128)S(1)} %get-tuple-element.87), channel_id=1, source_target_pairs={{0,8},{1,3},{2,10},{3,1},{4,12},{5,7},{6,14},{7,5},{8,0},{9,11},{1... | collective-permute-start | bytes 393224 | tf_op jit(solution)/shard_map/exchange_v/ppermute | solution.py:653
  25.5 5.8 %collective-permute-start.11 = (f32[256,128]{1,0:T(8,128)S(1)}, f32[256,128]{1,0:T(8,128)S(1)}, u32[]{:S(2)}, u32[]{:S(2)}) collective-permute-start(f32[256,128]{1,0:T(8,128)S(1)} %get-tuple-element.88), channel_id=1, source_target_pairs={{0,16},{1,5},{2,18},{3,7},{4,20},{5,1},{6,22},{7,3},{8,24},{9,13},... | collective-permute-start | bytes 393224 | tf_op jit(solution)/shard_map/exchange_v/ppermute | solution.py:653
  27.0 5.9 %collective-permute-start.12 = (f32[256,128]{1,0:T(8,128)S(1)}, f32[256,128]{1,0:T(8,128)S(1)}, u32[]{:S(2)}, u32[]{:S(2)}) collective-permute-start(f32[256,128]{1,0:T(8,128)S(1)} %get-tuple-element.89), channel_id=1, source_target_pairs={{0,24},{1,7},{2,26},{3,5},{4,28},{5,3},{6,30},{7,1},{8,16},{9,15},... | collective-permute-start | bytes 393224 | tf_op jit(solution)/shard_map/exchange_v/ppermute | solution.py:653
  33.6 25.8 %collective-permute-start.26 = (f32[2048,128]{1,0:T(8,128)S(1)}, f32[2048,128]{1,0:T(8,128)S(1)}, u32[]{:S(2)}, u32[]{:S(2)}) collective-permute-start(f32[2048,128]{1,0:T(8,128)S(1)} %get-tuple-element.125.own_ref), channel_id=1, source_target_pairs={{0,1},{1,0},{2,3},{3,2},{4,5},{5,4},{6,7},{7,6},{8,9},{9,8},{10,11... | collective-permute-start | bytes 3145736 | tf_op jit(solution)/shard_map/ppermute | solution.py:640
  33.8 5.0 %collective-permute-start.19 = (f32[256,128]{1,0:T(8,128)S(1)}, f32[256,128]{1,0:T(8,128)S(1)}, u32[]{:S(2)}, u32[]{:S(2)}) collective-permute-start(f32[256,128]{1,0:T(8,128)S(1)} %get-tuple-element.116), channel_id=1, source_target_pairs={{0,8},{1,3},{2,10},{3,1},{4,12},{5,7},{6,14},{7,5},{8,0},{9,11},{1... | collective-permute-start | bytes 393224 | tf_op jit(solution)/shard_map/exchange_v/ppermute | solution.py:653
  34.8 5.0 %collective-permute-start.20 = (f32[256,128]{1,0:T(8,128)S(1)}, f32[256,128]{1,0:T(8,128)S(1)}, u32[]{:S(2)}, u32[]{:S(2)}) collective-permute-start(f32[256,128]{1,0:T(8,128)S(1)} %get-tuple-element.117), channel_id=1, source_target_pairs={{0,16},{1,5},{2,18},{3,7},{4,20},{5,1},{6,22},{7,3},{8,24},{9,13},... | collective-permute-start | bytes 393224 | tf_op jit(solution)/shard_map/exchange_v/ppermute | solution.py:653
  36.3 5.9 %collective-permute-start.21 = (f32[256,128]{1,0:T(8,128)S(1)}, f32[256,128]{1,0:T(8,128)S(1)}, u32[]{:S(2)}, u32[]{:S(2)}) collective-permute-start(f32[256,128]{1,0:T(8,128)S(1)} %get-tuple-element.118), channel_id=1, source_target_pairs={{0,24},{1,7},{2,26},{3,5},{4,28},{5,3},{6,30},{7,1},{8,16},{9,15},... | collective-permute-start | bytes 393224 | tf_op jit(solution)/shard_map/exchange_v/ppermute | solution.py:653
  37.3 8.2 %collective-permute-start.13 = (f32[256,128]{1,0:T(8,128)S(1)}, f32[256,128]{1,0:T(8,128)S(1)}, u32[]{:S(2)}, u32[]{:S(2)}) collective-permute-start(f32[256,128]{1,0:T(8,128)S(1)} %get-tuple-element.104), channel_id=1, source_target_pairs={{0,8},{1,3},{2,10},{3,1},{4,12},{5,7},{6,14},{7,5},{8,0},{9,11},{1... | collective-permute-start | bytes 393224 | tf_op jit(solution)/shard_map/exchange_v/ppermute | solution.py:653
  38.8 7.9 %collective-permute-start.14 = (f32[256,128]{1,0:T(8,128)S(1)}, f32[256,128]{1,0:T(8,128)S(1)}, u32[]{:S(2)}, u32[]{:S(2)}) collective-permute-start(f32[256,128]{1,0:T(8,128)S(1)} %get-tuple-element.105), channel_id=1, source_target_pairs={{0,16},{1,5},{2,18},{3,7},{4,20},{5,1},{6,22},{7,3},{8,24},{9,13},... | collective-permute-start | bytes 393224 | tf_op jit(solution)/shard_map/exchange_v/ppermute | solution.py:653
  39.8 8.3 %collective-permute-start.15 = (f32[256,128]{1,0:T(8,128)S(1)}, f32[256,128]{1,0:T(8,128)S(1)}, u32[]{:S(2)}, u32[]{:S(2)}) collective-permute-start(f32[256,128]{1,0:T(8,128)S(1)} %get-tuple-element.106), channel_id=1, source_target_pairs={{0,24},{1,7},{2,26},{3,5},{4,28},{5,3},{6,30},{7,1},{8,16},{9,15},... | collective-permute-start | bytes 393224 | tf_op jit(solution)/shard_map/exchange_v/ppermute | solution.py:653
  43.5 6.7 %collective-permute-start.22 = (f32[256,128]{1,0:T(8,128)S(1)}, f32[256,128]{1,0:T(8,128)S(1)}, u32[]{:S(2)}, u32[]{:S(2)}) collective-permute-start(f32[256,128]{1,0:T(8,128)S(1)} %get-tuple-element.120), channel_id=1, source_target_pairs={{0,2},{1,9},{2,0},{3,11},{4,6},{5,13},{6,4},{7,15},{8,10},{9,1},{1... | collective-permute-start | bytes 393224 | tf_op jit(solution)/shard_map/exchange_u/ppermute | solution.py:653
  45.5 8.8 %collective-permute-start.23 = (f32[256,128]{1,0:T(8,128)S(1)}, f32[256,128]{1,0:T(8,128)S(1)}, u32[]{:S(2)}, u32[]{:S(2)}) collective-permute-start(f32[256,128]{1,0:T(8,128)S(1)} %get-tuple-element.121), channel_id=1, source_target_pairs={{0,4},{1,17},{2,6},{3,19},{4,0},{5,21},{6,2},{7,23},{8,12},{9,25},... | collective-permute-start | bytes 393224 | tf_op jit(solution)/shard_map/exchange_u/ppermute | solution.py:653
  46.7 7.7 %collective-permute-start.24 = (f32[256,128]{1,0:T(8,128)S(1)}, f32[256,128]{1,0:T(8,128)S(1)}, u32[]{:S(2)}, u32[]{:S(2)}) collective-permute-start(f32[256,128]{1,0:T(8,128)S(1)} %get-tuple-element.122), channel_id=1, source_target_pairs={{0,6},{1,25},{2,4},{3,27},{4,2},{5,29},{6,0},{7,31},{8,14},{9,17},... | collective-permute-start | bytes 393224 | tf_op jit(solution)/shard_map/exchange_u/ppermute | solution.py:653
  54.4 4.8 %copy-start.2 = (f32[1024,128]{1,0:T(8,128)S(1)}, f32[1024,128]{1,0:T(8,128)}, u32[]{:S(2)}) copy-start(f32[1024,128]{1,0:T(8,128)} %get-tuple-element.126.refs_0_) | copy-start | bytes 1572868
  54.4 4.8 %copy-start.3 = (f32[1024,128]{1,0:T(8,128)S(1)}, f32[1024,128]{1,0:T(8,128)}, u32[]{:S(2)}) copy-start(f32[1024,128]{1,0:T(8,128)} %get-tuple-element.81.refs_1_) | copy-start | bytes 1572868
  54.6 4.7 %collective-permute-start.25 = (f32[1024,128]{1,0:T(8,128)S(1)}, f32[1024,128]{1,0:T(8,128)S(1)}, u32[]{:S(2)}, u32[]{:S(2)}) collective-permute-start(f32[1024,128]{1,0:T(8,128)S(1)} %post_send.1), channel_id=1, source_target_pairs={{0,1},{1,0},{2,3},{3,2},{4,5},{5,4},{6,7},{7,6},{8,9},{9,8},{10,11... | collective-permute-start | bytes 1572872 | tf_op jit(solution)/shard_map/ppermute | solution.py:640
  54.7 5.9 %collective-permute-start.16 = (f32[256,128]{1,0:T(8,128)S(1)}, f32[256,128]{1,0:T(8,128)S(1)}, u32[]{:S(2)}, u32[]{:S(2)}) collective-permute-start(f32[256,128]{1,0:T(8,128)S(1)} %get-tuple-element.112), channel_id=1, source_target_pairs={{0,2},{1,9},{2,0},{3,11},{4,6},{5,13},{6,4},{7,15},{8,10},{9,1},{1... | collective-permute-start | bytes 393224 | tf_op jit(solution)/shard_map/exchange_u/ppermute | solution.py:653
  56.7 8.7 %collective-permute-start.17 = (f32[256,128]{1,0:T(8,128)S(1)}, f32[256,128]{1,0:T(8,128)S(1)}, u32[]{:S(2)}, u32[]{:S(2)}) collective-permute-start(f32[256,128]{1,0:T(8,128)S(1)} %get-tuple-element.113), channel_id=1, source_target_pairs={{0,4},{1,17},{2,6},{3,19},{4,0},{5,21},{6,2},{7,23},{8,12},{9,25},... | collective-permute-start | bytes 393224 | tf_op jit(solution)/shard_map/exchange_u/ppermute | solution.py:653
  57.8 7.6 %collective-permute-start.18 = (f32[256,128]{1,0:T(8,128)S(1)}, f32[256,128]{1,0:T(8,128)S(1)}, u32[]{:S(2)}, u32[]{:S(2)}) collective-permute-start(f32[256,128]{1,0:T(8,128)S(1)} %get-tuple-element.114), channel_id=1, source_target_pairs={{0,6},{1,25},{2,4},{3,27},{4,2},{5,29},{6,0},{7,31},{8,14},{9,17},... | collective-permute-start | bytes 393224 | tf_op jit(solution)/shard_map/exchange_u/ppermute | solution.py:653
  65.7 1.2 %collective-permute-start.27 = (f32[8,128]{1,0:T(8,128)S(1)}, f32[8,128]{1,0:T(8,128)S(1)}, u32[]{:S(2)}, u32[]{:S(2)}) collective-permute-start(f32[8,128]{1,0:T(8,128)S(1)} %join_grads.1.refs_0_), channel_id=1, source_target_pairs={{0,1},{1,0},{2,3},{3,2},{4,5},{5,4},{6,7},{7,6},{8,9},{9,8},{10,11... | collective-permute-start | bytes 12296 | tf_op jit(solution)/shard_map/ppermute | solution.py:675
  67.0 4.5 %collective-permute-start.30 = (f32[8,128]{1,0:T(8,128)S(1)}, f32[8,128]{1,0:T(8,128)S(1)}, u32[]{:S(2)}, u32[]{:S(2)}) collective-permute-start(f32[8,128]{1,0:T(8,128)S(1)} %add_grads.3.refs_0_), channel_id=1, source_target_pairs={{0,24},{8,16},{16,8},{24,0},{1,25},{9,17},{17,9},{25,1},{2,26},{10... | collective-permute-start | bytes 12296 | tf_op jit(solution)/shard_map/ppermute | solution.py:675
  69.0 3.6 %collective-permute-start.29 = (f32[8,128]{1,0:T(8,128)S(1)}, f32[8,128]{1,0:T(8,128)S(1)}, u32[]{:S(2)}, u32[]{:S(2)}) collective-permute-start(f32[8,128]{1,0:T(8,128)S(1)} %add_grads.3.refs_0_), channel_id=1, source_target_pairs={{0,16},{8,24},{16,0},{24,8},{1,17},{9,25},{17,1},{25,9},{2,18},{10... | collective-permute-start | bytes 12296 | tf_op jit(solution)/shard_map/ppermute | solution.py:675
  69.5 3.6 %collective-permute-start.28 = (f32[8,128]{1,0:T(8,128)S(1)}, f32[8,128]{1,0:T(8,128)S(1)}, u32[]{:S(2)}, u32[]{:S(2)}) collective-permute-start(f32[8,128]{1,0:T(8,128)S(1)} %add_grads.3.refs_0_), channel_id=1, source_target_pairs={{0,8},{8,0},{16,24},{24,16},{1,9},{9,1},{17,25},{25,17},{2,10},{10... | collective-permute-start | bytes 12296 | tf_op jit(solution)/shard_map/ppermute | solution.py:675
  73.1 5.6 %collective-permute-start.33 = (f32[8,128]{1,0:T(8,128)S(1)}, f32[8,128]{1,0:T(8,128)S(1)}, u32[]{:S(2)}, u32[]{:S(2)}) collective-permute-start(f32[8,128]{1,0:T(8,128)S(1)} %add_grads.4.refs_0_), channel_id=1, source_target_pairs={{0,6},{2,4},{4,2},{6,0},{1,7},{3,5},{5,3},{7,1},{8,14},{10,12},{12... | collective-permute-start | bytes 12296 | tf_op jit(solution)/shard_map/ppermute | solution.py:675
  75.4 4.5 %collective-permute-start.32 = (f32[8,128]{1,0:T(8,128)S(1)}, f32[8,128]{1,0:T(8,128)S(1)}, u32[]{:S(2)}, u32[]{:S(2)}) collective-permute-start(f32[8,128]{1,0:T(8,128)S(1)} %add_grads.4.refs_0_), channel_id=1, source_target_pairs={{0,4},{2,6},{4,0},{6,2},{1,5},{3,7},{5,1},{7,3},{8,12},{10,14},{12... | collective-permute-start | bytes 12296 | tf_op jit(solution)/shard_map/ppermute | solution.py:675
  76.5 3.6 %collective-permute-start.31 = (f32[8,128]{1,0:T(8,128)S(1)}, f32[8,128]{1,0:T(8,128)S(1)}, u32[]{:S(2)}, u32[]{:S(2)}) collective-permute-start(f32[8,128]{1,0:T(8,128)S(1)} %add_grads.4.refs_0_), channel_id=1, source_target_pairs={{0,2},{2,0},{4,6},{6,4},{1,3},{3,1},{5,7},{7,5},{8,10},{10,8},{12,... | collective-permute-start | bytes 12296 | tf_op jit(solution)/shard_map/ppermute | solution.py:675

commit v2 on v1

--- a/solution.py
+++ b/solution.py
@@ -13,7 +13,8 @@
 F32 = jnp.float32
 BF16 = jnp.bfloat16
 VMEM_LIMIT = 12 << 20
-VMEM_FIRST = 62 << 20
+PIECES = 4
+VMEM_FIRST = 52 << 20
 
 
 def vmem_call(name, body, out_shapes, inputs=(), smem_out=False, hold=()):
@@ -244,6 +245,7 @@
         self.part = self.rows // (groups * depth if self.tiles else self.devices)
         self.low = depth * self.part if self.tiles else min(self.rows, 2 * LANES)
         self.planes = self.rows // self.low
+        self.batch = max(depth // PIECES, 1)
 
     def own(self):
         return self.chip() * CORES + lax.axis_index("core")
@@ -277,6 +279,8 @@
             "v": (v, u),
             "all": (0, u * self.depth + v),
             "other": (0, v * self.depth + u),
+            "part": (u // self.batch, u % self.batch * self.depth + v),
+            "other_part": (v // self.batch, v % self.batch * self.depth + u),
         }[form]
         return refs[index], inner * 2 * self.part
 
@@ -312,6 +316,14 @@
     return total
 
 
+def sent_order(arrays):
+    return tuple(arrays[2:]) + (arrays[1], arrays[0])
+
+
+def plain_order(arrays):
+    return (arrays[-1], arrays[-2]) + tuple(arrays[:-2])
+
+
 def load_slots(shape, form, refs, start, slots):
     real, imag = [], []
     for slot in slots:
@@ -434,14 +446,14 @@
     def body(*refs):
         matrices = [m[...] for m in refs[1 + count : 5 + count]]
         sine, cosine = half_angle(refs[0][0:1, which : which + 1])
-        planes = load_planes(shape, form, refs[1 : 1 + count])
+        planes = load_planes(shape, form, plain_order(refs[1 : 1 + count]))
         store_planes(shape, new_form, refs[5 + count :], rotate_all(planes, *matrices, cosine, sine))
 
     return vmem_call(
         "rotate_local",
         body,
         [shape.array()] * shape.depth,
-        inputs=(angles,) + tuple(arrays) + tuple(mats),
+        inputs=(angles,) + sent_order(arrays) + tuple(mats),
         hold=hold,
     )
 
@@ -455,7 +467,7 @@
     size = shape.depth
 
     def body(*refs):
-        states = refs[1 : 1 + size], refs[1 + size : 1 + 2 * size]
+        states = plain_order(refs[1 : 1 + size]), plain_order(refs[1 + size : 1 + 2 * size])
         cos_b, sin_b = refs[1 + 2 * size : 3 + 2 * size]
         before = halves(shape, refs[3 + 2 * size])
         outs = refs[4 + 2 * size : 4 + 3 * size], refs[4 + 3 * size :]
@@ -482,7 +494,7 @@
         "turn",
         body,
         [((4 * shape.rows, LANES), F32)] + [shape.array()] * (2 * size),
-        inputs=(angles,) + tuple(near) + tuple(far) + (field_b[1], field_b[2]),
+        inputs=(angles,) + sent_order(near) + sent_order(far) + (field_b[1], field_b[2]),
     )
     return result[0], result[1 : 1 + size], result[1 + size :]
 
@@ -557,67 +569,78 @@
         for start in range(0, shape.part, TILE):
             for v in range(shape.depth):
                 slots = [(u, v) for u in range(shape.depth)]
-                real, imag = load_slots(shape, "u", refs[1 : 1 + count], start, slots)
+                real, imag = load_slots(shape, "u", plain_order(refs[1 : 1 + count]), start, slots)
+                real, imag = butterflies(real, imag, pair, shape.bits("v"))
+                store_slots(shape, "part", refs[1 + count :], start, slots, real, imag)
+
+    size = ((2 * shape.rows * shape.batch // shape.depth, LANES), F32)
+    return vmem_call(
+        "post_send", body, [size] * (shape.depth // shape.batch), inputs=(angles,) + sent_order(arrays), hold=hold
+    )
+
+
+def flips_other(shape, other):
+    def body(*refs):
+        slots = shape.slots()
+        for start in range(0, shape.part, TILE):
+            real, imag = load_slots(shape, "other_part", refs[:-1], start, slots)
+            flips = [[flip_sum(values, i) for i in range(len(slots))] for values in (real, imag)]
+            store_slots(shape, "all", refs[-1:], start, slots, *flips)
+
+    return vmem_call("flips_other", body, [shape.whole()], inputs=tuple(other))[0]
+
+
+def post_mix(shape, angles, arrays, hold=()):
+    count = len(arrays)
+
+    def body(*refs):
+        pair = angle_pair(refs[0], 1)
+        for start in range(0, shape.part, TILE):
+            for v in range(shape.depth):
+                slots = [(u, v) for u in range(shape.depth)]
+                real, imag = load_slots(shape, "u", plain_order(refs[1 : 1 + count]), start, slots)
                 real, imag = butterflies(real, imag, pair, shape.bits("v"))
                 store_slots(shape, "all", [refs[1 + count]], start, slots, real, imag)
 
-    return vmem_call("post_send", body, [shape.whole()], inputs=(angles,) + tuple(arrays), hold=hold)[0]
-
-
-def flips_other(shape, other):
-    def body(ref, out):
+    return vmem_call(
+        "post_mix", body, [shape.whole()], inputs=(angles,) + sent_order(arrays), hold=hold
+    )[0]
+
+
+def post_grads(shape, mixed, other, flips, cost_a, hold=()):
+    def body(mixed_ref, flips_ref, cost, *refs):
+        others, out = refs[:-1], refs[-1]
+        piece = shape.piece()
         slots = shape.slots()
-        for start in range(0, shape.part, TILE):
-            real, imag = load_slots(shape, "other", [ref], start, slots)
-            flips = [[flip_sum(values, i) for i in range(len(slots))] for values in (real, imag)]
-            store_slots(shape, "all", [out], start, slots, *flips)
-
-    return vmem_call("flips_other", body, [shape.whole()], inputs=(other,))[0]
-
-
-def post_grads(shape, angles, arrays, other, flips, cost_a, hold=()):
-    count = len(arrays)
-
-    def body(*refs):
-        other_ref, flips_ref, cost = refs[1 + count : 4 + count]
-        mixed, out = refs[4 + count :]
-        piece = shape.piece()
-        pair = angle_pair(refs[0], 1)
         mix = jnp.zeros((TILE, LANES), F32)
         inter = jnp.zeros((TILE, LANES), F32)
         for start in range(0, shape.part, TILE):
-            for v in range(shape.depth):
-                slots = [(u, v) for u in range(shape.depth)]
-                real, imag = load_slots(shape, "u", refs[1 : 1 + count], start, slots)
-                real, imag = butterflies(real, imag, pair, shape.bits("v"))
-                store_slots(shape, "all", [mixed], start, slots, real, imag)
-                other_re, other_im = load_slots(shape, "other", [other_ref], start, slots)
-                flip_re, flip_im = load_slots(shape, "all", [flips_ref], start, slots)
-                for i, slot in enumerate(slots):
-                    mix = mix + flip_re[i] * imag[i] - flip_im[i] * real[i]
-                    row = pl.multiple_of(piece(*slot) * shape.part + start, TILE)
-                    value = cost[pl.ds(row, TILE), :]
-                    inter = inter + value * (other_re[i] * imag[i] - other_im[i] * real[i])
+            real, imag = load_slots(shape, "all", [mixed_ref], start, slots)
+            other_re, other_im = load_slots(shape, "other_part", others, start, slots)
+            flip_re, flip_im = load_slots(shape, "all", [flips_ref], start, slots)
+            for i, slot in enumerate(slots):
+                mix = mix + flip_re[i] * imag[i] - flip_im[i] * real[i]
+                row = pl.multiple_of(piece(*slot) * shape.part + start, TILE)
+                value = cost[pl.ds(row, TILE), :]
+                inter = inter + value * (other_re[i] * imag[i] - other_im[i] * real[i])
         out[0:1, :] = sign(jnp.sum(inter, axis=0, keepdims=True))
         out[1:2, :] = sign(jnp.sum(mix, axis=0, keepdims=True))
 
     return vmem_call(
-        "post_grads",
-        body,
-        [shape.whole(), ((2, LANES), F32)],
-        inputs=(angles,) + tuple(arrays) + (other, flips, cost_a),
-        hold=hold,
-    )
+        "post_grads", body, [((2, LANES), F32)], inputs=(mixed, flips, cost_a, *other), hold=hold
+    )[0]
 
 
 def post_phase(shape, mixed, other, field_a):
-    def body(own_ref, other_ref, cos_a, sin_a, psi_out, lam_out):
+    def body(own_ref, cos_a, sin_a, *refs):
+        others, (psi_out, lam_out, token) = refs[:-3], refs[-3:]
+        token[...] = jnp.zeros_like(token)
         first = lax.axis_index("core") == 0
         piece = shape.piece()
         slots = shape.slots()
         for start in range(0, shape.part, TILE):
             own_re, own_im = load_slots(shape, "all", [own_ref], start, slots)
-            other_re, other_im = load_slots(shape, "other", [other_ref], start, slots)
+            other_re, other_im = load_slots(shape, "other_part", others, start, slots)
             for i, slot in enumerate(slots):
                 row = pl.multiple_of(piece(*slot) * shape.part + start, TILE)
                 cosine, sine = cos_a[pl.ds(row, TILE), :], sin_a[pl.ds(row, TILE), :]
@@ -629,7 +652,10 @@
                     lam_out[span, :] = jnp.where(first, other_pair[j], own_pair[j])
 
     return vmem_call(
-        "post_phase", body, [shape.whole()] * 2, inputs=(mixed, other, field_a[1], field_a[2])
+        "post_phase",
+        body,
+        [shape.whole()] * 2 + [((TILE, LANES), F32)],
+        inputs=(mixed, field_a[1], field_a[2], *other),
     )
 
 
@@ -644,7 +670,7 @@
     size = shape.depth
     out = list(arrays)
     with jax.named_scope("exchange_" + form):
-        for i in sorted(range(1, size), key=lambda i: (i.bit_count() == 1, -i)):
+        for i in sorted(range(1, size), key=lambda i: (i > 1, i.bit_count() == 1, -i)):
             pairs = []
             for chip in range(size * size):
                 for core in range(CORES):
@@ -654,7 +680,7 @@
     return out
 
 
-def total_grads(shape, parts):
+def total_grads(shape, parts, token=None):
     def join(early, mid_part, late, out):
         rows = [late[0:1, :], late[1:2, :] + mid_part[0:1, :], mid_part[1:2, :], mid_part[2:3, :] + early[...]]
         out[...] = jnp.concatenate(rows + [jnp.zeros((TILE - 4, LANES), F32)], axis=0)
@@ -667,14 +693,16 @@
 
     block_shape = [((TILE, LANES), F32)]
     block = vmem_call("join_grads", join, block_shape, inputs=tuple(parts))[0]
-    for axis, size in (("core", CORES), ("grp", shape.groups), ("z", shape.depth)):
+    for axis, size, most in (("core", CORES, 2), ("grp", shape.groups, 4), ("z", shape.depth, 4)):
         stride = 1
         while stride < size:
-            reach = min(4, size // stride)
+            reach = min(most, size // stride)
             others = [
                 lax.ppermute(block, axis, [(j, j ^ (stride * i)) for j in range(size)]) for i in range(1, reach)
             ]
-            block = vmem_call("add_grads", add, block_shape, inputs=(block, *others))[0]
+            last = axis == "z" and stride * reach == size and token is not None
+            hold = (token,) if last else ()
+            block = vmem_call("add_grads", add, block_shape, inputs=(block, *others), hold=hold)[0]
             stride *= reach
     scale = 2.0 / (shape.rows * LANES * shape.devices)
 
@@ -875,15 +903,16 @@
     far = swap(shape, far, "v")
     near = swap(shape, near, "v")
     other_before = swap_cores(own_before)
-    far = swap(shape, rotate_local(shape, angles, far, "v", "u", mats[0], 1), "u")
+    far = swap(shape, rotate_local(shape, angles, far, "v", "u", mats[0], 1, hold=(other_before,)), "u")
     near = rotate_local(shape, angles, near, "v", "u", mats[0], 1)
-    other = swap_cores(post_send(shape, angles, far, hold=near[:1]))
+    mid_part = gradients_mid(shape, field_b, own_before, other_before)
+    other = [swap_cores(array) for array in post_send(shape, angles, far, hold=(near[0], mid_part, early))]
     near = swap(shape, near, "u")
-    mid_part = gradients_mid(shape, field_b, own_before, other_before)
     flips = flips_other(shape, other)
-    mixed, late = post_grads(shape, angles, near, other, flips, field_a[0], hold=(mid_part, early))
-    grads = total_grads(shape, (early, mid_part, late))
-    psi_out, lam_out = post_phase(shape, mixed, other, field_a)
+    mixed = post_mix(shape, angles, near, hold=(mid_part, early))
+    late = post_grads(shape, mixed, other, flips, field_a[0])
+    psi_out, lam_out, token = post_phase(shape, mixed, other, field_a)
+    grads = total_grads(shape, (early, mid_part, late), token)
     return deinterleave(psi_out, rows), deinterleave(lam_out, rows), grads
 
 

time: 81.1 us -> 74.7 us (0.921)
  waiting for transfers between devices: 19.4 us -> 12.9 us
  starting transfers between devices: 41.5 us -> 43.6 us
  Pallas kernels: 16.8 us -> 15.8 us
  local copies, waits for them, and re-layouts: 2.24 us -> 1.32 us
    ppermute x24, waiting for transfers between devices: 14.1 us -> 8.23 us  [swap(): out[i] = lax.ppermute(arrays[i], AXES, pairs)]
    ppermute x24, starting transfers between devices: 32.7 us -> 34.1 us  [swap(): out[i] = lax.ppermute(arrays[i], AXES, pairs)]
    pallas_call x1, Pallas kernels: 2.52 us -> 1.38 us  [pre_near(): pl.pallas_call(body, name='pre_near', out_shape=[jax.ShapeDtypeStruct(siz...]
    unnamed x18 -> x10, local copies, waits for them, and re-layouts: 2.24 us -> 1.32 us
    pallas_call x18 -> x19, Pallas kernels: 10.5 us -> 10.6 us  [vmem_call(): pl.pallas_call(body, name=name, out_shape=[jax.ShapeDtypeStruct(shape, ki...]
  transfers between devices with their start and end apart: 34 -> 37, of which waited for: 13 -> 12; matrix products, arithmetic and copies ran while one was open for 0% -> 0% of each run, Pallas kernels for 15% -> 17%
where the time goes in v2:
time: 74.7 us; the launch traced here: 74.5 us
  starting transfers between devices  43.6 us (58%)
  Pallas kernels  15.8 us (21%)
  waiting for transfers between devices  12.9 us (17%)
  local copies, waits for them, and re-layouts  1.32 us (2%)
  between operations  1.02 us (1%)
    ppermute x24, starting transfers between devices, swap(): out[i] = lax.ppermute(arrays[i], AXES, pairs)  34.1 us
    pallas_call x19, Pallas kernels, vmem_call(): pl.pallas_call(body, name=name, out_shape=[jax.ShapeDtypeStruct(shape, ki...  10.6 us
    ppermute x24, waiting for transfers between devices, swap(): out[i] = lax.ppermute(arrays[i], AXES, pairs)  8.23 us
    ppermute x7, starting transfers between devices, total_grads(): lax.ppermute(block, axis, [(j, j ^ stride * i) for j in range(size)])  8.09 us
    ppermute x7, waiting for transfers between devices, total_grads(): lax.ppermute(block, axis, [(j, j ^ stride * i) for j in range(size)])  4.5 us
    pallas_call x2, Pallas kernels, make_fields(): pl.pallas_call(body, name='make_fields', out_shape=[jax.ShapeDtypeStruct(...  3.76 us
  transfers between devices with their start and end apart: 37, of which 12 were waited for; matrix products, arithmetic and copies ran while one was open for 0% of the time, Pallas kernels for 17%

profile of v2, /device:TPU:0, one launch (start us, length us, event | category | flops | bytes accessed | tf_op | source)
XLA Modules:
  0.0 74.5 jit_solution(4216139241117733319)
XLA Ops:
  0.6 0.6 copy-done
  1.3 1.4 %pre_near.1 = (f32[1024,128]{1,0:T(8,128)S(1)}, f32[1024,128]{1,0:T(8,128)S(1)}, f32[256,128]{1,0:T(8,128)S(1)}, f32[256,128]{1,0:T(8,128)S(1)}, f32[256,128]{1,0:T(8,128)S(1)}, /*index=5*/f32[256,128]{1,0:T(8,128)S(1)}) custom-call(f32[1,4]{1,0:T(1,128)S(1)} %bitcast.25, f32[1024,128]{1,0:T(8,128)} %bitcast.45, f32[1024,128]{1,0:T(8,128)} %bitcast.46), custom_call_target="tpu_custom_call" | custom-call | tf_op jit(solution)/shard_map/pre_near/pallas_call | solution.py:424
  2.7 0.5 collective-permute-start.6
  3.2 3.7 %collective-permute-start = (f32[256,128]{1,0:T(8,128)S(1)}, f32[256,128]{1,0:T(8,128)S(1)}, u32[]{:S(2)}, u32[]{:S(2)}) collective-permute-start(f32[256,128]{1,0:T(8,128)S(1)} %get-tuple-element.71), channel_id=1, source_target_pairs={{0,4},{1,17},{2,6},{3,19},{4,0},{5,21},{6,2},{7,23},{8,12},{9,25},... | collective-permute-start | bytes 393224 | tf_op jit(solution)/shard_map/exchange_u/ppermute | solution.py:679
  6.9 1.3 %collective-permute-start.1 = (f32[256,128]{1,0:T(8,128)S(1)}, f32[256,128]{1,0:T(8,128)S(1)}, u32[]{:S(2)}, u32[]{:S(2)}) collective-permute-start(f32[256,128]{1,0:T(8,128)S(1)} %get-tuple-element.72), channel_id=1, source_target_pairs={{0,6},{1,25},{2,4},{3,27},{4,2},{5,29},{6,0},{7,31},{8,14},{9,17},... | collective-permute-start | bytes 393224 | tf_op jit(solution)/shard_map/exchange_u/ppermute | solution.py:679
  8.2 0.2 collective-permute-start.2
  8.4 0.4 make_mats.1
  8.9 0.2 copy-done.3
  9.1 0.4 copy-done.1
  9.6 0.2 pre_far.1
  9.8 2.9 %collective-permute-start.7 = (f32[256,128]{1,0:T(8,128)S(1)}, f32[256,128]{1,0:T(8,128)S(1)}, u32[]{:S(2)}, u32[]{:S(2)}) collective-permute-start(f32[256,128]{1,0:T(8,128)S(1)} %get-tuple-element.85), channel_id=1, source_target_pairs={{0,4},{1,17},{2,6},{3,19},{4,0},{5,21},{6,2},{7,23},{8,12},{9,25},... | collective-permute-start | bytes 393224 | tf_op jit(solution)/shard_map/exchange_u/ppermute | solution.py:679
  12.6 1.3 %collective-permute-start.8 = (f32[256,128]{1,0:T(8,128)S(1)}, f32[256,128]{1,0:T(8,128)S(1)}, u32[]{:S(2)}, u32[]{:S(2)}) collective-permute-start(f32[256,128]{1,0:T(8,128)S(1)} %get-tuple-element.86), channel_id=1, source_target_pairs={{0,6},{1,25},{2,4},{3,27},{4,2},{5,29},{6,0},{7,31},{8,14},{9,17},... | collective-permute-start | bytes 393224 | tf_op jit(solution)/shard_map/exchange_u/ppermute | solution.py:679
  14.0 1.9 %collective-permute-done.2.refs_3_ = f32[256,128]{1,0:T(8,128)S(1)} collective-permute-done((f32[256,128]{1,0:T(8,128)S(1)}, f32[256,128]{1,0:T(8,128)S(1)}, u32[]{:S(2)}, u32[]{:S(2)}) %collective-permute-start.2) | collective-permute-done | bytes 131104 | tf_op jit(solution)/shard_map/exchange_u/ppermute | solution.py:679
  15.9 1.3 %rotate_local.4 = (f32[256,128]{1,0:T(8,128)S(1)}, f32[256,128]{1,0:T(8,128)S(1)}, f32[256,128]{1,0:T(8,128)S(1)}, f32[256,128]{1,0:T(8,128)S(1)}) custom-call(f32[1,4]{1,0:T(1,128)S(1)} %bitcast.29, f32[256,128]{1,0:T(8,128)S(1)} %collective-permute-done.refs_1_, f32[256,128]{1,0:T(8,128)S(1)} %collective-permute-done.1.refs_2_, ...), custom_call_target="tpu_custom_call" | custom-call | tf_op jit(solution)/shard_map/rotate_local/pallas_call | solution.py:31
  17.2 1.5 %collective-permute-start.3 = (f32[256,128]{1,0:T(8,128)S(1)}, f32[256,128]{1,0:T(8,128)S(1)}, u32[]{:S(2)}, u32[]{:S(2)}) collective-permute-start(f32[256,128]{1,0:T(8,128)S(1)} %get-tuple-element.80), channel_id=1, source_target_pairs={{0,16},{1,5},{2,18},{3,7},{4,20},{5,1},{6,22},{7,3},{8,24},{9,13},... | collective-permute-start | bytes 393224 | tf_op jit(solution)/shard_map/exchange_v/ppermute | solution.py:679
  18.8 1.4 %collective-permute-start.4 = (f32[256,128]{1,0:T(8,128)S(1)}, f32[256,128]{1,0:T(8,128)S(1)}, u32[]{:S(2)}, u32[]{:S(2)}) collective-permute-start(f32[256,128]{1,0:T(8,128)S(1)} %get-tuple-element.81), channel_id=1, source_target_pairs={{0,24},{1,7},{2,26},{3,5},{4,28},{5,3},{6,30},{7,1},{8,16},{9,15},... | collective-permute-start | bytes 393224 | tf_op jit(solution)/shard_map/exchange_v/ppermute | solution.py:679
  20.2 0.6 collective-permute-start.5
  20.8 0.7 collective-permute-done.9.refs_3_
  21.4 1.4 %rotate_local.5 = (f32[256,128]{1,0:T(8,128)S(1)}, f32[256,128]{1,0:T(8,128)S(1)}, f32[256,128]{1,0:T(8,128)S(1)}, f32[256,128]{1,0:T(8,128)S(1)}) custom-call(f32[1,4]{1,0:T(1,128)S(1)} %bitcast.30, f32[256,128]{1,0:T(8,128)S(1)} %collective-permute-done.7.refs_1_, f32[256,128]{1,0:T(8,128)S(1)} %collective-permute-done.8.refs_2_, ...), custom_call_target="tpu_custom_call" | custom-call | tf_op jit(solution)/shard_map/rotate_local/pallas_call | solution.py:31
  22.8 1.5 %collective-permute-start.10 = (f32[256,128]{1,0:T(8,128)S(1)}, f32[256,128]{1,0:T(8,128)S(1)}, u32[]{:S(2)}, u32[]{:S(2)}) collective-permute-start(f32[256,128]{1,0:T(8,128)S(1)} %get-tuple-element.89), channel_id=1, source_target_pairs={{0,16},{1,5},{2,18},{3,7},{4,20},{5,1},{6,22},{7,3},{8,24},{9,13},... | collective-permute-start | bytes 393224 | tf_op jit(solution)/shard_map/exchange_v/ppermute | solution.py:679
  24.3 1.4 %collective-permute-start.11 = (f32[256,128]{1,0:T(8,128)S(1)}, f32[256,128]{1,0:T(8,128)S(1)}, u32[]{:S(2)}, u32[]{:S(2)}) collective-permute-start(f32[256,128]{1,0:T(8,128)S(1)} %get-tuple-element.90), channel_id=1, source_target_pairs={{0,24},{1,7},{2,26},{3,5},{4,28},{5,3},{6,30},{7,1},{8,16},{9,15},... | collective-permute-start | bytes 393224 | tf_op jit(solution)/shard_map/exchange_v/ppermute | solution.py:679
  25.8 0.6 collective-permute-start.12
  26.4 3.8 %make_fields.3 = (f32[512,128]{1,0:T(8,128)S(1)}, f32[512,128]{1,0:T(8,128)S(1)}, f32[512,128]{1,0:T(8,128)S(1)}, f32[1024,128]{1,0:T(8,128)S(1)}, f32[1024,128]{1,0:T(8,128)S(1)}, /*index=5*/f32[1024,128]{1,0:T(8,128)S(1)}) custom-call(f32[1,4]{1,0:T(1,128)S(1)} %bitcast.31, ...), custom_call_target="tpu_custom_call", output_to_operand_aliasing={{0}: (5, {}), {1}: (6, {}), {2}: (7, {}), {3}: (8, {}), {4}... | custom-call | tf_op jit(solution)/shard_map/make_fields/pallas_call | solution.py:205
  30.2 0.5 collective-permute-done.12.refs_7_
  30.7 0.8 %turn.1 = (f32[2048,128]{1,0:T(8,128)S(1)}, f32[256,128]{1,0:T(8,128)S(1)}, f32[256,128]{1,0:T(8,128)S(1)}, f32[256,128]{1,0:T(8,128)S(1)}, f32[256,128]{1,0:T(8...) custom-call(f32[1,4]{1,0:T(1,128)S(1)} %bitcast.32, ...), custom_call_target="tpu_custom_call" | custom-call | tf_op jit(solution)/shard_map/turn/pallas_call | solution.py:31
  31.5 0.3 collective-permute-start.19
  31.8 1.6 %collective-permute-start.20 = (f32[256,128]{1,0:T(8,128)S(1)}, f32[256,128]{1,0:T(8,128)S(1)}, u32[]{:S(2)}, u32[]{:S(2)}) collective-permute-start(f32[256,128]{1,0:T(8,128)S(1)} %get-tuple-element.123), channel_id=1, source_target_pairs={{0,16},{1,5},{2,18},{3,7},{4,20},{5,1},{6,22},{7,3},{8,24},{9,13},... | collective-permute-start | bytes 393224 | tf_op jit(solution)/shard_map/exchange_v/ppermute | solution.py:679
  33.3 1.4 %collective-permute-start.21 = (f32[256,128]{1,0:T(8,128)S(1)}, f32[256,128]{1,0:T(8,128)S(1)}, u32[]{:S(2)}, u32[]{:S(2)}) collective-permute-start(f32[256,128]{1,0:T(8,128)S(1)} %get-tuple-element.124), channel_id=1, source_target_pairs={{0,24},{1,7},{2,26},{3,5},{4,28},{5,3},{6,30},{7,1},{8,16},{9,15},... | collective-permute-start | bytes 393224 | tf_op jit(solution)/shard_map/exchange_v/ppermute | solution.py:679
  34.8 0.5 collective-permute-start.22
  35.3 1.6 %collective-permute-start.13 = (f32[256,128]{1,0:T(8,128)S(1)}, f32[256,128]{1,0:T(8,128)S(1)}, u32[]{:S(2)}, u32[]{:S(2)}) collective-permute-start(f32[256,128]{1,0:T(8,128)S(1)} %get-tuple-element.106), channel_id=1, source_target_pairs={{0,16},{1,5},{2,18},{3,7},{4,20},{5,1},{6,22},{7,3},{8,24},{9,13},... | collective-permute-start | bytes 393224 | tf_op jit(solution)/shard_map/exchange_v/ppermute | solution.py:679
  36.8 2.4 %collective-permute-start.14 = (f32[256,128]{1,0:T(8,128)S(1)}, f32[256,128]{1,0:T(8,128)S(1)}, u32[]{:S(2)}, u32[]{:S(2)}) collective-permute-start(f32[256,128]{1,0:T(8,128)S(1)} %get-tuple-element.107), channel_id=1, source_target_pairs={{0,24},{1,7},{2,26},{3,5},{4,28},{5,3},{6,30},{7,1},{8,16},{9,15},... | collective-permute-start | bytes 393224 | tf_op jit(solution)/shard_map/exchange_v/ppermute | solution.py:679
  39.3 1.5 %collective-permute-start.15 = (f32[256,128]{1,0:T(8,128)S(1)}, f32[256,128]{1,0:T(8,128)S(1)}, u32[]{:S(2)}, u32[]{:S(2)}) collective-permute-start(f32[256,128]{1,0:T(8,128)S(1)} %get-tuple-element.108), channel_id=1, source_target_pairs={{0,8},{1,3},{2,10},{3,1},{4,12},{5,7},{6,14},{7,5},{8,0},{9,11},{1... | collective-permute-start | bytes 393224 | tf_op jit(solution)/shard_map/exchange_v/ppermute | solution.py:679
  40.7 1.4 %rotate_local.7 = (f32[256,128]{1,0:T(8,128)S(1)}, f32[256,128]{1,0:T(8,128)S(1)}, f32[256,128]{1,0:T(8,128)S(1)}, f32[256,128]{1,0:T(8,128)S(1)}) custom-call(f32[1,4]{1,0:T(1,128)S(1)} %bitcast.33, f32[256,128]{1,0:T(8,128)S(1)} %collective-permute-done.20.refs_1_, f32[256,128]{1,0:T(8,128)S(1)} %collective-permute-done.21.refs_2_, ...), custom_call_target="tpu_custom_call" | custom-call | tf_op jit(solution)/shard_map/rotate_local/pallas_call | solution.py:31
  42.1 3.4 %collective-permute-start.23 = (f32[256,128]{1,0:T(8,128)S(1)}, f32[256,128]{1,0:T(8,128)S(1)}, u32[]{:S(2)}, u32[]{:S(2)}) collective-permute-start(f32[256,128]{1,0:T(8,128)S(1)} %get-tuple-element.127), channel_id=1, source_target_pairs={{0,4},{1,17},{2,6},{3,19},{4,0},{5,21},{6,2},{7,23},{8,12},{9,25},... | collective-permute-start | bytes 393224 | tf_op jit(solution)/shard_map/exchange_u/ppermute | solution.py:679
  45.5 0.1 collective-permute-start.24
  45.7 0.5 collective-permute-start.25
  46.2 1.3 %rotate_local.6 = (f32[256,128]{1,0:T(8,128)S(1)}, f32[256,128]{1,0:T(8,128)S(1)}, f32[256,128]{1,0:T(8,128)S(1)}, f32[256,128]{1,0:T(8,128)S(1)}) custom-call(f32[1,4]{1,0:T(1,128)S(1)} %bitcast.34, f32[256,128]{1,0:T(8,128)S(1)} %collective-permute-done.13.refs_1_, f32[256,128]{1,0:T(8,128)S(1)} %collective-permute-done.14.refs_2_, ...), custom_call_target="tpu_custom_call" | custom-call | tf_op jit(solution)/shard_map/rotate_local/pallas_call | solution.py:31
  47.5 3.8 %collective-permute-start.16 = (f32[256,128]{1,0:T(8,128)S(1)}, f32[256,128]{1,0:T(8,128)S(1)}, u32[]{:S(2)}, u32[]{:S(2)}) collective-permute-start(f32[256,128]{1,0:T(8,128)S(1)} %get-tuple-element.114), channel_id=1, source_target_pairs={{0,4},{1,17},{2,6},{3,19},{4,0},{5,21},{6,2},{7,23},{8,12},{9,25},... | collective-permute-start | bytes 393224 | tf_op jit(solution)/shard_map/exchange_u/ppermute | solution.py:679
  51.4 0.1 collective-permute-start.17
  51.5 0.1 flip_raw.1.refs_6_.refs_7_.early
  51.6 1.2 %gradients_mid.1.refs_5_.refs_6_.mid_part = f32[3,128]{1,0:T(4,128)S(1)} custom-call(f32[1024,128]{1,0:T(8,128)S(1)} %get-tuple-element.118.cost, f32[1024,128]{1,0:T(8,128)S(1)} %get-tuple-element.104.refs_9_.cos_b, f32[1024,128]{1,0:T(8,128)S(1)} %get-tuple-element.105.refs_10_.sin_b, f32[2048,128]{1,0:T(8,128)S(1)} %get-tuple-element.119.own_ref, ...), custom_call_target="tpu_custom_call" | custom-call | tf_op jit(solution)/shard_map/gradients_mid/pallas_call | solution.py:31
  52.8 0.6 collective-permute-start.18
  53.4 0.2 post_send.1
  53.7 0.5 collective-permute-start.27
  54.2 1.5 %collective-permute-done.16.refs_1_ = f32[256,128]{1,0:T(8,128)S(1)} collective-permute-done((f32[256,128]{1,0:T(8,128)S(1)}, f32[256,128]{1,0:T(8,128)S(1)}, u32[]{:S(2)}, u32[]{:S(2)}) %collective-permute-start.16) | collective-permute-done | bytes 131104 | tf_op jit(solution)/shard_map/exchange_u/ppermute | solution.py:679
  55.7 2.6 %collective-permute-done.17.refs_2_ = f32[256,128]{1,0:T(8,128)S(1)} collective-permute-done((f32[256,128]{1,0:T(8,128)S(1)}, f32[256,128]{1,0:T(8,128)S(1)}, u32[]{:S(2)}, u32[]{:S(2)}) %collective-permute-start.17) | collective-permute-done | bytes 131104 | tf_op jit(solution)/shard_map/exchange_u/ppermute | solution.py:679
  58.3 1.0 %collective-permute-done.18.refs_3_ = f32[256,128]{1,0:T(8,128)S(1)} collective-permute-done((f32[256,128]{1,0:T(8,128)S(1)}, f32[256,128]{1,0:T(8,128)S(1)}, u32[]{:S(2)}, u32[]{:S(2)}) %collective-permute-start.18) | collective-permute-done | bytes 131104 | tf_op jit(solution)/shard_map/exchange_u/ppermute | solution.py:679
  59.3 0.2 post_mix.1.own_ref.mixed_ref
  59.5 0.1 collective-permute-done.29.refs_3_
  59.7 0.2 post_grads.1.late
  60.0 0.2 collective-permute-start.30
  60.2 1.0 %collective-permute-done.30.refs_1_ = f32[8,128]{1,0:T(8,128)S(1)} collective-permute-done((f32[8,128]{1,0:T(8,128)S(1)}, f32[8,128]{1,0:T(8,128)S(1)}, u32[]{:S(2)}, u32[]{:S(2)}) %collective-permute-start.30) | collective-permute-done | bytes 4128 | tf_op jit(solution)/shard_map/ppermute | solution.py:701
  61.2 1.6 %collective-permute-start.33 = (f32[8,128]{1,0:T(8,128)S(1)}, f32[8,128]{1,0:T(8,128)S(1)}, u32[]{:S(2)}, u32[]{:S(2)}) collective-permute-start(f32[8,128]{1,0:T(8,128)S(1)} %add_grads.3.refs_0_), channel_id=1, source_target_pairs={{0,24},{8,16},{16,8},{24,0},{1,25},{9,17},{17,9},{25,1},{2,26},{10... | collective-permute-start | bytes 12296 | tf_op jit(solution)/shard_map/ppermute | solution.py:701
  62.8 0.5 collective-permute-start.32
  63.3 1.4 %collective-permute-start.31 = (f32[8,128]{1,0:T(8,128)S(1)}, f32[8,128]{1,0:T(8,128)S(1)}, u32[]{:S(2)}, u32[]{:S(2)}) collective-permute-start(f32[8,128]{1,0:T(8,128)S(1)} %add_grads.3.refs_0_), channel_id=1, source_target_pairs={{0,8},{8,0},{16,24},{24,16},{1,9},{9,1},{17,25},{25,17},{2,10},{10... | collective-permute-start | bytes 12296 | tf_op jit(solution)/shard_map/ppermute | solution.py:701
  64.7 1.0 %collective-permute-done.33.refs_3_ = f32[8,128]{1,0:T(8,128)S(1)} collective-permute-done((f32[8,128]{1,0:T(8,128)S(1)}, f32[8,128]{1,0:T(8,128)S(1)}, u32[]{:S(2)}, u32[]{:S(2)}) %collective-permute-start.33) | collective-permute-done | bytes 4128 | tf_op jit(solution)/shard_map/ppermute | solution.py:701
  65.7 0.7 collective-permute-done.32.refs_2_
  66.4 0.5 collective-permute-done.31.refs_1_
  66.9 2.3 %collective-permute-start.36 = (f32[8,128]{1,0:T(8,128)S(1)}, f32[8,128]{1,0:T(8,128)S(1)}, u32[]{:S(2)}, u32[]{:S(2)}) collective-permute-start(f32[8,128]{1,0:T(8,128)S(1)} %add_grads.4.refs_0_), channel_id=1, source_target_pairs={{0,6},{2,4},{4,2},{6,0},{1,7},{3,5},{5,3},{7,1},{8,14},{10,12},{12... | collective-permute-start | bytes 12296 | tf_op jit(solution)/shard_map/ppermute | solution.py:701
  69.2 0.8 %collective-permute-start.35 = (f32[8,128]{1,0:T(8,128)S(1)}, f32[8,128]{1,0:T(8,128)S(1)}, u32[]{:S(2)}, u32[]{:S(2)}) collective-permute-start(f32[8,128]{1,0:T(8,128)S(1)} %add_grads.4.refs_0_), channel_id=1, source_target_pairs={{0,4},{2,6},{4,0},{6,2},{1,5},{3,7},{5,1},{7,3},{8,12},{10,14},{12... | collective-permute-start | bytes 12296 | tf_op jit(solution)/shard_map/ppermute | solution.py:701
  70.0 1.3 %collective-permute-start.34 = (f32[8,128]{1,0:T(8,128)S(1)}, f32[8,128]{1,0:T(8,128)S(1)}, u32[]{:S(2)}, u32[]{:S(2)}) collective-permute-start(f32[8,128]{1,0:T(8,128)S(1)} %add_grads.4.refs_0_), channel_id=1, source_target_pairs={{0,2},{2,0},{4,6},{6,4},{1,3},{3,1},{5,7},{7,5},{8,10},{10,8},{12,... | collective-permute-start | bytes 12296 | tf_op jit(solution)/shard_map/ppermute | solution.py:701
  71.3 1.2 %post_phase.1 = (f32[1024,128]{1,0:T(8,128)}, f32[1024,128]{1,0:T(8,128)}, f32[8,128]{1,0:T(8,128)S(1)}) custom-call(f32[1024,128]{1,0:T(8,128)S(1)} %post_mix.1.own_ref.mixed_ref, f32[512,128]{1,0:T(8,128)S(1)} %get-tuple-element.121.cos_a, f32[512,128]{1,0:T(8,128)S(1)} %get-tuple-element.122.sin_a, f32[256,128]{1,0:T(8,128)S(1)} %collective-permute-done.26.refs_0_, ...), custom_call_target="tpu_custom_call" | custom-call | tf_op jit(solution)/shard_map/post_phase/pallas_call | solution.py:31
  72.5 1.3 %collective-permute-done.35.refs_2_ = f32[8,128]{1,0:T(8,128)S(1)} collective-permute-done((f32[8,128]{1,0:T(8,128)S(1)}, f32[8,128]{1,0:T(8,128)S(1)}, u32[]{:S(2)}, u32[]{:S(2)}) %collective-permute-start.35) | collective-permute-done | bytes 4128 | tf_op jit(solution)/shard_map/ppermute | solution.py:701
  73.8 0.6 finish_grads.1
  (42 shorter events, 0.3 us)
Async XLA Ops:
  0.6 0.7 copy-start
  2.7 6.9 %collective-permute-start.6 = (f32[1024,128]{1,0:T(8,128)S(1)}, f32[1024,128]{1,0:T(8,128)S(1)}, u32[]{:S(2)}, u32[]{:S(2)}) collective-permute-start(f32[1024,128]{1,0:T(8,128)S(1)} %get-tuple-element.84.refs_1_), channel_id=1, source_target_pairs={{0,1},{1,0},{2,3},{3,2},{4,5},{5,4},{6,7},{7,6},{8,9},{9,8},{10,11... | collective-permute-start | bytes 1572872 | tf_op jit(solution)/shard_map/ppermute | solution.py:666
  3.2 10.8 %collective-permute-start = (f32[256,128]{1,0:T(8,128)S(1)}, f32[256,128]{1,0:T(8,128)S(1)}, u32[]{:S(2)}, u32[]{:S(2)}) collective-permute-start(f32[256,128]{1,0:T(8,128)S(1)} %get-tuple-element.71), channel_id=1, source_target_pairs={{0,4},{1,17},{2,6},{3,19},{4,0},{5,21},{6,2},{7,23},{8,12},{9,25},... | collective-permute-start | bytes 393224 | tf_op jit(solution)/shard_map/exchange_u/ppermute | solution.py:679
  6.9 7.1 %collective-permute-start.1 = (f32[256,128]{1,0:T(8,128)S(1)}, f32[256,128]{1,0:T(8,128)S(1)}, u32[]{:S(2)}, u32[]{:S(2)}) collective-permute-start(f32[256,128]{1,0:T(8,128)S(1)} %get-tuple-element.72), channel_id=1, source_target_pairs={{0,6},{1,25},{2,4},{3,27},{4,2},{5,29},{6,0},{7,31},{8,14},{9,17},... | collective-permute-start | bytes 393224 | tf_op jit(solution)/shard_map/exchange_u/ppermute | solution.py:679
  8.2 7.7 %collective-permute-start.2 = (f32[256,128]{1,0:T(8,128)S(1)}, f32[256,128]{1,0:T(8,128)S(1)}, u32[]{:S(2)}, u32[]{:S(2)}) collective-permute-start(f32[256,128]{1,0:T(8,128)S(1)} %get-tuple-element.73), channel_id=1, source_target_pairs={{0,2},{1,9},{2,0},{3,11},{4,6},{5,13},{6,4},{7,15},{8,10},{9,1},{1... | collective-permute-start | bytes 393224 | tf_op jit(solution)/shard_map/exchange_u/ppermute | solution.py:679
  8.4 0.7 copy-start.3
  8.4 0.7 copy-start.4
  8.9 0.7 copy-start.1
  8.9 0.7 copy-start.2
  9.8 10.4 %collective-permute-start.7 = (f32[256,128]{1,0:T(8,128)S(1)}, f32[256,128]{1,0:T(8,128)S(1)}, u32[]{:S(2)}, u32[]{:S(2)}) collective-permute-start(f32[256,128]{1,0:T(8,128)S(1)} %get-tuple-element.85), channel_id=1, source_target_pairs={{0,4},{1,17},{2,6},{3,19},{4,0},{5,21},{6,2},{7,23},{8,12},{9,25},... | collective-permute-start | bytes 393224 | tf_op jit(solution)/shard_map/exchange_u/ppermute | solution.py:679
  12.6 8.1 %collective-permute-start.8 = (f32[256,128]{1,0:T(8,128)S(1)}, f32[256,128]{1,0:T(8,128)S(1)}, u32[]{:S(2)}, u32[]{:S(2)}) collective-permute-start(f32[256,128]{1,0:T(8,128)S(1)} %get-tuple-element.86), channel_id=1, source_target_pairs={{0,6},{1,25},{2,4},{3,27},{4,2},{5,29},{6,0},{7,31},{8,14},{9,17},... | collective-permute-start | bytes 393224 | tf_op jit(solution)/shard_map/exchange_u/ppermute | solution.py:679
  14.0 7.4 %collective-permute-start.9 = (f32[256,128]{1,0:T(8,128)S(1)}, f32[256,128]{1,0:T(8,128)S(1)}, u32[]{:S(2)}, u32[]{:S(2)}) collective-permute-start(f32[256,128]{1,0:T(8,128)S(1)} %get-tuple-element.87), channel_id=1, source_target_pairs={{0,2},{1,9},{2,0},{3,11},{4,6},{5,13},{6,4},{7,15},{8,10},{9,1},{1... | collective-permute-start | bytes 393224 | tf_op jit(solution)/shard_map/exchange_u/ppermute | solution.py:679
  17.2 8.5 %collective-permute-start.3 = (f32[256,128]{1,0:T(8,128)S(1)}, f32[256,128]{1,0:T(8,128)S(1)}, u32[]{:S(2)}, u32[]{:S(2)}) collective-permute-start(f32[256,128]{1,0:T(8,128)S(1)} %get-tuple-element.80), channel_id=1, source_target_pairs={{0,16},{1,5},{2,18},{3,7},{4,20},{5,1},{6,22},{7,3},{8,24},{9,13},... | collective-permute-start | bytes 393224 | tf_op jit(solution)/shard_map/exchange_v/ppermute | solution.py:679
  18.8 11.4 %collective-permute-start.4 = (f32[256,128]{1,0:T(8,128)S(1)}, f32[256,128]{1,0:T(8,128)S(1)}, u32[]{:S(2)}, u32[]{:S(2)}) collective-permute-start(f32[256,128]{1,0:T(8,128)S(1)} %get-tuple-element.81), channel_id=1, source_target_pairs={{0,24},{1,7},{2,26},{3,5},{4,28},{5,3},{6,30},{7,1},{8,16},{9,15},... | collective-permute-start | bytes 393224 | tf_op jit(solution)/shard_map/exchange_v/ppermute | solution.py:679
  20.2 9.9 %collective-permute-start.5 = (f32[256,128]{1,0:T(8,128)S(1)}, f32[256,128]{1,0:T(8,128)S(1)}, u32[]{:S(2)}, u32[]{:S(2)}) collective-permute-start(f32[256,128]{1,0:T(8,128)S(1)} %get-tuple-element.82), channel_id=1, source_target_pairs={{0,8},{1,3},{2,10},{3,1},{4,12},{5,7},{6,14},{7,5},{8,0},{9,11},{1... | collective-permute-start | bytes 393224 | tf_op jit(solution)/shard_map/exchange_v/ppermute | solution.py:679
  22.8 7.4 %collective-permute-start.10 = (f32[256,128]{1,0:T(8,128)S(1)}, f32[256,128]{1,0:T(8,128)S(1)}, u32[]{:S(2)}, u32[]{:S(2)}) collective-permute-start(f32[256,128]{1,0:T(8,128)S(1)} %get-tuple-element.89), channel_id=1, source_target_pairs={{0,16},{1,5},{2,18},{3,7},{4,20},{5,1},{6,22},{7,3},{8,24},{9,13},... | collective-permute-start | bytes 393224 | tf_op jit(solution)/shard_map/exchange_v/ppermute | solution.py:679
  24.3 5.9 %collective-permute-start.11 = (f32[256,128]{1,0:T(8,128)S(1)}, f32[256,128]{1,0:T(8,128)S(1)}, u32[]{:S(2)}, u32[]{:S(2)}) collective-permute-start(f32[256,128]{1,0:T(8,128)S(1)} %get-tuple-element.90), channel_id=1, source_target_pairs={{0,24},{1,7},{2,26},{3,5},{4,28},{5,3},{6,30},{7,1},{8,16},{9,15},... | collective-permute-start | bytes 393224 | tf_op jit(solution)/shard_map/exchange_v/ppermute | solution.py:679
  25.8 5.0 %collective-permute-start.12 = (f32[256,128]{1,0:T(8,128)S(1)}, f32[256,128]{1,0:T(8,128)S(1)}, u32[]{:S(2)}, u32[]{:S(2)}) collective-permute-start(f32[256,128]{1,0:T(8,128)S(1)} %get-tuple-element.91), channel_id=1, source_target_pairs={{0,8},{1,3},{2,10},{3,1},{4,12},{5,7},{6,14},{7,5},{8,0},{9,11},{1... | collective-permute-start | bytes 393224 | tf_op jit(solution)/shard_map/exchange_v/ppermute | solution.py:679
  31.5 9.2 %collective-permute-start.19 = (f32[2048,128]{1,0:T(8,128)S(1)}, f32[2048,128]{1,0:T(8,128)S(1)}, u32[]{:S(2)}, u32[]{:S(2)}) collective-permute-start(f32[2048,128]{1,0:T(8,128)S(1)} %get-tuple-element.119.own_ref), channel_id=1, source_target_pairs={{0,1},{1,0},{2,3},{3,2},{4,5},{5,4},{6,7},{7,6},{8,9},{9,8},{10,11... | collective-permute-start | bytes 3145736 | tf_op jit(solution)/shard_map/ppermute | solution.py:666
  31.8 5.1 %collective-permute-start.20 = (f32[256,128]{1,0:T(8,128)S(1)}, f32[256,128]{1,0:T(8,128)S(1)}, u32[]{:S(2)}, u32[]{:S(2)}) collective-permute-start(f32[256,128]{1,0:T(8,128)S(1)} %get-tuple-element.123), channel_id=1, source_target_pairs={{0,16},{1,5},{2,18},{3,7},{4,20},{5,1},{6,22},{7,3},{8,24},{9,13},... | collective-permute-start | bytes 393224 | tf_op jit(solution)/shard_map/exchange_v/ppermute | solution.py:679
  33.3 5.9 %collective-permute-start.21 = (f32[256,128]{1,0:T(8,128)S(1)}, f32[256,128]{1,0:T(8,128)S(1)}, u32[]{:S(2)}, u32[]{:S(2)}) collective-permute-start(f32[256,128]{1,0:T(8,128)S(1)} %get-tuple-element.124), channel_id=1, source_target_pairs={{0,24},{1,7},{2,26},{3,5},{4,28},{5,3},{6,30},{7,1},{8,16},{9,15},... | collective-permute-start | bytes 393224 | tf_op jit(solution)/shard_map/exchange_v/ppermute | solution.py:679
  34.8 6.0 %collective-permute-start.22 = (f32[256,128]{1,0:T(8,128)S(1)}, f32[256,128]{1,0:T(8,128)S(1)}, u32[]{:S(2)}, u32[]{:S(2)}) collective-permute-start(f32[256,128]{1,0:T(8,128)S(1)} %get-tuple-element.125), channel_id=1, source_target_pairs={{0,8},{1,3},{2,10},{3,1},{4,12},{5,7},{6,14},{7,5},{8,0},{9,11},{1... | collective-permute-start | bytes 393224 | tf_op jit(solution)/shard_map/exchange_v/ppermute | solution.py:679
  35.3 10.4 %collective-permute-start.13 = (f32[256,128]{1,0:T(8,128)S(1)}, f32[256,128]{1,0:T(8,128)S(1)}, u32[]{:S(2)}, u32[]{:S(2)}) collective-permute-start(f32[256,128]{1,0:T(8,128)S(1)} %get-tuple-element.106), channel_id=1, source_target_pairs={{0,16},{1,5},{2,18},{3,7},{4,20},{5,1},{6,22},{7,3},{8,24},{9,13},... | collective-permute-start | bytes 393224 | tf_op jit(solution)/shard_map/exchange_v/ppermute | solution.py:679
  36.8 9.3 %collective-permute-start.14 = (f32[256,128]{1,0:T(8,128)S(1)}, f32[256,128]{1,0:T(8,128)S(1)}, u32[]{:S(2)}, u32[]{:S(2)}) collective-permute-start(f32[256,128]{1,0:T(8,128)S(1)} %get-tuple-element.107), channel_id=1, source_target_pairs={{0,24},{1,7},{2,26},{3,5},{4,28},{5,3},{6,30},{7,1},{8,16},{9,15},... | collective-permute-start | bytes 393224 | tf_op jit(solution)/shard_map/exchange_v/ppermute | solution.py:679
  39.3 6.9 %collective-permute-start.15 = (f32[256,128]{1,0:T(8,128)S(1)}, f32[256,128]{1,0:T(8,128)S(1)}, u32[]{:S(2)}, u32[]{:S(2)}) collective-permute-start(f32[256,128]{1,0:T(8,128)S(1)} %get-tuple-element.108), channel_id=1, source_target_pairs={{0,8},{1,3},{2,10},{3,1},{4,12},{5,7},{6,14},{7,5},{8,0},{9,11},{1... | collective-permute-start | bytes 393224 | tf_op jit(solution)/shard_map/exchange_v/ppermute | solution.py:679
  42.1 10.7 %collective-permute-start.23 = (f32[256,128]{1,0:T(8,128)S(1)}, f32[256,128]{1,0:T(8,128)S(1)}, u32[]{:S(2)}, u32[]{:S(2)}) collective-permute-start(f32[256,128]{1,0:T(8,128)S(1)} %get-tuple-element.127), channel_id=1, source_target_pairs={{0,4},{1,17},{2,6},{3,19},{4,0},{5,21},{6,2},{7,23},{8,12},{9,25},... | collective-permute-start | bytes 393224 | tf_op jit(solution)/shard_map/exchange_u/ppermute | solution.py:679
  45.5 7.9 %collective-permute-start.24 = (f32[256,128]{1,0:T(8,128)S(1)}, f32[256,128]{1,0:T(8,128)S(1)}, u32[]{:S(2)}, u32[]{:S(2)}) collective-permute-start(f32[256,128]{1,0:T(8,128)S(1)} %get-tuple-element.128), channel_id=1, source_target_pairs={{0,6},{1,25},{2,4},{3,27},{4,2},{5,29},{6,0},{7,31},{8,14},{9,17},... | collective-permute-start | bytes 393224 | tf_op jit(solution)/shard_map/exchange_u/ppermute | solution.py:679
  45.7 7.7 %collective-permute-start.25 = (f32[256,128]{1,0:T(8,128)S(1)}, f32[256,128]{1,0:T(8,128)S(1)}, u32[]{:S(2)}, u32[]{:S(2)}) collective-permute-start(f32[256,128]{1,0:T(8,128)S(1)} %get-tuple-element.129), channel_id=1, source_target_pairs={{0,2},{1,9},{2,0},{3,11},{4,6},{5,13},{6,4},{7,15},{8,10},{9,1},{1... | collective-permute-start | bytes 393224 | tf_op jit(solution)/shard_map/exchange_u/ppermute | solution.py:679
  47.5 8.2 %collective-permute-start.16 = (f32[256,128]{1,0:T(8,128)S(1)}, f32[256,128]{1,0:T(8,128)S(1)}, u32[]{:S(2)}, u32[]{:S(2)}) collective-permute-start(f32[256,128]{1,0:T(8,128)S(1)} %get-tuple-element.114), channel_id=1, source_target_pairs={{0,4},{1,17},{2,6},{3,19},{4,0},{5,21},{6,2},{7,23},{8,12},{9,25},... | collective-permute-start | bytes 393224 | tf_op jit(solution)/shard_map/exchange_u/ppermute | solution.py:679
  51.4 6.9 %collective-permute-start.17 = (f32[256,128]{1,0:T(8,128)S(1)}, f32[256,128]{1,0:T(8,128)S(1)}, u32[]{:S(2)}, u32[]{:S(2)}) collective-permute-start(f32[256,128]{1,0:T(8,128)S(1)} %get-tuple-element.115), channel_id=1, source_target_pairs={{0,6},{1,25},{2,4},{3,27},{4,2},{5,29},{6,0},{7,31},{8,14},{9,17},... | collective-permute-start | bytes 393224 | tf_op jit(solution)/shard_map/exchange_u/ppermute | solution.py:679
  52.8 6.4 %collective-permute-start.18 = (f32[256,128]{1,0:T(8,128)S(1)}, f32[256,128]{1,0:T(8,128)S(1)}, u32[]{:S(2)}, u32[]{:S(2)}) collective-permute-start(f32[256,128]{1,0:T(8,128)S(1)} %get-tuple-element.116), channel_id=1, source_target_pairs={{0,2},{1,9},{2,0},{3,11},{4,6},{5,13},{6,4},{7,15},{8,10},{9,1},{1... | collective-permute-start | bytes 393224 | tf_op jit(solution)/shard_map/exchange_u/ppermute | solution.py:679
  53.6 5.9 %collective-permute-start.26 = (f32[256,128]{1,0:T(8,128)S(1)}, f32[256,128]{1,0:T(8,128)S(1)}, u32[]{:S(2)}, u32[]{:S(2)}) collective-permute-start(f32[256,128]{1,0:T(8,128)S(1)} %get-tuple-element.131), channel_id=1, source_target_pairs={{0,1},{1,0},{2,3},{3,2},{4,5},{5,4},{6,7},{7,6},{8,9},{9,8},{10,11... | collective-permute-start | bytes 393224 | tf_op jit(solution)/shard_map/ppermute | solution.py:666
  53.7 5.8 %collective-permute-start.27 = (f32[256,128]{1,0:T(8,128)S(1)}, f32[256,128]{1,0:T(8,128)S(1)}, u32[]{:S(2)}, u32[]{:S(2)}) collective-permute-start(f32[256,128]{1,0:T(8,128)S(1)} %get-tuple-element.132), channel_id=1, source_target_pairs={{0,1},{1,0},{2,3},{3,2},{4,5},{5,4},{6,7},{7,6},{8,9},{9,8},{10,11... | collective-permute-start | bytes 393224 | tf_op jit(solution)/shard_map/ppermute | solution.py:666
  55.7 3.8 %collective-permute-start.28 = (f32[256,128]{1,0:T(8,128)S(1)}, f32[256,128]{1,0:T(8,128)S(1)}, u32[]{:S(2)}, u32[]{:S(2)}) collective-permute-start(f32[256,128]{1,0:T(8,128)S(1)} %get-tuple-element.133), channel_id=1, source_target_pairs={{0,1},{1,0},{2,3},{3,2},{4,5},{5,4},{6,7},{7,6},{8,9},{9,8},{10,11... | collective-permute-start | bytes 393224 | tf_op jit(solution)/shard_map/ppermute | solution.py:666
  58.3 1.3 %collective-permute-start.29 = (f32[256,128]{1,0:T(8,128)S(1)}, f32[256,128]{1,0:T(8,128)S(1)}, u32[]{:S(2)}, u32[]{:S(2)}) collective-permute-start(f32[256,128]{1,0:T(8,128)S(1)} %get-tuple-element.134), channel_id=1, source_target_pairs={{0,1},{1,0},{2,3},{3,2},{4,5},{5,4},{6,7},{7,6},{8,9},{9,8},{10,11... | collective-permute-start | bytes 393224 | tf_op jit(solution)/shard_map/ppermute | solution.py:666
  60.0 1.2 %collective-permute-start.30 = (f32[8,128]{1,0:T(8,128)S(1)}, f32[8,128]{1,0:T(8,128)S(1)}, u32[]{:S(2)}, u32[]{:S(2)}) collective-permute-start(f32[8,128]{1,0:T(8,128)S(1)} %join_grads.1.refs_0_), channel_id=1, source_target_pairs={{0,1},{1,0},{2,3},{3,2},{4,5},{5,4},{6,7},{7,6},{8,9},{9,8},{10,11... | collective-permute-start | bytes 12296 | tf_op jit(solution)/shard_map/ppermute | solution.py:701
  61.2 4.5 %collective-permute-start.33 = (f32[8,128]{1,0:T(8,128)S(1)}, f32[8,128]{1,0:T(8,128)S(1)}, u32[]{:S(2)}, u32[]{:S(2)}) collective-permute-start(f32[8,128]{1,0:T(8,128)S(1)} %add_grads.3.refs_0_), channel_id=1, source_target_pairs={{0,24},{8,16},{16,8},{24,0},{1,25},{9,17},{17,9},{25,1},{2,26},{10... | collective-permute-start | bytes 12296 | tf_op jit(solution)/shard_map/ppermute | solution.py:701
  62.8 3.6 %collective-permute-start.32 = (f32[8,128]{1,0:T(8,128)S(1)}, f32[8,128]{1,0:T(8,128)S(1)}, u32[]{:S(2)}, u32[]{:S(2)}) collective-permute-start(f32[8,128]{1,0:T(8,128)S(1)} %add_grads.3.refs_0_), channel_id=1, source_target_pairs={{0,16},{8,24},{16,0},{24,8},{1,17},{9,25},{17,1},{25,9},{2,18},{10... | collective-permute-start | bytes 12296 | tf_op jit(solution)/shard_map/ppermute | solution.py:701
  63.3 3.6 %collective-permute-start.31 = (f32[8,128]{1,0:T(8,128)S(1)}, f32[8,128]{1,0:T(8,128)S(1)}, u32[]{:S(2)}, u32[]{:S(2)}) collective-permute-start(f32[8,128]{1,0:T(8,128)S(1)} %add_grads.3.refs_0_), channel_id=1, source_target_pairs={{0,8},{8,0},{16,24},{24,16},{1,9},{9,1},{17,25},{25,17},{2,10},{10... | collective-permute-start | bytes 12296 | tf_op jit(solution)/shard_map/ppermute | solution.py:701
  66.9 5.6 %collective-permute-start.36 = (f32[8,128]{1,0:T(8,128)S(1)}, f32[8,128]{1,0:T(8,128)S(1)}, u32[]{:S(2)}, u32[]{:S(2)}) collective-permute-start(f32[8,128]{1,0:T(8,128)S(1)} %add_grads.4.refs_0_), channel_id=1, source_target_pairs={{0,6},{2,4},{4,2},{6,0},{1,7},{3,5},{5,3},{7,1},{8,14},{10,12},{12... | collective-permute-start | bytes 12296 | tf_op jit(solution)/shard_map/ppermute | solution.py:701
  69.2 4.5 %collective-permute-start.35 = (f32[8,128]{1,0:T(8,128)S(1)}, f32[8,128]{1,0:T(8,128)S(1)}, u32[]{:S(2)}, u32[]{:S(2)}) collective-permute-start(f32[8,128]{1,0:T(8,128)S(1)} %add_grads.4.refs_0_), channel_id=1, source_target_pairs={{0,4},{2,6},{4,0},{6,2},{1,5},{3,7},{5,1},{7,3},{8,12},{10,14},{12... | collective-permute-start | bytes 12296 | tf_op jit(solution)/shard_map/ppermute | solution.py:701
  70.0 3.7 %collective-permute-start.34 = (f32[8,128]{1,0:T(8,128)S(1)}, f32[8,128]{1,0:T(8,128)S(1)}, u32[]{:S(2)}, u32[]{:S(2)}) collective-permute-start(f32[8,128]{1,0:T(8,128)S(1)} %add_grads.4.refs_0_), channel_id=1, source_target_pairs={{0,2},{2,0},{4,6},{6,4},{1,3},{3,1},{5,7},{7,5},{8,10},{10,8},{12,... | collective-permute-start | bytes 12296 | tf_op jit(solution)/shard_map/ppermute | solution.py:701

commit v3 on v2

--- a/solution.py
+++ b/solution.py
@@ -579,17 +579,6 @@
     )
 
 
-def flips_other(shape, other):
-    def body(*refs):
-        slots = shape.slots()
-        for start in range(0, shape.part, TILE):
-            real, imag = load_slots(shape, "other_part", refs[:-1], start, slots)
-            flips = [[flip_sum(values, i) for i in range(len(slots))] for values in (real, imag)]
-            store_slots(shape, "all", refs[-1:], start, slots, *flips)
-
-    return vmem_call("flips_other", body, [shape.whole()], inputs=tuple(other))[0]
-
-
 def post_mix(shape, angles, arrays, hold=()):
     count = len(arrays)
 
@@ -607,8 +596,8 @@
     )[0]
 
 
-def post_grads(shape, mixed, other, flips, cost_a, hold=()):
-    def body(mixed_ref, flips_ref, cost, *refs):
+def post_grads(shape, mixed, other, cost_a, early, mid_part):
+    def body(mixed_ref, cost, early_ref, mid_ref, *refs):
         others, out = refs[:-1], refs[-1]
         piece = shape.piece()
         slots = shape.slots()
@@ -617,17 +606,21 @@
         for start in range(0, shape.part, TILE):
             real, imag = load_slots(shape, "all", [mixed_ref], start, slots)
             other_re, other_im = load_slots(shape, "other_part", others, start, slots)
-            flip_re, flip_im = load_slots(shape, "all", [flips_ref], start, slots)
             for i, slot in enumerate(slots):
-                mix = mix + flip_re[i] * imag[i] - flip_im[i] * real[i]
+                mix = mix + flip_sum(other_re, i) * imag[i] - flip_sum(other_im, i) * real[i]
                 row = pl.multiple_of(piece(*slot) * shape.part + start, TILE)
                 value = cost[pl.ds(row, TILE), :]
                 inter = inter + value * (other_re[i] * imag[i] - other_im[i] * real[i])
-        out[0:1, :] = sign(jnp.sum(inter, axis=0, keepdims=True))
-        out[1:2, :] = sign(jnp.sum(mix, axis=0, keepdims=True))
+        rows = [
+            sign(jnp.sum(inter, axis=0, keepdims=True)),
+            sign(jnp.sum(mix, axis=0, keepdims=True)) + mid_ref[0:1, :],
+            mid_ref[1:2, :],
+            mid_ref[2:3, :] + early_ref[...],
+        ]
+        out[...] = jnp.concatenate(rows + [jnp.zeros((TILE - 4, LANES), F32)], axis=0)
 
     return vmem_call(
-        "post_grads", body, [((2, LANES), F32)], inputs=(mixed, flips, cost_a, *other), hold=hold
+        "post_grads", body, [((TILE, LANES), F32)], inputs=(mixed, cost_a, early, mid_part, *other)
     )[0]
 
 
@@ -680,11 +673,15 @@
     return out
 
 
-def total_grads(shape, parts, token=None):
+def join_grads(parts):
     def join(early, mid_part, late, out):
         rows = [late[0:1, :], late[1:2, :] + mid_part[0:1, :], mid_part[1:2, :], mid_part[2:3, :] + early[...]]
         out[...] = jnp.concatenate(rows + [jnp.zeros((TILE - 4, LANES), F32)], axis=0)
 
+    return vmem_call("join_grads", join, [((TILE, LANES), F32)], inputs=tuple(parts))[0]
+
+
+def total_grads(shape, block, token=None):
     def add(*refs):
         values = [ref[...] for ref in refs[:-1]]
         while len(values) > 1:
@@ -692,7 +689,6 @@
         refs[-1][...] = values[0]
 
     block_shape = [((TILE, LANES), F32)]
-    block = vmem_call("join_grads", join, block_shape, inputs=tuple(parts))[0]
     for axis, size, most in (("core", CORES, 2), ("grp", shape.groups, 4), ("z", shape.depth, 4)):
         stride = 1
         while stride < size:
@@ -855,7 +851,7 @@
     late = jnp.concatenate(
         [plain_cross(lam_mixed, plain_phase(shape, psi_mixed, field_a, True)), plain_cross(lam, flips)], axis=0
     )
-    grads = total_grads(shape, (early, mid_part, late))
+    grads = total_grads(shape, join_grads((early, mid_part, late)))
     outs = [narrow(plain_phase(shape, state, field_a, False)) for state in (psi_mixed, lam_mixed)]
     return outs[0], outs[1], grads
 
@@ -908,11 +904,10 @@
     mid_part = gradients_mid(shape, field_b, own_before, other_before)
     other = [swap_cores(array) for array in post_send(shape, angles, far, hold=(near[0], mid_part, early))]
     near = swap(shape, near, "u")
-    flips = flips_other(shape, other)
     mixed = post_mix(shape, angles, near, hold=(mid_part, early))
-    late = post_grads(shape, mixed, other, flips, field_a[0])
+    block = post_grads(shape, mixed, other, field_a[0], early, mid_part)
     psi_out, lam_out, token = post_phase(shape, mixed, other, field_a)
-    grads = total_grads(shape, (early, mid_part, late), token)
+    grads = total_grads(shape, block, token)
     return deinterleave(psi_out, rows), deinterleave(lam_out, rows), grads
 
 

time: 74.7 us -> 74.6 us (level)
    pallas_call x19 -> x17, Pallas kernels: 10.6 us -> 10.5 us  [vmem_call(): pl.pallas_call(body, name=name, out_shape=[jax.ShapeDtypeStruct(shape, ki...]
where the time goes in v3:
time: 74.6 us; the launch traced here: 74.4 us
  starting transfers between devices  43.6 us (58%)
  Pallas kernels  15.6 us (21%)
  waiting for transfers between devices  12.9 us (17%)
  local copies, waits for them, and re-layouts  1.32 us (2%)
  between operations  1.01 us (1%)
    ppermute x24, starting transfers between devices, swap(): out[i] = lax.ppermute(arrays[i], AXES, pairs)  34.1 us
    pallas_call x17, Pallas kernels, vmem_call(): pl.pallas_call(body, name=name, out_shape=[jax.ShapeDtypeStruct(shape, ki...  10.5 us
    ppermute x24, waiting for transfers between devices, swap(): out[i] = lax.ppermute(arrays[i], AXES, pairs)  8.23 us
    ppermute x7, starting transfers between devices, total_grads(): lax.ppermute(block, axis, [(j, j ^ stride * i) for j in range(size)])  8.09 us
    ppermute x7, waiting for transfers between devices, total_grads(): lax.ppermute(block, axis, [(j, j ^ stride * i) for j in range(size)])  4.5 us
    pallas_call x2, Pallas kernels, make_fields(): pl.pallas_call(body, name='make_fields', out_shape=[jax.ShapeDtypeStruct(...  3.76 us
  transfers between devices with their start and end apart: 37, of which 12 were waited for; matrix products, arithmetic and copies ran while one was open for 0% of the time, Pallas kernels for 17%

profile of v3, /device:TPU:0, one launch (start us, length us, event | category | flops | bytes accessed | tf_op | source)
XLA Modules:
  0.0 74.4 jit_solution(1981782899550599243)
XLA Ops:
  0.6 0.6 copy-done
  1.3 1.4 %pre_near.1 = (f32[1024,128]{1,0:T(8,128)S(1)}, f32[1024,128]{1,0:T(8,128)S(1)}, f32[256,128]{1,0:T(8,128)S(1)}, f32[256,128]{1,0:T(8,128)S(1)}, f32[256,128]{1,0:T(8,128)S(1)}, /*index=5*/f32[256,128]{1,0:T(8,128)S(1)}) custom-call(f32[1,4]{1,0:T(1,128)S(1)} %bitcast.25, f32[1024,128]{1,0:T(8,128)} %bitcast.45, f32[1024,128]{1,0:T(8,128)} %bitcast.46), custom_call_target="tpu_custom_call" | custom-call | tf_op jit(solution)/shard_map/pre_near/pallas_call | solution.py:424
  2.7 0.5 collective-permute-start.6
  3.2 3.7 %collective-permute-start = (f32[256,128]{1,0:T(8,128)S(1)}, f32[256,128]{1,0:T(8,128)S(1)}, u32[]{:S(2)}, u32[]{:S(2)}) collective-permute-start(f32[256,128]{1,0:T(8,128)S(1)} %get-tuple-element.71), channel_id=1, source_target_pairs={{0,4},{1,17},{2,6},{3,19},{4,0},{5,21},{6,2},{7,23},{8,12},{9,25},... | collective-permute-start | bytes 393224 | tf_op jit(solution)/shard_map/exchange_u/ppermute | solution.py:672
  6.9 1.3 %collective-permute-start.1 = (f32[256,128]{1,0:T(8,128)S(1)}, f32[256,128]{1,0:T(8,128)S(1)}, u32[]{:S(2)}, u32[]{:S(2)}) collective-permute-start(f32[256,128]{1,0:T(8,128)S(1)} %get-tuple-element.72), channel_id=1, source_target_pairs={{0,6},{1,25},{2,4},{3,27},{4,2},{5,29},{6,0},{7,31},{8,14},{9,17},... | collective-permute-start | bytes 393224 | tf_op jit(solution)/shard_map/exchange_u/ppermute | solution.py:672
  8.2 0.2 collective-permute-start.2
  8.4 0.4 make_mats.1
  8.9 0.2 copy-done.3
  9.1 0.4 copy-done.1
  9.6 0.2 pre_far.1
  9.8 2.9 %collective-permute-start.7 = (f32[256,128]{1,0:T(8,128)S(1)}, f32[256,128]{1,0:T(8,128)S(1)}, u32[]{:S(2)}, u32[]{:S(2)}) collective-permute-start(f32[256,128]{1,0:T(8,128)S(1)} %get-tuple-element.85), channel_id=1, source_target_pairs={{0,4},{1,17},{2,6},{3,19},{4,0},{5,21},{6,2},{7,23},{8,12},{9,25},... | collective-permute-start | bytes 393224 | tf_op jit(solution)/shard_map/exchange_u/ppermute | solution.py:672
  12.6 1.3 %collective-permute-start.8 = (f32[256,128]{1,0:T(8,128)S(1)}, f32[256,128]{1,0:T(8,128)S(1)}, u32[]{:S(2)}, u32[]{:S(2)}) collective-permute-start(f32[256,128]{1,0:T(8,128)S(1)} %get-tuple-element.86), channel_id=1, source_target_pairs={{0,6},{1,25},{2,4},{3,27},{4,2},{5,29},{6,0},{7,31},{8,14},{9,17},... | collective-permute-start | bytes 393224 | tf_op jit(solution)/shard_map/exchange_u/ppermute | solution.py:672
  14.0 1.9 %collective-permute-done.2.refs_3_ = f32[256,128]{1,0:T(8,128)S(1)} collective-permute-done((f32[256,128]{1,0:T(8,128)S(1)}, f32[256,128]{1,0:T(8,128)S(1)}, u32[]{:S(2)}, u32[]{:S(2)}) %collective-permute-start.2) | collective-permute-done | bytes 131104 | tf_op jit(solution)/shard_map/exchange_u/ppermute | solution.py:672
  15.9 1.3 %rotate_local.4 = (f32[256,128]{1,0:T(8,128)S(1)}, f32[256,128]{1,0:T(8,128)S(1)}, f32[256,128]{1,0:T(8,128)S(1)}, f32[256,128]{1,0:T(8,128)S(1)}) custom-call(f32[1,4]{1,0:T(1,128)S(1)} %bitcast.29, f32[256,128]{1,0:T(8,128)S(1)} %collective-permute-done.refs_1_, f32[256,128]{1,0:T(8,128)S(1)} %collective-permute-done.1.refs_2_, ...), custom_call_target="tpu_custom_call" | custom-call | tf_op jit(solution)/shard_map/rotate_local/pallas_call | solution.py:31
  17.2 1.5 %collective-permute-start.3 = (f32[256,128]{1,0:T(8,128)S(1)}, f32[256,128]{1,0:T(8,128)S(1)}, u32[]{:S(2)}, u32[]{:S(2)}) collective-permute-start(f32[256,128]{1,0:T(8,128)S(1)} %get-tuple-element.80), channel_id=1, source_target_pairs={{0,16},{1,5},{2,18},{3,7},{4,20},{5,1},{6,22},{7,3},{8,24},{9,13},... | collective-permute-start | bytes 393224 | tf_op jit(solution)/shard_map/exchange_v/ppermute | solution.py:672
  18.8 1.4 %collective-permute-start.4 = (f32[256,128]{1,0:T(8,128)S(1)}, f32[256,128]{1,0:T(8,128)S(1)}, u32[]{:S(2)}, u32[]{:S(2)}) collective-permute-start(f32[256,128]{1,0:T(8,128)S(1)} %get-tuple-element.81), channel_id=1, source_target_pairs={{0,24},{1,7},{2,26},{3,5},{4,28},{5,3},{6,30},{7,1},{8,16},{9,15},... | collective-permute-start | bytes 393224 | tf_op jit(solution)/shard_map/exchange_v/ppermute | solution.py:672
  20.2 0.6 collective-permute-start.5
  20.8 0.7 collective-permute-done.9.refs_3_
  21.4 1.4 %rotate_local.5 = (f32[256,128]{1,0:T(8,128)S(1)}, f32[256,128]{1,0:T(8,128)S(1)}, f32[256,128]{1,0:T(8,128)S(1)}, f32[256,128]{1,0:T(8,128)S(1)}) custom-call(f32[1,4]{1,0:T(1,128)S(1)} %bitcast.30, f32[256,128]{1,0:T(8,128)S(1)} %collective-permute-done.7.refs_1_, f32[256,128]{1,0:T(8,128)S(1)} %collective-permute-done.8.refs_2_, ...), custom_call_target="tpu_custom_call" | custom-call | tf_op jit(solution)/shard_map/rotate_local/pallas_call | solution.py:31
  22.8 1.5 %collective-permute-start.10 = (f32[256,128]{1,0:T(8,128)S(1)}, f32[256,128]{1,0:T(8,128)S(1)}, u32[]{:S(2)}, u32[]{:S(2)}) collective-permute-start(f32[256,128]{1,0:T(8,128)S(1)} %get-tuple-element.89), channel_id=1, source_target_pairs={{0,16},{1,5},{2,18},{3,7},{4,20},{5,1},{6,22},{7,3},{8,24},{9,13},... | collective-permute-start | bytes 393224 | tf_op jit(solution)/shard_map/exchange_v/ppermute | solution.py:672
  24.3 1.4 %collective-permute-start.11 = (f32[256,128]{1,0:T(8,128)S(1)}, f32[256,128]{1,0:T(8,128)S(1)}, u32[]{:S(2)}, u32[]{:S(2)}) collective-permute-start(f32[256,128]{1,0:T(8,128)S(1)} %get-tuple-element.90), channel_id=1, source_target_pairs={{0,24},{1,7},{2,26},{3,5},{4,28},{5,3},{6,30},{7,1},{8,16},{9,15},... | collective-permute-start | bytes 393224 | tf_op jit(solution)/shard_map/exchange_v/ppermute | solution.py:672
  25.8 0.6 collective-permute-start.12
  26.4 3.8 %make_fields.3 = (f32[512,128]{1,0:T(8,128)S(1)}, f32[512,128]{1,0:T(8,128)S(1)}, f32[512,128]{1,0:T(8,128)S(1)}, f32[1024,128]{1,0:T(8,128)S(1)}, f32[1024,128]{1,0:T(8,128)S(1)}, /*index=5*/f32[1024,128]{1,0:T(8,128)S(1)}) custom-call(f32[1,4]{1,0:T(1,128)S(1)} %bitcast.31, ...), custom_call_target="tpu_custom_call", output_to_operand_aliasing={{0}: (5, {}), {1}: (6, {}), {2}: (7, {}), {3}: (8, {}), {4}... | custom-call | tf_op jit(solution)/shard_map/make_fields/pallas_call | solution.py:205
  30.2 0.5 collective-permute-done.12.refs_7_
  30.7 0.8 %turn.1 = (f32[2048,128]{1,0:T(8,128)S(1)}, f32[256,128]{1,0:T(8,128)S(1)}, f32[256,128]{1,0:T(8,128)S(1)}, f32[256,128]{1,0:T(8,128)S(1)}, f32[256,128]{1,0:T(8...) custom-call(f32[1,4]{1,0:T(1,128)S(1)} %bitcast.32, ...), custom_call_target="tpu_custom_call" | custom-call | tf_op jit(solution)/shard_map/turn/pallas_call | solution.py:31
  31.5 0.3 collective-permute-start.19
  31.8 1.6 %collective-permute-start.20 = (f32[256,128]{1,0:T(8,128)S(1)}, f32[256,128]{1,0:T(8,128)S(1)}, u32[]{:S(2)}, u32[]{:S(2)}) collective-permute-start(f32[256,128]{1,0:T(8,128)S(1)} %get-tuple-element.123), channel_id=1, source_target_pairs={{0,16},{1,5},{2,18},{3,7},{4,20},{5,1},{6,22},{7,3},{8,24},{9,13},... | collective-permute-start | bytes 393224 | tf_op jit(solution)/shard_map/exchange_v/ppermute | solution.py:672
  33.3 1.4 %collective-permute-start.21 = (f32[256,128]{1,0:T(8,128)S(1)}, f32[256,128]{1,0:T(8,128)S(1)}, u32[]{:S(2)}, u32[]{:S(2)}) collective-permute-start(f32[256,128]{1,0:T(8,128)S(1)} %get-tuple-element.124), channel_id=1, source_target_pairs={{0,24},{1,7},{2,26},{3,5},{4,28},{5,3},{6,30},{7,1},{8,16},{9,15},... | collective-permute-start | bytes 393224 | tf_op jit(solution)/shard_map/exchange_v/ppermute | solution.py:672
  34.8 0.5 collective-permute-start.22
  35.3 1.6 %collective-permute-start.13 = (f32[256,128]{1,0:T(8,128)S(1)}, f32[256,128]{1,0:T(8,128)S(1)}, u32[]{:S(2)}, u32[]{:S(2)}) collective-permute-start(f32[256,128]{1,0:T(8,128)S(1)} %get-tuple-element.106), channel_id=1, source_target_pairs={{0,16},{1,5},{2,18},{3,7},{4,20},{5,1},{6,22},{7,3},{8,24},{9,13},... | collective-permute-start | bytes 393224 | tf_op jit(solution)/shard_map/exchange_v/ppermute | solution.py:672
  36.8 2.4 %collective-permute-start.14 = (f32[256,128]{1,0:T(8,128)S(1)}, f32[256,128]{1,0:T(8,128)S(1)}, u32[]{:S(2)}, u32[]{:S(2)}) collective-permute-start(f32[256,128]{1,0:T(8,128)S(1)} %get-tuple-element.107), channel_id=1, source_target_pairs={{0,24},{1,7},{2,26},{3,5},{4,28},{5,3},{6,30},{7,1},{8,16},{9,15},... | collective-permute-start | bytes 393224 | tf_op jit(solution)/shard_map/exchange_v/ppermute | solution.py:672
  39.3 1.5 %collective-permute-start.15 = (f32[256,128]{1,0:T(8,128)S(1)}, f32[256,128]{1,0:T(8,128)S(1)}, u32[]{:S(2)}, u32[]{:S(2)}) collective-permute-start(f32[256,128]{1,0:T(8,128)S(1)} %get-tuple-element.108), channel_id=1, source_target_pairs={{0,8},{1,3},{2,10},{3,1},{4,12},{5,7},{6,14},{7,5},{8,0},{9,11},{1... | collective-permute-start | bytes 393224 | tf_op jit(solution)/shard_map/exchange_v/ppermute | solution.py:672
  40.7 1.4 %rotate_local.7 = (f32[256,128]{1,0:T(8,128)S(1)}, f32[256,128]{1,0:T(8,128)S(1)}, f32[256,128]{1,0:T(8,128)S(1)}, f32[256,128]{1,0:T(8,128)S(1)}) custom-call(f32[1,4]{1,0:T(1,128)S(1)} %bitcast.33, f32[256,128]{1,0:T(8,128)S(1)} %collective-permute-done.20.refs_1_, f32[256,128]{1,0:T(8,128)S(1)} %collective-permute-done.21.refs_2_, ...), custom_call_target="tpu_custom_call" | custom-call | tf_op jit(solution)/shard_map/rotate_local/pallas_call | solution.py:31
  42.1 3.4 %collective-permute-start.23 = (f32[256,128]{1,0:T(8,128)S(1)}, f32[256,128]{1,0:T(8,128)S(1)}, u32[]{:S(2)}, u32[]{:S(2)}) collective-permute-start(f32[256,128]{1,0:T(8,128)S(1)} %get-tuple-element.127), channel_id=1, source_target_pairs={{0,4},{1,17},{2,6},{3,19},{4,0},{5,21},{6,2},{7,23},{8,12},{9,25},... | collective-permute-start | bytes 393224 | tf_op jit(solution)/shard_map/exchange_u/ppermute | solution.py:672
  45.5 0.1 collective-permute-start.24
  45.7 0.5 collective-permute-start.25
  46.2 1.3 %rotate_local.6 = (f32[256,128]{1,0:T(8,128)S(1)}, f32[256,128]{1,0:T(8,128)S(1)}, f32[256,128]{1,0:T(8,128)S(1)}, f32[256,128]{1,0:T(8,128)S(1)}) custom-call(f32[1,4]{1,0:T(1,128)S(1)} %bitcast.34, f32[256,128]{1,0:T(8,128)S(1)} %collective-permute-done.13.refs_1_, f32[256,128]{1,0:T(8,128)S(1)} %collective-permute-done.14.refs_2_, ...), custom_call_target="tpu_custom_call" | custom-call | tf_op jit(solution)/shard_map/rotate_local/pallas_call | solution.py:31
  47.5 3.8 %collective-permute-start.16 = (f32[256,128]{1,0:T(8,128)S(1)}, f32[256,128]{1,0:T(8,128)S(1)}, u32[]{:S(2)}, u32[]{:S(2)}) collective-permute-start(f32[256,128]{1,0:T(8,128)S(1)} %get-tuple-element.114), channel_id=1, source_target_pairs={{0,4},{1,17},{2,6},{3,19},{4,0},{5,21},{6,2},{7,23},{8,12},{9,25},... | collective-permute-start | bytes 393224 | tf_op jit(solution)/shard_map/exchange_u/ppermute | solution.py:672
  51.4 0.1 collective-permute-start.17
  51.5 0.1 flip_raw.1.refs_6_.refs_7_.early_ref
  51.6 1.2 %gradients_mid.1.refs_5_.refs_6_.mid_ref = f32[3,128]{1,0:T(4,128)S(1)} custom-call(f32[1024,128]{1,0:T(8,128)S(1)} %get-tuple-element.118.cost, f32[1024,128]{1,0:T(8,128)S(1)} %get-tuple-element.104.refs_9_.cos_b, f32[1024,128]{1,0:T(8,128)S(1)} %get-tuple-element.105.refs_10_.sin_b, f32[2048,128]{1,0:T(8,128)S(1)} %get-tuple-element.119.own_ref, ...), custom_call_target="tpu_custom_call" | custom-call | tf_op jit(solution)/shard_map/gradients_mid/pallas_call | solution.py:31
  52.8 0.6 collective-permute-start.18
  53.4 0.2 post_send.1
  53.7 0.5 collective-permute-start.27
  54.2 1.5 %collective-permute-done.16.refs_1_ = f32[256,128]{1,0:T(8,128)S(1)} collective-permute-done((f32[256,128]{1,0:T(8,128)S(1)}, f32[256,128]{1,0:T(8,128)S(1)}, u32[]{:S(2)}, u32[]{:S(2)}) %collective-permute-start.16) | collective-permute-done | bytes 131104 | tf_op jit(solution)/shard_map/exchange_u/ppermute | solution.py:672
  55.7 2.6 %collective-permute-done.17.refs_2_ = f32[256,128]{1,0:T(8,128)S(1)} collective-permute-done((f32[256,128]{1,0:T(8,128)S(1)}, f32[256,128]{1,0:T(8,128)S(1)}, u32[]{:S(2)}, u32[]{:S(2)}) %collective-permute-start.17) | collective-permute-done | bytes 131104 | tf_op jit(solution)/shard_map/exchange_u/ppermute | solution.py:672
  58.3 1.0 %collective-permute-done.18.refs_3_ = f32[256,128]{1,0:T(8,128)S(1)} collective-permute-done((f32[256,128]{1,0:T(8,128)S(1)}, f32[256,128]{1,0:T(8,128)S(1)}, u32[]{:S(2)}, u32[]{:S(2)}) %collective-permute-start.18) | collective-permute-done | bytes 131104 | tf_op jit(solution)/shard_map/exchange_u/ppermute | solution.py:672
  59.3 0.2 post_mix.1.own_ref.mixed_ref
  59.5 0.1 collective-permute-done.29.refs_3_
  59.6 0.2 post_grads.1.refs_0_
  59.8 0.2 collective-permute-start.30
  60.0 1.0 %collective-permute-done.30.refs_1_ = f32[8,128]{1,0:T(8,128)S(1)} collective-permute-done((f32[8,128]{1,0:T(8,128)S(1)}, f32[8,128]{1,0:T(8,128)S(1)}, u32[]{:S(2)}, u32[]{:S(2)}) %collective-permute-start.30) | collective-permute-done | bytes 4128 | tf_op jit(solution)/shard_map/ppermute | solution.py:697
  61.1 1.6 %collective-permute-start.33 = (f32[8,128]{1,0:T(8,128)S(1)}, f32[8,128]{1,0:T(8,128)S(1)}, u32[]{:S(2)}, u32[]{:S(2)}) collective-permute-start(f32[8,128]{1,0:T(8,128)S(1)} %add_grads.3.refs_0_), channel_id=1, source_target_pairs={{0,24},{8,16},{16,8},{24,0},{1,25},{9,17},{17,9},{25,1},{2,26},{10... | collective-permute-start | bytes 12296 | tf_op jit(solution)/shard_map/ppermute | solution.py:697
  62.6 0.5 collective-permute-start.32
  63.1 1.4 %collective-permute-start.31 = (f32[8,128]{1,0:T(8,128)S(1)}, f32[8,128]{1,0:T(8,128)S(1)}, u32[]{:S(2)}, u32[]{:S(2)}) collective-permute-start(f32[8,128]{1,0:T(8,128)S(1)} %add_grads.3.refs_0_), channel_id=1, source_target_pairs={{0,8},{8,0},{16,24},{24,16},{1,9},{9,1},{17,25},{25,17},{2,10},{10... | collective-permute-start | bytes 12296 | tf_op jit(solution)/shard_map/ppermute | solution.py:697
  64.5 1.0 %collective-permute-done.33.refs_3_ = f32[8,128]{1,0:T(8,128)S(1)} collective-permute-done((f32[8,128]{1,0:T(8,128)S(1)}, f32[8,128]{1,0:T(8,128)S(1)}, u32[]{:S(2)}, u32[]{:S(2)}) %collective-permute-start.33) | collective-permute-done | bytes 4128 | tf_op jit(solution)/shard_map/ppermute | solution.py:697
  65.6 0.7 collective-permute-done.32.refs_2_
  66.2 0.5 collective-permute-done.31.refs_1_
  66.8 2.3 %collective-permute-start.36 = (f32[8,128]{1,0:T(8,128)S(1)}, f32[8,128]{1,0:T(8,128)S(1)}, u32[]{:S(2)}, u32[]{:S(2)}) collective-permute-start(f32[8,128]{1,0:T(8,128)S(1)} %add_grads.4.refs_0_), channel_id=1, source_target_pairs={{0,6},{2,4},{4,2},{6,0},{1,7},{3,5},{5,3},{7,1},{8,14},{10,12},{12... | collective-permute-start | bytes 12296 | tf_op jit(solution)/shard_map/ppermute | solution.py:697
  69.1 0.8 %collective-permute-start.35 = (f32[8,128]{1,0:T(8,128)S(1)}, f32[8,128]{1,0:T(8,128)S(1)}, u32[]{:S(2)}, u32[]{:S(2)}) collective-permute-start(f32[8,128]{1,0:T(8,128)S(1)} %add_grads.4.refs_0_), channel_id=1, source_target_pairs={{0,4},{2,6},{4,0},{6,2},{1,5},{3,7},{5,1},{7,3},{8,12},{10,14},{12... | collective-permute-start | bytes 12296 | tf_op jit(solution)/shard_map/ppermute | solution.py:697
  69.9 1.3 %collective-permute-start.34 = (f32[8,128]{1,0:T(8,128)S(1)}, f32[8,128]{1,0:T(8,128)S(1)}, u32[]{:S(2)}, u32[]{:S(2)}) collective-permute-start(f32[8,128]{1,0:T(8,128)S(1)} %add_grads.4.refs_0_), channel_id=1, source_target_pairs={{0,2},{2,0},{4,6},{6,4},{1,3},{3,1},{5,7},{7,5},{8,10},{10,8},{12,... | collective-permute-start | bytes 12296 | tf_op jit(solution)/shard_map/ppermute | solution.py:697
  71.1 1.2 %post_phase.1 = (f32[1024,128]{1,0:T(8,128)}, f32[1024,128]{1,0:T(8,128)}, f32[8,128]{1,0:T(8,128)S(1)}) custom-call(f32[1024,128]{1,0:T(8,128)S(1)} %post_mix.1.own_ref.mixed_ref, f32[512,128]{1,0:T(8,128)S(1)} %get-tuple-element.121.cos_a, f32[512,128]{1,0:T(8,128)S(1)} %get-tuple-element.122.sin_a, f32[256,128]{1,0:T(8,128)S(1)} %collective-permute-done.26.refs_0_, ...), custom_call_target="tpu_custom_call" | custom-call | tf_op jit(solution)/shard_map/post_phase/pallas_call | solution.py:31
  72.3 1.3 %collective-permute-done.35.refs_2_ = f32[8,128]{1,0:T(8,128)S(1)} collective-permute-done((f32[8,128]{1,0:T(8,128)S(1)}, f32[8,128]{1,0:T(8,128)S(1)}, u32[]{:S(2)}, u32[]{:S(2)}) %collective-permute-start.35) | collective-permute-done | bytes 4128 | tf_op jit(solution)/shard_map/ppermute | solution.py:697
  73.6 0.6 finish_grads.1
  (40 shorter events, 0.2 us)
Async XLA Ops:
  0.6 0.7 copy-start
  2.7 6.9 %collective-permute-start.6 = (f32[1024,128]{1,0:T(8,128)S(1)}, f32[1024,128]{1,0:T(8,128)S(1)}, u32[]{:S(2)}, u32[]{:S(2)}) collective-permute-start(f32[1024,128]{1,0:T(8,128)S(1)} %get-tuple-element.84.refs_1_), channel_id=1, source_target_pairs={{0,1},{1,0},{2,3},{3,2},{4,5},{5,4},{6,7},{7,6},{8,9},{9,8},{10,11... | collective-permute-start | bytes 1572872 | tf_op jit(solution)/shard_map/ppermute | solution.py:659
  3.2 10.8 %collective-permute-start = (f32[256,128]{1,0:T(8,128)S(1)}, f32[256,128]{1,0:T(8,128)S(1)}, u32[]{:S(2)}, u32[]{:S(2)}) collective-permute-start(f32[256,128]{1,0:T(8,128)S(1)} %get-tuple-element.71), channel_id=1, source_target_pairs={{0,4},{1,17},{2,6},{3,19},{4,0},{5,21},{6,2},{7,23},{8,12},{9,25},... | collective-permute-start | bytes 393224 | tf_op jit(solution)/shard_map/exchange_u/ppermute | solution.py:672
  6.9 7.1 %collective-permute-start.1 = (f32[256,128]{1,0:T(8,128)S(1)}, f32[256,128]{1,0:T(8,128)S(1)}, u32[]{:S(2)}, u32[]{:S(2)}) collective-permute-start(f32[256,128]{1,0:T(8,128)S(1)} %get-tuple-element.72), channel_id=1, source_target_pairs={{0,6},{1,25},{2,4},{3,27},{4,2},{5,29},{6,0},{7,31},{8,14},{9,17},... | collective-permute-start | bytes 393224 | tf_op jit(solution)/shard_map/exchange_u/ppermute | solution.py:672
  8.2 7.7 %collective-permute-start.2 = (f32[256,128]{1,0:T(8,128)S(1)}, f32[256,128]{1,0:T(8,128)S(1)}, u32[]{:S(2)}, u32[]{:S(2)}) collective-permute-start(f32[256,128]{1,0:T(8,128)S(1)} %get-tuple-element.73), channel_id=1, source_target_pairs={{0,2},{1,9},{2,0},{3,11},{4,6},{5,13},{6,4},{7,15},{8,10},{9,1},{1... | collective-permute-start | bytes 393224 | tf_op jit(solution)/shard_map/exchange_u/ppermute | solution.py:672
  8.4 0.7 copy-start.3
  8.4 0.7 copy-start.4
  8.9 0.7 copy-start.1
  8.9 0.7 copy-start.2
  9.8 10.4 %collective-permute-start.7 = (f32[256,128]{1,0:T(8,128)S(1)}, f32[256,128]{1,0:T(8,128)S(1)}, u32[]{:S(2)}, u32[]{:S(2)}) collective-permute-start(f32[256,128]{1,0:T(8,128)S(1)} %get-tuple-element.85), channel_id=1, source_target_pairs={{0,4},{1,17},{2,6},{3,19},{4,0},{5,21},{6,2},{7,23},{8,12},{9,25},... | collective-permute-start | bytes 393224 | tf_op jit(solution)/shard_map/exchange_u/ppermute | solution.py:672
  12.6 8.1 %collective-permute-start.8 = (f32[256,128]{1,0:T(8,128)S(1)}, f32[256,128]{1,0:T(8,128)S(1)}, u32[]{:S(2)}, u32[]{:S(2)}) collective-permute-start(f32[256,128]{1,0:T(8,128)S(1)} %get-tuple-element.86), channel_id=1, source_target_pairs={{0,6},{1,25},{2,4},{3,27},{4,2},{5,29},{6,0},{7,31},{8,14},{9,17},... | collective-permute-start | bytes 393224 | tf_op jit(solution)/shard_map/exchange_u/ppermute | solution.py:672
  14.0 7.4 %collective-permute-start.9 = (f32[256,128]{1,0:T(8,128)S(1)}, f32[256,128]{1,0:T(8,128)S(1)}, u32[]{:S(2)}, u32[]{:S(2)}) collective-permute-start(f32[256,128]{1,0:T(8,128)S(1)} %get-tuple-element.87), channel_id=1, source_target_pairs={{0,2},{1,9},{2,0},{3,11},{4,6},{5,13},{6,4},{7,15},{8,10},{9,1},{1... | collective-permute-start | bytes 393224 | tf_op jit(solution)/shard_map/exchange_u/ppermute | solution.py:672
  17.2 8.5 %collective-permute-start.3 = (f32[256,128]{1,0:T(8,128)S(1)}, f32[256,128]{1,0:T(8,128)S(1)}, u32[]{:S(2)}, u32[]{:S(2)}) collective-permute-start(f32[256,128]{1,0:T(8,128)S(1)} %get-tuple-element.80), channel_id=1, source_target_pairs={{0,16},{1,5},{2,18},{3,7},{4,20},{5,1},{6,22},{7,3},{8,24},{9,13},... | collective-permute-start | bytes 393224 | tf_op jit(solution)/shard_map/exchange_v/ppermute | solution.py:672
  18.8 11.4 %collective-permute-start.4 = (f32[256,128]{1,0:T(8,128)S(1)}, f32[256,128]{1,0:T(8,128)S(1)}, u32[]{:S(2)}, u32[]{:S(2)}) collective-permute-start(f32[256,128]{1,0:T(8,128)S(1)} %get-tuple-element.81), channel_id=1, source_target_pairs={{0,24},{1,7},{2,26},{3,5},{4,28},{5,3},{6,30},{7,1},{8,16},{9,15},... | collective-permute-start | bytes 393224 | tf_op jit(solution)/shard_map/exchange_v/ppermute | solution.py:672
  20.2 9.9 %collective-permute-start.5 = (f32[256,128]{1,0:T(8,128)S(1)}, f32[256,128]{1,0:T(8,128)S(1)}, u32[]{:S(2)}, u32[]{:S(2)}) collective-permute-start(f32[256,128]{1,0:T(8,128)S(1)} %get-tuple-element.82), channel_id=1, source_target_pairs={{0,8},{1,3},{2,10},{3,1},{4,12},{5,7},{6,14},{7,5},{8,0},{9,11},{1... | collective-permute-start | bytes 393224 | tf_op jit(solution)/shard_map/exchange_v/ppermute | solution.py:672
  22.8 7.4 %collective-permute-start.10 = (f32[256,128]{1,0:T(8,128)S(1)}, f32[256,128]{1,0:T(8,128)S(1)}, u32[]{:S(2)}, u32[]{:S(2)}) collective-permute-start(f32[256,128]{1,0:T(8,128)S(1)} %get-tuple-element.89), channel_id=1, source_target_pairs={{0,16},{1,5},{2,18},{3,7},{4,20},{5,1},{6,22},{7,3},{8,24},{9,13},... | collective-permute-start | bytes 393224 | tf_op jit(solution)/shard_map/exchange_v/ppermute | solution.py:672
  24.3 5.9 %collective-permute-start.11 = (f32[256,128]{1,0:T(8,128)S(1)}, f32[256,128]{1,0:T(8,128)S(1)}, u32[]{:S(2)}, u32[]{:S(2)}) collective-permute-start(f32[256,128]{1,0:T(8,128)S(1)} %get-tuple-element.90), channel_id=1, source_target_pairs={{0,24},{1,7},{2,26},{3,5},{4,28},{5,3},{6,30},{7,1},{8,16},{9,15},... | collective-permute-start | bytes 393224 | tf_op jit(solution)/shard_map/exchange_v/ppermute | solution.py:672
  25.8 5.0 %collective-permute-start.12 = (f32[256,128]{1,0:T(8,128)S(1)}, f32[256,128]{1,0:T(8,128)S(1)}, u32[]{:S(2)}, u32[]{:S(2)}) collective-permute-start(f32[256,128]{1,0:T(8,128)S(1)} %get-tuple-element.91), channel_id=1, source_target_pairs={{0,8},{1,3},{2,10},{3,1},{4,12},{5,7},{6,14},{7,5},{8,0},{9,11},{1... | collective-permute-start | bytes 393224 | tf_op jit(solution)/shard_map/exchange_v/ppermute | solution.py:672
  31.5 9.2 %collective-permute-start.19 = (f32[2048,128]{1,0:T(8,128)S(1)}, f32[2048,128]{1,0:T(8,128)S(1)}, u32[]{:S(2)}, u32[]{:S(2)}) collective-permute-start(f32[2048,128]{1,0:T(8,128)S(1)} %get-tuple-element.119.own_ref), channel_id=1, source_target_pairs={{0,1},{1,0},{2,3},{3,2},{4,5},{5,4},{6,7},{7,6},{8,9},{9,8},{10,11... | collective-permute-start | bytes 3145736 | tf_op jit(solution)/shard_map/ppermute | solution.py:659
  31.8 5.1 %collective-permute-start.20 = (f32[256,128]{1,0:T(8,128)S(1)}, f32[256,128]{1,0:T(8,128)S(1)}, u32[]{:S(2)}, u32[]{:S(2)}) collective-permute-start(f32[256,128]{1,0:T(8,128)S(1)} %get-tuple-element.123), channel_id=1, source_target_pairs={{0,16},{1,5},{2,18},{3,7},{4,20},{5,1},{6,22},{7,3},{8,24},{9,13},... | collective-permute-start | bytes 393224 | tf_op jit(solution)/shard_map/exchange_v/ppermute | solution.py:672
  33.3 5.9 %collective-permute-start.21 = (f32[256,128]{1,0:T(8,128)S(1)}, f32[256,128]{1,0:T(8,128)S(1)}, u32[]{:S(2)}, u32[]{:S(2)}) collective-permute-start(f32[256,128]{1,0:T(8,128)S(1)} %get-tuple-element.124), channel_id=1, source_target_pairs={{0,24},{1,7},{2,26},{3,5},{4,28},{5,3},{6,30},{7,1},{8,16},{9,15},... | collective-permute-start | bytes 393224 | tf_op jit(solution)/shard_map/exchange_v/ppermute | solution.py:672
  34.8 6.0 %collective-permute-start.22 = (f32[256,128]{1,0:T(8,128)S(1)}, f32[256,128]{1,0:T(8,128)S(1)}, u32[]{:S(2)}, u32[]{:S(2)}) collective-permute-start(f32[256,128]{1,0:T(8,128)S(1)} %get-tuple-element.125), channel_id=1, source_target_pairs={{0,8},{1,3},{2,10},{3,1},{4,12},{5,7},{6,14},{7,5},{8,0},{9,11},{1... | collective-permute-start | bytes 393224 | tf_op jit(solution)/shard_map/exchange_v/ppermute | solution.py:672
  35.3 10.4 %collective-permute-start.13 = (f32[256,128]{1,0:T(8,128)S(1)}, f32[256,128]{1,0:T(8,128)S(1)}, u32[]{:S(2)}, u32[]{:S(2)}) collective-permute-start(f32[256,128]{1,0:T(8,128)S(1)} %get-tuple-element.106), channel_id=1, source_target_pairs={{0,16},{1,5},{2,18},{3,7},{4,20},{5,1},{6,22},{7,3},{8,24},{9,13},... | collective-permute-start | bytes 393224 | tf_op jit(solution)/shard_map/exchange_v/ppermute | solution.py:672
  36.8 9.3 %collective-permute-start.14 = (f32[256,128]{1,0:T(8,128)S(1)}, f32[256,128]{1,0:T(8,128)S(1)}, u32[]{:S(2)}, u32[]{:S(2)}) collective-permute-start(f32[256,128]{1,0:T(8,128)S(1)} %get-tuple-element.107), channel_id=1, source_target_pairs={{0,24},{1,7},{2,26},{3,5},{4,28},{5,3},{6,30},{7,1},{8,16},{9,15},... | collective-permute-start | bytes 393224 | tf_op jit(solution)/shard_map/exchange_v/ppermute | solution.py:672
  39.3 6.9 %collective-permute-start.15 = (f32[256,128]{1,0:T(8,128)S(1)}, f32[256,128]{1,0:T(8,128)S(1)}, u32[]{:S(2)}, u32[]{:S(2)}) collective-permute-start(f32[256,128]{1,0:T(8,128)S(1)} %get-tuple-element.108), channel_id=1, source_target_pairs={{0,8},{1,3},{2,10},{3,1},{4,12},{5,7},{6,14},{7,5},{8,0},{9,11},{1... | collective-permute-start | bytes 393224 | tf_op jit(solution)/shard_map/exchange_v/ppermute | solution.py:672
  42.1 10.7 %collective-permute-start.23 = (f32[256,128]{1,0:T(8,128)S(1)}, f32[256,128]{1,0:T(8,128)S(1)}, u32[]{:S(2)}, u32[]{:S(2)}) collective-permute-start(f32[256,128]{1,0:T(8,128)S(1)} %get-tuple-element.127), channel_id=1, source_target_pairs={{0,4},{1,17},{2,6},{3,19},{4,0},{5,21},{6,2},{7,23},{8,12},{9,25},... | collective-permute-start | bytes 393224 | tf_op jit(solution)/shard_map/exchange_u/ppermute | solution.py:672
  45.5 7.9 %collective-permute-start.24 = (f32[256,128]{1,0:T(8,128)S(1)}, f32[256,128]{1,0:T(8,128)S(1)}, u32[]{:S(2)}, u32[]{:S(2)}) collective-permute-start(f32[256,128]{1,0:T(8,128)S(1)} %get-tuple-element.128), channel_id=1, source_target_pairs={{0,6},{1,25},{2,4},{3,27},{4,2},{5,29},{6,0},{7,31},{8,14},{9,17},... | collective-permute-start | bytes 393224 | tf_op jit(solution)/shard_map/exchange_u/ppermute | solution.py:672
  45.7 7.7 %collective-permute-start.25 = (f32[256,128]{1,0:T(8,128)S(1)}, f32[256,128]{1,0:T(8,128)S(1)}, u32[]{:S(2)}, u32[]{:S(2)}) collective-permute-start(f32[256,128]{1,0:T(8,128)S(1)} %get-tuple-element.129), channel_id=1, source_target_pairs={{0,2},{1,9},{2,0},{3,11},{4,6},{5,13},{6,4},{7,15},{8,10},{9,1},{1... | collective-permute-start | bytes 393224 | tf_op jit(solution)/shard_map/exchange_u/ppermute | solution.py:672
  47.5 8.2 %collective-permute-start.16 = (f32[256,128]{1,0:T(8,128)S(1)}, f32[256,128]{1,0:T(8,128)S(1)}, u32[]{:S(2)}, u32[]{:S(2)}) collective-permute-start(f32[256,128]{1,0:T(8,128)S(1)} %get-tuple-element.114), channel_id=1, source_target_pairs={{0,4},{1,17},{2,6},{3,19},{4,0},{5,21},{6,2},{7,23},{8,12},{9,25},... | collective-permute-start | bytes 393224 | tf_op jit(solution)/shard_map/exchange_u/ppermute | solution.py:672
  51.4 6.9 %collective-permute-start.17 = (f32[256,128]{1,0:T(8,128)S(1)}, f32[256,128]{1,0:T(8,128)S(1)}, u32[]{:S(2)}, u32[]{:S(2)}) collective-permute-start(f32[256,128]{1,0:T(8,128)S(1)} %get-tuple-element.115), channel_id=1, source_target_pairs={{0,6},{1,25},{2,4},{3,27},{4,2},{5,29},{6,0},{7,31},{8,14},{9,17},... | collective-permute-start | bytes 393224 | tf_op jit(solution)/shard_map/exchange_u/ppermute | solution.py:672
  52.8 6.4 %collective-permute-start.18 = (f32[256,128]{1,0:T(8,128)S(1)}, f32[256,128]{1,0:T(8,128)S(1)}, u32[]{:S(2)}, u32[]{:S(2)}) collective-permute-start(f32[256,128]{1,0:T(8,128)S(1)} %get-tuple-element.116), channel_id=1, source_target_pairs={{0,2},{1,9},{2,0},{3,11},{4,6},{5,13},{6,4},{7,15},{8,10},{9,1},{1... | collective-permute-start | bytes 393224 | tf_op jit(solution)/shard_map/exchange_u/ppermute | solution.py:672
  53.6 5.9 %collective-permute-start.26 = (f32[256,128]{1,0:T(8,128)S(1)}, f32[256,128]{1,0:T(8,128)S(1)}, u32[]{:S(2)}, u32[]{:S(2)}) collective-permute-start(f32[256,128]{1,0:T(8,128)S(1)} %get-tuple-element.131), channel_id=1, source_target_pairs={{0,1},{1,0},{2,3},{3,2},{4,5},{5,4},{6,7},{7,6},{8,9},{9,8},{10,11... | collective-permute-start | bytes 393224 | tf_op jit(solution)/shard_map/ppermute | solution.py:659
  53.7 5.8 %collective-permute-start.27 = (f32[256,128]{1,0:T(8,128)S(1)}, f32[256,128]{1,0:T(8,128)S(1)}, u32[]{:S(2)}, u32[]{:S(2)}) collective-permute-start(f32[256,128]{1,0:T(8,128)S(1)} %get-tuple-element.132), channel_id=1, source_target_pairs={{0,1},{1,0},{2,3},{3,2},{4,5},{5,4},{6,7},{7,6},{8,9},{9,8},{10,11... | collective-permute-start | bytes 393224 | tf_op jit(solution)/shard_map/ppermute | solution.py:659
  55.7 3.8 %collective-permute-start.28 = (f32[256,128]{1,0:T(8,128)S(1)}, f32[256,128]{1,0:T(8,128)S(1)}, u32[]{:S(2)}, u32[]{:S(2)}) collective-permute-start(f32[256,128]{1,0:T(8,128)S(1)} %get-tuple-element.133), channel_id=1, source_target_pairs={{0,1},{1,0},{2,3},{3,2},{4,5},{5,4},{6,7},{7,6},{8,9},{9,8},{10,11... | collective-permute-start | bytes 393224 | tf_op jit(solution)/shard_map/ppermute | solution.py:659
  58.3 1.3 %collective-permute-start.29 = (f32[256,128]{1,0:T(8,128)S(1)}, f32[256,128]{1,0:T(8,128)S(1)}, u32[]{:S(2)}, u32[]{:S(2)}) collective-permute-start(f32[256,128]{1,0:T(8,128)S(1)} %get-tuple-element.134), channel_id=1, source_target_pairs={{0,1},{1,0},{2,3},{3,2},{4,5},{5,4},{6,7},{7,6},{8,9},{9,8},{10,11... | collective-permute-start | bytes 393224 | tf_op jit(solution)/shard_map/ppermute | solution.py:659
  59.8 1.2 %collective-permute-start.30 = (f32[8,128]{1,0:T(8,128)S(1)}, f32[8,128]{1,0:T(8,128)S(1)}, u32[]{:S(2)}, u32[]{:S(2)}) collective-permute-start(f32[8,128]{1,0:T(8,128)S(1)} %post_grads.1.refs_0_), channel_id=1, source_target_pairs={{0,1},{1,0},{2,3},{3,2},{4,5},{5,4},{6,7},{7,6},{8,9},{9,8},{10,11... | collective-permute-start | bytes 12296 | tf_op jit(solution)/shard_map/ppermute | solution.py:697
  61.1 4.5 %collective-permute-start.33 = (f32[8,128]{1,0:T(8,128)S(1)}, f32[8,128]{1,0:T(8,128)S(1)}, u32[]{:S(2)}, u32[]{:S(2)}) collective-permute-start(f32[8,128]{1,0:T(8,128)S(1)} %add_grads.3.refs_0_), channel_id=1, source_target_pairs={{0,24},{8,16},{16,8},{24,0},{1,25},{9,17},{17,9},{25,1},{2,26},{10... | collective-permute-start | bytes 12296 | tf_op jit(solution)/shard_map/ppermute | solution.py:697
  62.6 3.6 %collective-permute-start.32 = (f32[8,128]{1,0:T(8,128)S(1)}, f32[8,128]{1,0:T(8,128)S(1)}, u32[]{:S(2)}, u32[]{:S(2)}) collective-permute-start(f32[8,128]{1,0:T(8,128)S(1)} %add_grads.3.refs_0_), channel_id=1, source_target_pairs={{0,16},{8,24},{16,0},{24,8},{1,17},{9,25},{17,1},{25,9},{2,18},{10... | collective-permute-start | bytes 12296 | tf_op jit(solution)/shard_map/ppermute | solution.py:697
  63.1 3.6 %collective-permute-start.31 = (f32[8,128]{1,0:T(8,128)S(1)}, f32[8,128]{1,0:T(8,128)S(1)}, u32[]{:S(2)}, u32[]{:S(2)}) collective-permute-start(f32[8,128]{1,0:T(8,128)S(1)} %add_grads.3.refs_0_), channel_id=1, source_target_pairs={{0,8},{8,0},{16,24},{24,16},{1,9},{9,1},{17,25},{25,17},{2,10},{10... | collective-permute-start | bytes 12296 | tf_op jit(solution)/shard_map/ppermute | solution.py:697
  66.8 5.6 %collective-permute-start.36 = (f32[8,128]{1,0:T(8,128)S(1)}, f32[8,128]{1,0:T(8,128)S(1)}, u32[]{:S(2)}, u32[]{:S(2)}) collective-permute-start(f32[8,128]{1,0:T(8,128)S(1)} %add_grads.4.refs_0_), channel_id=1, source_target_pairs={{0,6},{2,4},{4,2},{6,0},{1,7},{3,5},{5,3},{7,1},{8,14},{10,12},{12... | collective-permute-start | bytes 12296 | tf_op jit(solution)/shard_map/ppermute | solution.py:697
  69.1 4.5 %collective-permute-start.35 = (f32[8,128]{1,0:T(8,128)S(1)}, f32[8,128]{1,0:T(8,128)S(1)}, u32[]{:S(2)}, u32[]{:S(2)}) collective-permute-start(f32[8,128]{1,0:T(8,128)S(1)} %add_grads.4.refs_0_), channel_id=1, source_target_pairs={{0,4},{2,6},{4,0},{6,2},{1,5},{3,7},{5,1},{7,3},{8,12},{10,14},{12... | collective-permute-start | bytes 12296 | tf_op jit(solution)/shard_map/ppermute | solution.py:697
  69.9 3.7 %collective-permute-start.34 = (f32[8,128]{1,0:T(8,128)S(1)}, f32[8,128]{1,0:T(8,128)S(1)}, u32[]{:S(2)}, u32[]{:S(2)}) collective-permute-start(f32[8,128]{1,0:T(8,128)S(1)} %add_grads.4.refs_0_), channel_id=1, source_target_pairs={{0,2},{2,0},{4,6},{6,4},{1,3},{3,1},{5,7},{7,5},{8,10},{10,8},{12,... | collective-permute-start | bytes 12296 | tf_op jit(solution)/shard_map/ppermute | solution.py:697
